TPU v7x, 256 devices: a whole 4x4x8 slice. The times are simulated.
256 devices in a mesh: grp: 8 (over x, core), dev: 32 (over y, z).
Axes of the slice: x: 4, y: 4, z: 8, core: 2. Of those that a mesh axis runs over, the one named last changes fastest.
Arguments:
- features: bfloat16 [131072, 128], P(('grp', 'dev')), may hold values from -6 to 6
- hub_list: int32 [256, 4], P(('grp', 'dev')), may hold values from 0 to 511
- send_list: int32 [256, 32, 32], P(('grp', 'dev')), may hold values from 0 to 511
- send_count: int32 [256, 32], P(('grp', 'dev')), may hold values from 1 to 32, as said below
- tile_dst: int32 [256, 32], P(('grp', 'dev')), may hold values from 0 to 3
- tile_src: int32 [256, 32], P(('grp', 'dev')), may hold values from 0 to 19
- tile_count: int32 [256], P(('grp', 'dev')), may hold values from 1 to 32, as said below
- tile_adj: bfloat16 [8192, 128, 128], P(('grp', 'dev')), may hold values from 0 to 1, as said below
- sample_ids: int32 [256, 256], P(('grp', 'dev')), may hold values from 0 to 511
- labels: int32 [131072], P(('grp', 'dev')), may hold values from 0 to 171
- first_self: bfloat16 [128, 512], replicated, may hold values from -0.5 to 0.5
- first_mean: bfloat16 [128, 512], replicated, may hold values from -0.5 to 0.5
- second_self: bfloat16 [512, 172], replicated, may hold values from -0.75 to 0.75
- second_mean: bfloat16 [512, 172], replicated, may hold values from -0.75 to 0.75
Outputs:
- hidden: bfloat16 [131072, 512], P(('grp', 'dev'))
- grad_hidden: float32 [131072, 512], P(('grp', 'dev'))
- loss_value: float32 [], replicated
- grad_first_self: float32 [128, 512], replicated
- grad_first_mean: float32 [128, 512], replicated
- grad_second_self: float32 [512, 172], replicated
- grad_second_mean: float32 [512, 172], replicated
Inputs may be any that keep to these rules, and one draw needn't show every extreme that they name: `send_count`: each partition sends exactly 32 rows to at least one peer. `tile_count`: some partition uses all 32 tiles. `tile_adj`: entries are 0 or 1.
All inputs are finite; a program needn't handle non-finite values.
Results may differ from a plain program's by a relative error of at most 0.004.
The roundings to bfloat16 on the way count: a program that leaves them out, or rounds other values in their place, can miss the bound.
Values may be sent and summed in bfloat16 or wider, within the bound.
No kernel may reach another device: no remote copies, remote signals or barrier semaphores. Data moves between devices by JAX's collectives and lax.ppermute only.
A program may use at most 64 MiB of HBM per device.

v0:
```python
import jax
import jax.numpy as jnp
from jax import lax
from jax.sharding import PartitionSpec as P


def placement(indices, count, blocks):
    tiles = indices.shape[0]
    live = jnp.arange(tiles, dtype=jnp.int32)[None, :] < count
    hit = indices[None, :] == jnp.arange(blocks, dtype=jnp.int32)[:, None]
    return jnp.where(hit & live, 1.0, 0.0).astype(jnp.float32)


def degree_rows(adjacent, targets, count, node_rows):
    tile_size = adjacent.shape[1]
    sums = jnp.sum(adjacent.astype(jnp.float32), axis=2)
    table = placement(targets, count, node_rows // tile_size)
    total = jnp.dot(
        table, sums, precision=lax.Precision.HIGHEST, preferred_element_type=jnp.float32
    )
    return total.reshape(node_rows)


def aggregate(source, adjacent, targets, anchors, count, node_rows):
    tile_size = adjacent.shape[1]
    width = source.shape[1]
    blocks = source.reshape(source.shape[0] // tile_size, tile_size, width)
    picked = blocks[anchors]
    terms = jnp.einsum("tij,tjw->tiw", adjacent, picked, preferred_element_type=jnp.float32)
    table = placement(targets, count, node_rows // tile_size)
    total = jnp.einsum(
        "bt,tiw->biw",
        table,
        terms,
        precision=lax.Precision.HIGHEST,
        preferred_element_type=jnp.float32,
    )
    return total.reshape(node_rows, width)


def scatter_back(upstream, adjacent, targets, anchors, count, source_rows):
    tile_size = adjacent.shape[1]
    width = upstream.shape[1]
    blocks = upstream.reshape(upstream.shape[0] // tile_size, tile_size, width)
    picked = blocks[targets]
    terms = jnp.einsum("tji,tjw->tiw", adjacent, picked, preferred_element_type=jnp.float32)
    table = placement(anchors, count, source_rows // tile_size)
    total = jnp.einsum(
        "bt,tiw->biw",
        table,
        terms,
        precision=lax.Precision.HIGHEST,
        preferred_element_type=jnp.float32,
    )
    return total.reshape(source_rows, width)


def contract_rows(left_side, right_side):
    return lax.dot_general(
        left_side, right_side, (((0,), (0,)), ((), ())), preferred_element_type=jnp.float32
    )


def on_device(
    features,
    hub_list,
    send_list,
    send_count,
    tile_dst,
    tile_src,
    tile_count,
    tile_adj,
    sample_ids,
    labels,
    first_self,
    first_mean,
    second_self,
    second_mean,
):
    hubs = hub_list[0]
    sends = send_list[0]
    counts = send_count[0]
    targets = tile_dst[0]
    anchors = tile_src[0]
    live_tiles = tile_count[0]
    picked = sample_ids[0]
    node_rows = features.shape[0]
    capacity = sends.shape[1]
    members = lax.axis_size("dev")
    samples_all = picked.shape[0] * lax.axis_size("grp") * lax.axis_size("dev")
    live_slots = jnp.arange(capacity, dtype=jnp.int32)[None, :] < counts[:, None]

    def outgoing(values):
        taken = values[sends]
        return jnp.where(live_slots[:, :, None], taken, jnp.zeros_like(taken))

    hub_feature = lax.all_gather(features[hubs], ("grp", "dev"), axis=0, tiled=True)
    edge_feature = lax.all_to_all(
        outgoing(features), "dev", split_axis=0, concat_axis=0, tiled=True
    )
    source = jnp.concatenate(
        [features, hub_feature, edge_feature.reshape(members * capacity, features.shape[1])], 0
    )
    degree = degree_rows(tile_adj, targets, live_tiles, node_rows)
    floor_deg = jnp.maximum(degree, 1.0)
    mean_rows_first = (
        aggregate(source, tile_adj, targets, anchors, live_tiles, node_rows) / floor_deg[:, None]
    ).astype(jnp.bfloat16)
    linear = jnp.dot(features, first_self, preferred_element_type=jnp.float32) + jnp.dot(
        mean_rows_first, first_mean, preferred_element_type=jnp.float32
    )
    hidden = jnp.maximum(linear, 0.0).astype(jnp.bfloat16)
    hub_hidden = lax.all_gather(hidden[hubs], ("grp", "dev"), axis=0, tiled=True)
    edge_hidden = lax.all_to_all(outgoing(hidden), "dev", split_axis=0, concat_axis=0, tiled=True)
    hub_count = hub_hidden.shape[0]
    source = jnp.concatenate(
        [hidden, hub_hidden, edge_hidden.reshape(members * capacity, hidden.shape[1])], 0
    )
    mean_rows = (
        aggregate(source, tile_adj, targets, anchors, live_tiles, node_rows) / floor_deg[:, None]
    ).astype(jnp.bfloat16)
    logits = jnp.dot(hidden, second_self, preferred_element_type=jnp.float32) + jnp.dot(
        mean_rows, second_mean, preferred_element_type=jnp.float32
    )
    classes = labels[picked]
    chosen = logits[picked]
    log_total = jnp.log(jnp.sum(jnp.exp(chosen), axis=1))
    loss_part = jnp.sum(log_total - jnp.take_along_axis(chosen, classes[:, None], 1)[:, 0])
    softmax_rows = jnp.exp(chosen - log_total[:, None])
    onehot = (classes[:, None] == jnp.arange(logits.shape[1], dtype=jnp.int32)[None, :]).astype(
        jnp.float32
    )
    grad_logits = (
        jnp.zeros(logits.shape, jnp.float32)
        .at[picked]
        .add((softmax_rows - onehot) / samples_all)
        .astype(jnp.bfloat16)
    )
    sum_self = contract_rows(hidden, grad_logits)
    sum_mean = contract_rows(mean_rows, grad_logits)
    direct = jnp.dot(grad_logits, second_self.T, preferred_element_type=jnp.float32)
    grad_mean = (
        jnp.dot(grad_logits, second_mean.T, preferred_element_type=jnp.float32) / floor_deg[:, None]
    ).astype(jnp.bfloat16)
    spread = scatter_back(grad_mean, tile_adj, targets, anchors, live_tiles, source.shape[0])
    edge_part = spread[node_rows + hub_count :].reshape(members, capacity, spread.shape[1])
    returned = lax.all_to_all(
        edge_part.astype(jnp.bfloat16), "dev", split_axis=0, concat_axis=0, tiled=True
    ).astype(edge_part.dtype)
    returned = jnp.where(live_slots[:, :, None], returned, jnp.zeros_like(returned))
    grad_hidden = (direct + spread[:node_rows]).at[sends].add(returned)
    hub_part = spread[node_rows : node_rows + hub_count]
    summed = lax.psum(hub_part, ("grp", "dev"))
    share = lax.dynamic_slice_in_dim(
        summed, lax.axis_index(("grp", "dev")) * hubs.shape[0], hubs.shape[0], 0
    )
    grad_hidden = grad_hidden.at[hubs].add(share)
    grad_first = jnp.where(hidden > 0, grad_hidden, jnp.zeros_like(grad_hidden)).astype(
        jnp.bfloat16
    )
    first_self_sum = contract_rows(features, grad_first)
    first_mean_sum = contract_rows(mean_rows_first, grad_first)
    first_self_sum, first_mean_sum, sum_self, sum_mean, loss_total = lax.psum(
        (first_self_sum, first_mean_sum, sum_self, sum_mean, loss_part), ("grp", "dev")
    )
    return (
        hidden,
        grad_hidden,
        loss_total / samples_all,
        first_self_sum,
        first_mean_sum,
        sum_self,
        sum_mean,
    )


def solution(mesh):
    placed = (
        P(("grp", "dev"), None),
        P(("grp", "dev"), None),
        P(("grp", "dev"), None, None),
        P(("grp", "dev"), None),
        P(("grp", "dev"), None),
        P(("grp", "dev"), None),
        P(("grp", "dev")),
        P(("grp", "dev"), None, None),
        P(("grp", "dev"), None),
        P(("grp", "dev")),
        P(),
        P(),
        P(),
        P(),
    )
    return jax.shard_map(
        on_device,
        mesh=mesh,
        in_specs=placed,
        out_specs=(P(("grp", "dev"), None), P(("grp", "dev"), None), P(), P(), P(), P(), P()),
        check_vma=False,
    )
```

profile of v0, /device:TPU:1, one launch (start us, length us, event | category | flops | bytes accessed | tf_op | source)
XLA Modules:
  0.0 843.0 jit_solution(2756379421726202309)
XLA Ops:
  8.9 3.8 gather_fusion.1
  13.6 12.0 %all-to-all-start = ((bf16[32,32,128]{2,1,0:T(8,128)(2,1)}), bf16[32,32,128]{2,1,0:T(8,128)(2,1)S(1)}, u32[]{:S(2)}, u32[]{:S(2)}) async-start(bf16[32,32,128]{2,1,0:T(8,128)(2,1)} %broadcast_select_fusion.1), calls=%async_computation | async-start | bytes 524288 | tf_op jit(solution)/shard_map/all_to_all | solution.py:98
  28.8 62.4 %all-gather.2 = bf16[256,4,128]{2,1,0:T(4,128)(2,1)S(1)} all-gather(bf16[1,4,128]{2,1,0:T(4,128)(2,1)S(1)} %bitcast.112), channel_id=2, replica_groups=mesh['grp'=8,'dev'=32] {'grp','dev'}, dimensions={0}, use_global_device_ids=true | all-gather | bytes 263168 | tf_op jit(solution)/shard_map/all_gather | solution.py:97
  94.1 3.4 convolution_bitcast_fusion.2
  103.5 4.0 gather_fusion.4
  109.8 6.8 all-to-all-start.1
  119.7 92.6 %all-gather.6.cloned.1.call-done = bf16[256,4,512]{2,1,0:T(4,128)(2,1)} async-done(((bf16[1,4,512]{2,1,0:T(4,128)(2,1)}), bf16[256,4,512]{2,1,0:T(4,128)(2,1)}) %all-gather.6.cloned.1.call-update) | async-done | bytes 1048592 | tf_op jit(solution)/shard_map/all_gather | solution.py:113
  217.2 2.8 gather_fusion.5
  220.0 7.0 convolution_bitcast_fusion.1
  227.0 10.3 %copy.46 = f32[32,128,512]{2,0,1:T(8,128)} copy(f32[32,128,512]{1,2,0:T(8,128)} %convolution_bitcast_fusion.1) | data formatting | bytes 16777216 | tf_op jit(solution)/shard_map/tij,tjw->tiw/dot_general | solution.py:29
  237.3 6.4 fusion.29
  251.6 2.8 gather_fusion.8
  254.4 6.7 convolution_bitcast_fusion
  261.1 10.3 %copy.50 = f32[32,128,512]{2,0,1:T(8,128)} copy(f32[32,128,512]{1,2,0:T(8,128)} %convolution_bitcast_fusion) | data formatting | bytes 16777216 | tf_op jit(solution)/shard_map/tji,tjw->tiw/dot_general | solution.py:46
  271.4 8.9 %fusion.16 = f32[20,128,512]{2,0,1:T(8,128)S(1)} fusion(f32[32,128,512]{2,0,1:T(8,128)} %copy.50, s32[32]{0:T(128)S(1)} %bitcast.115, pred[32]{0:T(512)(128)(4,1)S(1)} %iota_compare_fusion.5), kind=kOutput, calls=%fused_computation.52 | convolution fusion | flops 503318400 | bytes 13631648 | tf_op jit(solution)/shard_map/bt,tiw->biw/dot_general | solution.py:48
  280.3 2.6 copy-done.6
  284.9 7.5 all-to-all-start.2
  294.2 2.7 slice.44
  304.4 13.1 %all-to-all-done.2 = bf16[32,32,512]{2,1,0:T(8,128)(2,1)} async-done(((bf16[32,32,512]{2,1,0:T(8,128)(2,1)}), bf16[32,32,512]{2,1,0:T(8,128)(2,1)}, u32[]{:S(2)}, u32[]{:S(2)}) %all-to-all-start.2) | async-done | bytes 1048608 | tf_op jit(solution)/shard_map/all_to_all | solution.py:147
  317.5 2.9 convert_select_fusion
  320.4 7.9 scatter_fusion
  328.3 234.2 %all-reduce.4.cloned.1.call-done = f32[1024,512]{1,0:T(8,128)} async-done(((f32[1024,512]{1,0:T(8,128)}), f32[1024,512]{1,0:T(8,128)}) %all-reduce.4.cloned.1.call-update) | async-done | bytes 2097168 | tf_op jit(solution)/shard_map/psum | solution.py:153
  565.9 77.7 %psum.43 = f32[]{:T(128)} all-reduce(f32[]{:T(128)} %get-tuple-element.39), channel_id=1, replica_groups=mesh['grp'=8,'dev'=32] {'grp','dev'}, use_global_device_ids=true, to_apply=%region_7.8 | all-reduce | flops 1 | bytes 8 | tf_op jit(solution)/shard_map/psum | solution.py:163
  644.3 184.1 %all-reduce.6.cloned.1.call-done = (f32[128,512]{0,1:T(8,128)}, f32[128,512]{1,0:T(8,128)}, f32[512,172]{0,1:T(8,128)}, f32[512,172]{0,1:T(8,128)}) async-done(((f32[128,512]{0,1:T(8,128)}, f32[128,512]{1,0:T(8,128)}, f32[512,172]{0,1:T(8,128)}, f32[512,172]{0,1:T(8,128)}), (f32[128,512]{0,1:T(8,128)}, f32[128,512]{1,0:T(8,128)}, f32[512,172]{0,1:T(8,128)}, ...) | async-done | bytes 1228816 | tf_op jit(solution)/shard_map/psum | solution.py:163
  (108 shorter events, 53.3 us)
Async XLA Ops:
  7.2 237.1 %copy-start = (bf16[512,172]{0,1:T(8,128)(2,1)S(1)}, bf16[512,172]{0,1:T(8,128)(2,1)}, u32[]{:S(2)}) copy-start(bf16[512,172]{0,1:T(8,128)(2,1)} %param.27) | copy-start | bytes 528388
  7.2 20.9 %copy-start.5 = (bf16[512,128]{1,0:T(8,128)(2,1)S(1)}, bf16[512,128]{1,0:T(8,128)(2,1)}, u32[]{:S(2)}) copy-start(bf16[512,128]{1,0:T(8,128)(2,1)} %param.14) | copy-start | bytes 393220
  7.2 20.5 %copy-start.7 = (bf16[32,128,128]{2,1,0:T(8,128)(2,1)S(1)}, bf16[32,128,128]{2,1,0:T(8,128)(2,1)}, u32[]{:S(2)}) copy-start(bf16[32,128,128]{2,1,0:T(8,128)(2,1)} %param.21) | copy-start | bytes 3145732
  7.2 21.4 %copy-start.17 = (s32[1,32]{1,0:T(1,128)S(1)}, s32[1,32]{1,0:T(1,128)}, u32[]{:S(2)}) copy-start(s32[1,32]{1,0:T(1,128)} %param.18) | copy-start | bytes 388
  7.2 83.9 %copy-start.16 = (bf16[128,512]{1,0:T(8,128)(2,1)S(1)}, bf16[128,512]{1,0:T(8,128)(2,1)}, u32[]{:S(2)}) copy-start(bf16[128,512]{1,0:T(8,128)(2,1)} %param.24) | copy-start | bytes 393220
  13.6 78.8 %all-to-all-start = ((bf16[32,32,128]{2,1,0:T(8,128)(2,1)}), bf16[32,32,128]{2,1,0:T(8,128)(2,1)S(1)}, u32[]{:S(2)}, u32[]{:S(2)}) async-start(bf16[32,32,128]{2,1,0:T(8,128)(2,1)} %broadcast_select_fusion.1), calls=%async_computation | async-start | bytes 524288 | tf_op jit(solution)/shard_map/all_to_all | solution.py:98
  25.6 186.7 %all-gather.6.cloned.1.call-start = ((), (), s32[]{:S(2)}) async-start(), calls=%async_computation.4 | async-start | bytes 1052672 | tf_op jit(solution)/shard_map/all_gather | solution.py:113
  97.6 4.4 copy-start.15
  103.4 461.4 %copy-start.4 = (bf16[512,512]{1,0:T(8,128)(2,1)}, bf16[512,512]{1,0:T(8,128)(2,1)S(1)}, u32[]{:S(2)}) copy-start(bf16[512,512]{1,0:T(8,128)(2,1)S(1)} %fusion.2) | copy-start | bytes 1572868
  107.4 9.2 %copy-start.18 = (s32[1,256]{1,0:T(1,128)S(1)}, s32[1,256]{1,0:T(1,128)}, u32[]{:S(2)}) copy-start(s32[1,256]{1,0:T(1,128)} %param.22) | copy-start | bytes 3076
  107.4 9.2 %copy-start.2 = (s32[512]{0:T(512)S(1)}, s32[512]{0:T(512)}, u32[]{:S(2)}) copy-start(s32[512]{0:T(512)} %param.23) | copy-start | bytes 6148
  107.5 11.2 %copy-start.13 = (bf16[512,172]{0,1:T(8,128)(2,1)S(1)}, bf16[512,172]{0,1:T(8,128)(2,1)}, u32[]{:S(2)}) copy-start(bf16[512,172]{0,1:T(8,128)(2,1)} %param.26) | copy-start | bytes 528388
  109.8 104.7 %all-to-all-start.1 = ((bf16[32,32,512]{2,1,0:T(8,128)(2,1)}), bf16[32,32,512]{2,1,0:T(8,128)(2,1)S(1)}, u32[]{:S(2)}, u32[]{:S(2)}) async-start(bf16[32,32,512]{2,1,0:T(8,128)(2,1)} %broadcast_select_fusion), calls=%async_computation.1 | async-start | bytes 2097152 | tf_op jit(solution)/shard_map/all_to_all | solution.py:114
  237.3 6.9 copy-start.10
  251.6 2.8 copy-start.8
  261.1 10.3 %copy-start.19 = (s32[1,32]{1,0:T(1,128)S(1)}, s32[1,32]{1,0:T(1,128)}, u32[]{:S(2)}) copy-start(s32[1,32]{1,0:T(1,128)} %param.19) | copy-start | bytes 388
  280.3 2.7 copy-start.6
  284.9 32.7 %all-to-all-start.2 = ((bf16[32,32,512]{2,1,0:T(8,128)(2,1)}), bf16[32,32,512]{2,1,0:T(8,128)(2,1)}, u32[]{:S(2)}, u32[]{:S(2)}) async-start(bf16[32,32,512]{2,1,0:T(8,128)(2,1)} %bitcast.32), calls=%async_computation.2 | async-start | bytes 2097152 | tf_op jit(solution)/shard_map/all_to_all | solution.py:147
  292.4 270.2 %all-reduce.4.cloned.1.call-start = ((), (), s32[]{:S(2)}) async-start(), calls=%async_computation.3 | async-start | bytes 4194304 | tf_op jit(solution)/shard_map/psum | solution.py:153
  298.2 4.7 copy-start.14
  300.8 527.7 %all-reduce.6.cloned.1.call-start = ((), (), s32[]{:S(2)}) async-start(), calls=%async_computation.5 | async-start | bytes 2490368 | tf_op jit(solution)/shard_map/psum | solution.py:163
  320.4 243.4 %copy-start.12 = (bf16[512,128]{1,0:T(8,128)(2,1)S(1)}, bf16[512,128]{1,0:T(8,128)(2,1)}, u32[]{:S(2)}) copy-start(bf16[512,128]{1,0:T(8,128)(2,1)} %copy-done.11) | copy-start | bytes 393220
  320.4 515.0 %copy-start.1 = (bf16[512,172]{0,1:T(8,128)(2,1)S(1)}, bf16[512,172]{0,1:T(8,128)(2,1)}, u32[]{:S(2)}) copy-start(bf16[512,172]{0,1:T(8,128)(2,1)} %param.27) | copy-start | bytes 528388
  563.8 271.6 %copy-start.3 = (f32[512,512]{1,0:T(8,128)}, f32[512,512]{1,0:T(8,128)S(1)}, u32[]{:S(2)}) copy-start(f32[512,512]{1,0:T(8,128)S(1)} %scatter_custom_fusion.2) | copy-start | bytes 3145732
  (2 other events, 1.6 us)
Sparse Core Ops, SparseCore 0:
  108.8 103.5 all-gather.5
  300.9 261.6 all-reduce.3
  569.1 259.2 all-reduce.5
where the time goes:
time: 845 us; the launch traced here: 843 us
  waiting for transfers between devices  524 us (62%)
  blocking collectives  140 us (17%)
  local copies, waits for them, and re-layouts  69.2 us (8%)
  matrix products  43.8 us (5%)
  starting transfers between devices  26.4 us (3%)
  other arithmetic  22.6 us (3%)
  between operations  16.7 us (2%)
    psum x1, waiting for transfers between devices, on_device(): summed = lax.psum(hub_part, ('grp', 'dev'))  234 us
    psum x1, waiting for transfers between devices, on_device(): lax.psum((first_self_sum, first_mean_sum, sum_self, sum_mean, loss_part),...  184 us
    all_gather x1, waiting for transfers between devices, on_device(): lax.all_gather(hidden[hubs], ('grp', 'dev'), axis=0, tiled=True)  92.6 us
    psum x1, blocking collectives, on_device(): lax.psum((first_self_sum, first_mean_sum, sum_self, sum_mean, loss_part),...  77.7 us
    all_gather x1, blocking collectives, on_device(): lax.all_gather(features[hubs], ('grp', 'dev'), axis=0, tiled=True)  62.4 us
  transfers between devices with their start and end apart: 6, of which 4 were waited for; matrix products, arithmetic and copies ran while one was open for 4% of the time, Pallas kernels for 0%

commit v1 on v0

v1 whole, which is shorter than its diff:
```python
import functools

import jax
import jax.numpy as jnp
from jax import lax
from jax.experimental import pallas as pl
from jax.experimental.pallas import tpu as pltpu
from jax.sharding import PartitionSpec as P

F32 = jnp.float32
BF16 = jnp.bfloat16
MIB = 1 << 20
TILE = 128
SLOTS = 48
HUB_AT = 32
WEIGHT_AT = 36
CLASS_ROWS = 176
STACK_ROWS = 640


def nn(left, right):
    return jnp.dot(left, right, preferred_element_type=F32)


def nt(left, right):
    return lax.dot_general(left, right, (((1,), (1,)), ((), ())), preferred_element_type=F32)


def tn(left, right):
    return lax.dot_general(left, right, (((0,), (0,)), ((), ())), preferred_element_type=F32)


def split(values):
    high = values.astype(BF16)
    low = (values - high.astype(F32)).astype(BF16)
    return high, low


def kernel_call(body, outs, scratch=(), in_specs=None, limit=24, flops=0, moved=0):
    placed = {} if in_specs is None else {"in_specs": in_specs}
    return pl.pallas_call(
        body,
        out_shape=outs,
        **placed,
        scratch_shapes=list(scratch),
        compiler_params=pltpu.CompilerParams(vmem_limit_bytes=limit * MIB),
        cost_estimate=pl.CostEstimate(flops=flops, bytes_accessed=moved, transcendentals=0),
    )


VM = pl.BlockSpec(memory_space=pltpu.VMEM)
SM = pl.BlockSpec(memory_space=pltpu.SMEM)


def pick_matrix(send_ref, count_ref, hub_ref, pick_ref):
    peers = send_ref.shape[0]
    nodes = pick_ref.shape[1]
    send = jnp.transpose(send_ref[...])
    slot = lax.broadcasted_iota(jnp.int32, send.shape, 0)
    send = jnp.where(slot < count_ref[...], send, -1)
    row = lax.broadcasted_iota(jnp.int32, (SLOTS - HUB_AT, 1), 0)
    hubs = jnp.full((SLOTS - HUB_AT, 1), -1, jnp.int32)
    for k in range(hub_ref.shape[1]):
        hubs = jnp.where(row == k, hub_ref[0, k], hubs)
    lane = lax.broadcasted_iota(jnp.int32, (HUB_AT, nodes), 1)
    lane_hub = lax.broadcasted_iota(jnp.int32, (SLOTS - HUB_AT, nodes), 1)
    hub_part = jnp.where(hubs == lane_hub, 1.0, 0.0).astype(BF16)
    for n in range(peers):
        body = jnp.where(send[:, n : n + 1] == lane, 1.0, 0.0).astype(BF16)
        pick_ref[n * SLOTS : n * SLOTS + HUB_AT, :] = body
        pick_ref[n * SLOTS + HUB_AT : (n + 1) * SLOTS, :] = hub_part


def send_features(features_ref, send_ref, count_ref, hub_ref, out_ref, pick_ref):
    pick_matrix(send_ref, count_ref, hub_ref, pick_ref)
    out_ref[...] = nn(pick_ref[...], features_ref[...]).astype(BF16)


def build_dense(adj_ref, dst_ref, src_ref, count_ref, dense_ref, turned_ref, degree_ref):
    dense_ref[...] = jnp.zeros_like(dense_ref)
    turned_ref[...] = jnp.zeros_like(turned_ref)

    def add(t, carry):
        rows = pl.ds(pl.multiple_of(dst_ref[0, t] * TILE, TILE), TILE)
        columns = pl.ds(pl.multiple_of(src_ref[0, t] * TILE, TILE), TILE)
        tile = adj_ref[t]
        dense_ref[rows, columns] += tile
        turned_ref[columns, rows] += jnp.transpose(tile)
        return carry

    lax.fori_loop(0, count_ref[0], add, 0)
    ones = jnp.ones((dense_ref.shape[1], TILE), BF16)
    degree_ref[...] = jnp.maximum(nn(dense_ref[...], ones), 1.0)


def spread_hubs(arrived_ref, out_ref):
    hubs = out_ref.shape[1]
    rows = arrived_ref.shape[0]
    i = lax.broadcasted_iota(jnp.int32, (hubs, rows), 0)
    j = lax.broadcasted_iota(jnp.int32, (hubs, rows), 1)
    pick = jnp.where(j == (i >> 2) * SLOTS + HUB_AT + (i & 3), 1.0, 0.0).astype(BF16)
    found = nn(pick, arrived_ref[...]).astype(BF16)
    for g in range(out_ref.shape[0]):
        out_ref[g] = found


def assemble(table_ref, own_ref, hub_ref, arrived_ref, lanes):
    own = own_ref.shape[0]
    hubs = hub_ref.shape[0]
    table_ref[0:own, lanes] = own_ref[...]
    table_ref[own : own + hubs, lanes] = hub_ref[...]
    for n in range(arrived_ref.shape[0] // SLOTS):
        at = own + hubs + n * HUB_AT
        table_ref[at : at + HUB_AT, lanes] = arrived_ref[n * SLOTS : n * SLOTS + HUB_AT, :]


def first_mean_rows(
    features_ref, hub_ref, arrived_ref, dense_ref, degree_ref, send_ref, count_ref, hub_list_ref,
    mean_ref, out_ref, table_ref, pick_ref,
):
    assemble(table_ref, features_ref, hub_ref, arrived_ref, slice(0, TILE))
    pick_matrix(send_ref, count_ref, hub_list_ref, pick_ref)
    total = nn(dense_ref[...], table_ref[...])
    mean = (total / degree_ref[...]).astype(BF16)
    mean_ref[...] = mean
    out_ref[...] = nn(pick_ref[...], mean).astype(BF16)


def main_part(
    samples_all,
    features_ref, feature_hub_ref, feature_arrived_ref,
    mean_ref, mean_hub_ref, mean_arrived_ref,
    dense_ref, turned_ref, degree_ref, sample_ref, label_ref,
    first_self_ref, first_mean_ref, second_self_ref, second_mean_ref,
    hidden_ref, base_ref, edge_ref, out_ref,
    table_ref, source_ref, first_ref, self_ref, both_ref, scaled_ref, stack_ref,
):
    nodes, width = hidden_ref.shape
    classes = second_self_ref.shape[1]
    padded = self_ref.shape[1]
    chunks = table_ref.shape[0] // nodes
    hub_rows = feature_hub_ref.shape[0]
    assemble(table_ref, features_ref, feature_hub_ref, feature_arrived_ref, slice(0, TILE))
    assemble(table_ref, mean_ref, mean_hub_ref, mean_arrived_ref, slice(TILE, 2 * TILE))
    first_ref[0:TILE, :] = first_self_ref[...]
    first_ref[TILE : 2 * TILE, :] = first_mean_ref[...]
    self_ref[...] = jnp.zeros_like(self_ref)
    both_ref[...] = jnp.zeros_like(both_ref)
    self_ref[:, 0:classes] = second_self_ref[...]
    both_ref[:, 0:classes] = second_mean_ref[...]
    both_ref[:, padded : padded + classes] = second_mean_ref[...]

    def rows_of(i):
        return pl.ds(pl.multiple_of(i * nodes, nodes), nodes)

    def forward(i, carry):
        rows = rows_of(i)
        linear = nn(table_ref[rows, :], first_ref[...])
        source_ref[rows, :] = jnp.maximum(linear, 0.0).astype(BF16)
        return carry

    lax.fori_loop(0, chunks, forward, 0)
    hidden = source_ref[0:nodes, :]
    hidden_ref[...] = hidden
    degree = degree_ref[:, 0:1]
    mean = (nn(dense_ref[...], source_ref[...]) / degree).astype(BF16)
    logits = nn(hidden, self_ref[...]) + nn(mean, both_ref[:, 0:padded])

    lane = lax.broadcasted_iota(jnp.int32, (nodes, padded), 1)
    real = lane < classes
    node = lax.broadcasted_iota(jnp.int32, (nodes, sample_ref.shape[1]), 0)
    hits = jnp.where(node == sample_ref[...], 1.0, 0.0)
    times = jnp.sum(hits, axis=1, keepdims=True)
    label = jnp.transpose(jnp.broadcast_to(label_ref[...], (8, nodes)))[:, 0:1]
    onehot = jnp.where(lane == label, 1.0, 0.0)
    top = jnp.max(jnp.where(real, logits, -jnp.inf), axis=1, keepdims=True)
    shifted = logits - top
    powers = jnp.where(real, jnp.exp(shifted), 0.0)
    total = jnp.sum(powers, axis=1, keepdims=True)
    chosen = jnp.sum(onehot * shifted, axis=1, keepdims=True)
    loss = jnp.sum(times * (jnp.log(total) - chosen), axis=0, keepdims=True)
    upstream = times * ((powers / total - onehot) / samples_all)
    upstream = upstream.astype(BF16)

    stack_ref[2 * TILE : 2 * TILE + CLASS_ROWS, :] = tn(upstream, hidden)[0:CLASS_ROWS]
    stack_ref[2 * TILE + CLASS_ROWS : 2 * TILE + 2 * CLASS_ROWS, :] = tn(upstream, mean)[0:CLASS_ROWS]
    tail = STACK_ROWS - 2 * TILE - 2 * CLASS_ROWS
    loss_high, loss_low = split(loss)
    place = lax.broadcasted_iota(jnp.int32, (tail, width), 0)
    marks = jnp.where(place == 0, loss_high.astype(F32), 0.0)
    stack_ref[2 * TILE + 2 * CLASS_ROWS :, :] = jnp.where(place == 1, loss_low.astype(F32), marks)

    high, low = split(upstream.astype(F32) / degree)
    scaled_ref[:, 0:padded] = high
    scaled_ref[:, padded : 2 * padded] = low

    def back(rows):
        pair = nn(turned_ref[rows, :], scaled_ref[...])
        high, low = split(pair[:, 0:padded] + pair[:, padded : 2 * padded])
        spread = nt(high, both_ref[:, 0:padded]) + nt(low, both_ref[:, 0:padded])
        return high, spread

    def weights(rows, grad):
        masked = jnp.where(source_ref[rows, :] > 0, grad, 0.0).astype(BF16)
        return tn(table_ref[rows, :], masked)

    own = rows_of(0)
    unused, spread = back(own)
    base = nt(upstream, self_ref[...]) + spread
    base_ref[...] = base
    stack_ref[0 : 2 * TILE, :] = weights(own, base)

    def hub_chunk(i, carry):
        rows = rows_of(i + 1)
        high, spread = back(rows)
        stack_ref[0 : 2 * TILE, :] += weights(rows, spread)
        for part in range(nodes // TILE):
            out_ref[i * (nodes // TILE) + part, 0:TILE, :] = high[part * TILE : (part + 1) * TILE]
        return carry

    lax.fori_loop(0, hub_rows // nodes, hub_chunk, 0)

    def edge_chunk(i, carry):
        rows = rows_of(i + 1 + hub_rows // nodes)
        high, spread = back(rows)
        stack_ref[0 : 2 * TILE, :] += weights(rows, spread)
        edge_ref[rows_of(i), :] = high
        return carry

    lax.fori_loop(0, edge_ref.shape[0] // nodes, edge_chunk, 0)
    groups = out_ref.shape[0]
    share = STACK_ROWS // groups
    for g in range(groups):
        part = stack_ref[g * share : (g + 1) * share, :].astype(BF16)
        out_ref[g, TILE : TILE + share, :] = part[:, 0:padded]
        out_ref[g, TILE + share : TILE + 2 * share, :] = part[:, padded : 2 * padded]


def sum_groups(arrived_ref, edge_ref, out_ref, total_ref, block_ref):
    share = STACK_ROWS // arrived_ref.shape[0]
    total = arrived_ref[0].astype(F32)
    for g in range(1, arrived_ref.shape[0]):
        total += arrived_ref[g].astype(F32)
    total_ref[...] = total
    block_ref[...] = jnp.zeros_like(block_ref)
    peers = out_ref.shape[0] // SLOTS
    hubs = TILE // peers
    piece = share // (peers // 4)
    lanes = out_ref.shape[1] // 2
    for n in range(peers):
        i, j = n // 4, n % 4
        at = TILE + (j // 2) * share + piece * i
        block_ref[n, 0:hubs, :] = total_ref[hubs * n : hubs * (n + 1), :]
        part = total_ref[at : at + piece, (j % 2) * lanes : (j % 2 + 1) * lanes]
        high = part.astype(BF16).astype(F32)
        block_ref[n, hubs : hubs + piece, 0:lanes] = high
        block_ref[n, hubs : hubs + piece, lanes : 2 * lanes] = part - high
        out_ref[n * SLOTS : n * SLOTS + HUB_AT, :] = edge_ref[n * HUB_AT : (n + 1) * HUB_AT, :]
        out_ref[n * SLOTS + HUB_AT : (n + 1) * SLOTS, :] = block_ref[n].astype(BF16)


def sum_peers(arrived_ref, out_ref):
    peers = out_ref.shape[0]
    lanes = out_ref.shape[2]
    total = jnp.zeros((SLOTS - HUB_AT, 2 * lanes), F32)
    for n in range(peers):
        total += arrived_ref[n * SLOTS + HUB_AT : (n + 1) * SLOTS, :].astype(F32)
    own = total[:, 0:lanes] + total[:, lanes : 2 * lanes]
    for n in range(peers):
        out_ref[n] = own


def join_pieces(arrived_ref, out_ref, whole_ref):
    peers = arrived_ref.shape[0]
    share = out_ref.shape[1]
    piece = share // (peers // 4)
    lanes = arrived_ref.shape[2]
    at = WEIGHT_AT - HUB_AT
    for n in range(peers):
        i, j = n // 4, n % 4
        whole_ref[piece * i : piece * (i + 1), lanes * j : lanes * (j + 1)] = arrived_ref[n, at : at + piece, :]
    whole = whole_ref[...]
    for g in range(out_ref.shape[0]):
        out_ref[g] = whole


def weight_outputs(samples_all, stack_ref, first_self_ref, first_mean_ref, self_ref, mean_ref, loss_ref):
    classes = self_ref.shape[1]
    first_self_ref[...] = stack_ref[0:TILE, :]
    first_mean_ref[...] = stack_ref[TILE : 2 * TILE, :]
    at = 2 * TILE
    self_ref[...] = jnp.transpose(stack_ref[at : at + CLASS_ROWS, :])[:, 0:classes]
    at += CLASS_ROWS
    mean_ref[...] = jnp.transpose(stack_ref[at : at + CLASS_ROWS, :])[:, 0:classes]
    at += CLASS_ROWS
    loss_ref[...] = (stack_ref[at : at + 1, 0:1] + stack_ref[at + 1 : at + 2, 0:1]) / samples_all


def return_rows(base_ref, arrived_ref, send_ref, count_ref, hub_ref, mean_ref, out_ref, pick_ref, padded_ref):
    pick_matrix(send_ref, count_ref, hub_ref, pick_ref)
    padded_ref[...] = jnp.zeros_like(padded_ref)
    padded_ref[:, 0 : mean_ref.shape[1]] = mean_ref[...]
    high, low = split(tn(pick_ref[...], arrived_ref[...]))
    out_ref[...] = base_ref[...] + nt(high, padded_ref[...]) + nt(low, padded_ref[...])


def shape(dims, dtype):
    return jax.ShapeDtypeStruct(dims, dtype)


def swap(values, axis):
    return lax.all_to_all(values, axis, split_axis=0, concat_axis=0, tiled=True)


def on_device(
    features,
    hub_list,
    send_list,
    send_count,
    tile_dst,
    tile_src,
    tile_count,
    tile_adj,
    sample_ids,
    labels,
    first_self,
    first_mean,
    second_self,
    second_mean,
):
    nodes, inputs = features.shape
    width, classes = second_self.shape
    groups = lax.axis_size("grp")
    peers = lax.axis_size("dev")
    sends = send_list[0]
    capacity = sends.shape[1]
    group_hubs = peers * hub_list.shape[1]
    hubs = groups * group_hubs
    table = nodes + hubs + peers * capacity
    slots = peers * SLOTS
    padded = 2 * TILE
    samples_all = float(sample_ids.shape[1] * groups * peers)
    pick = pltpu.VMEM((slots, nodes), BF16)

    rows = kernel_call(
        send_features, shape((slots, inputs), BF16), [pick], [VM, VM, VM, SM]
    )(features, sends, send_count, hub_list)
    feature_arrived = swap(rows.reshape(peers, SLOTS, inputs), "dev").reshape(slots, inputs)

    dense, turned, degree = kernel_call(
        build_dense,
        (shape((nodes, table), BF16), shape((table, nodes), BF16), shape((nodes, TILE), F32)),
        in_specs=[VM, SM, SM, SM],
        flops=2 * nodes * table * TILE,
        moved=8 * MIB,
    )(tile_adj, tile_dst, tile_src, tile_count)

    gather_hubs = kernel_call(spread_hubs, shape((groups, group_hubs, inputs), BF16))
    feature_hubs = swap(gather_hubs(feature_arrived), "grp").reshape(hubs, inputs)
    mean_rows, rows = kernel_call(
        first_mean_rows,
        (shape((nodes, inputs), BF16), shape((slots, inputs), BF16)),
        [pltpu.VMEM((table, inputs), BF16), pick],
        [VM] * 7 + [SM],
    )(features, feature_hubs, feature_arrived, dense, degree, sends, send_count, hub_list)
    mean_arrived = swap(rows.reshape(peers, SLOTS, inputs), "dev").reshape(slots, inputs)
    mean_hubs = swap(gather_hubs(mean_arrived), "grp").reshape(hubs, inputs)

    share = STACK_ROWS // groups
    hidden, base, edges, partial = kernel_call(
        functools.partial(main_part, samples_all),
        (
            shape((nodes, width), BF16),
            shape((nodes, width), F32),
            shape((peers * capacity, padded), BF16),
            shape((groups, TILE + 2 * share, padded), BF16),
        ),
        [
            pltpu.VMEM((table, 2 * inputs), BF16),
            pltpu.VMEM((table, width), BF16),
            pltpu.VMEM((2 * inputs, width), BF16),
            pltpu.VMEM((width, padded), BF16),
            pltpu.VMEM((width, 2 * padded), BF16),
            pltpu.VMEM((nodes, 2 * padded), BF16),
            pltpu.VMEM((STACK_ROWS, width), F32),
        ],
        limit=48,
    )(
        features, feature_hubs, feature_arrived, mean_rows, mean_hubs, mean_arrived,
        dense, turned, degree, sample_ids, labels.reshape(1, nodes),
        first_self, first_mean, second_self, second_mean,
    )
    partial = swap(partial, "grp")
    rows = kernel_call(
        sum_groups,
        shape((slots, padded), BF16),
        [pltpu.VMEM(partial.shape[1:], F32), pltpu.VMEM((peers, SLOTS - HUB_AT, padded), F32)],
    )(partial, edges)
    arrived = swap(rows.reshape(peers, SLOTS, padded), "dev").reshape(slots, padded)

    pieces = kernel_call(sum_peers, shape((peers, SLOTS - HUB_AT, TILE), F32))(arrived)
    pieces = swap(pieces, "dev")
    grad_hidden = kernel_call(
        return_rows,
        shape((nodes, width), F32),
        [pick, pltpu.VMEM((width, padded), BF16)],
        [VM, VM, VM, VM, SM, VM],
        flops=2 * nodes * (slots * padded + 2 * width * padded),
        moved=6 * MIB,
    )(base, arrived, sends, send_count, hub_list, second_mean)
    stack = kernel_call(
        join_pieces, shape((groups, share, width), F32), [pltpu.VMEM((share, width), F32)]
    )(pieces)
    stack = swap(stack, "grp").reshape(STACK_ROWS, width)
    first_self_sum, first_mean_sum, self_sum, mean_sum, loss = kernel_call(
        functools.partial(weight_outputs, samples_all),
        (
            shape(first_self.shape, F32),
            shape(first_mean.shape, F32),
            shape((width, classes), F32),
            shape((width, classes), F32),
            shape((1, 1), F32),
        ),
    )(stack)
    return hidden, grad_hidden, loss[0, 0], first_self_sum, first_mean_sum, self_sum, mean_sum


def solution(mesh):
    both = ("grp", "dev")
    placed = (
        P(both, None),
        P(both, None),
        P(both, None, None),
        P(both, None),
        P(both, None),
        P(both, None),
        P(both),
        P(both, None, None),
        P(both, None),
        P(both),
        P(),
        P(),
        P(),
        P(),
    )
    return jax.shard_map(
        on_device,
        mesh=mesh,
        in_specs=placed,
        out_specs=(P(both, None), P(both, None), P(), P(), P(), P(), P()),
        check_vma=False,
    )
```

time: 845 us -> 191 us (0.23)
  waiting for transfers between devices: 524 us -> 21 us
  local copies, waits for them, and re-layouts: 69.2 us -> 12.9 us
  matrix products: 43.8 us -> 0 us
  blocking collectives: 140 us -> 103 us
  Pallas kernels: 0 us -> 29.3 us
  other arithmetic: 22.6 us -> 0 us
  between operations: 16.7 us -> 1.52 us
    psum x2 -> x0, waiting for transfers between devices: 418 us -> none  [the longest x1 234 us: on_device(): summed = lax.psum(hub_part, ('grp', 'dev'))]
    all_to_all x0 -> x5, blocking collectives: none -> 103 us  [swap(): return lax.all_to_all(values, axis, split_axis=0, concat_axis=0, tiled=True)]
    all_gather x1 -> x0, waiting for transfers between devices: 92.6 us -> none  [on_device(): lax.all_gather(hidden[hubs], ('grp', 'dev'), axis=0, tiled=True)]
    psum x1 -> x0, blocking collectives: 77.7 us -> none  [on_device(): lax.psum((first_self_sum, first_mean_sum, sum_self, sum_mean, loss_part),...]
    all_gather x1 -> x0, blocking collectives: 62.4 us -> none  [on_device(): lax.all_gather(features[hubs], ('grp', 'dev'), axis=0, tiled=True)]
    dot_general x17 -> x0, matrix products: 43.8 us -> none  [the longest x2 10.5 us: aggregate(): jnp.einsum('tij,tjw->tiw', adjacent, picked, preferred_element_type=jnp.f...]
    pallas_call x0 -> x11, Pallas kernels: none -> 29.3 us  [the longest x1 14 us: on_device(): kernel_call(functools.partial(main_part, samples_all), (shape((nodes, wid...]
    dot_general x5 -> x0, local copies, waits for them, and re-layouts: 23.4 us -> none  [the longest x2 12.7 us: aggregate(): jnp.einsum('tij,tjw->tiw', adjacent, picked, preferred_element_type=jnp.f...]
  transfers between devices with their start and end apart: 6 -> 3, of which waited for: 4 -> 2; matrix products, arithmetic and copies ran while one was open for 4% -> 0% of each run, Pallas kernels for 0% -> 4%
where the time goes in v1:
time: 191 us; the launch traced here: 190 us
  blocking collectives  103 us (54%)
  Pallas kernels  29.3 us (15%)
  starting transfers between devices  23 us (12%)
  waiting for transfers between devices  21 us (11%)
  local copies, waits for them, and re-layouts  12.9 us (7%)
    all_to_all x5, blocking collectives, swap(): return lax.all_to_all(values, axis, split_axis=0, concat_axis=0, tiled=True)  103 us
    all_to_all x3, starting transfers between devices, swap(): return lax.all_to_all(values, axis, split_axis=0, concat_axis=0, tiled=True)  23 us
    all_to_all x3, waiting for transfers between devices, swap(): return lax.all_to_all(values, axis, split_axis=0, concat_axis=0, tiled=True)  21 us
    pallas_call x1, Pallas kernels, on_device(): kernel_call(functools.partial(main_part, samples_all), (shape((nodes, wid...  14 us
    unnamed x60, local copies, waits for them, and re-layouts  12.9 us
  transfers between devices with their start and end apart: 3, of which 2 were waited for; matrix products, arithmetic and copies ran while one was open for 0% of the time, Pallas kernels for 4%

profile of v1, /device:TPU:1, one launch (start us, length us, event | category | flops | bytes accessed | tf_op | source)
XLA Modules:
  0.0 190.4 jit_solution(8859747545917087196)
XLA Ops:
  3.6 1.2 shard_map.189
  4.8 23.5 %all_to_all.40 = bf16[32,48,128]{2,1,0:T(8,128)(2,1)S(1)} all-to-all(bf16[32,48,128]{2,1,0:T(8,128)(2,1)S(1)} %bitcast.23), channel_id=1, replica_groups=mesh['grp'=8,'dev'=32] {'dev'}, dimensions={0} | all-to-all | bytes 786432 | tf_op jit(solution)/shard_map/all_to_all | solution.py:312
  28.3 1.0 shard_map.190
  29.3 8.1 %all-to-all-start.1 = ((bf16[8,128,128]{2,1,0:T(8,128)(2,1)}), bf16[8,128,128]{2,1,0:T(8,128)(2,1)S(1)}, u32[]{:S(2)}, u32[]{:S(2)}) async-start(bf16[8,128,128]{2,1,0:T(8,128)(2,1)} %shard_map.190), calls=%async_computation.1 | async-start | bytes 524288 | tf_op jit(solution)/shard_map/all_to_all | solution.py:312
  38.1 1.2 copy-done.23
  39.3 3.5 %shard_map.191 = (bf16[512,2560]{1,0:T(8,128)(2,1)S(1)}, bf16[2560,512]{1,0:T(8,128)(2,1)S(1)}, f32[512,128]{1,0:T(8,128)S(1)}) custom-call(bf16[32,128,128]{2,1,0:T(8,128)(2,1)S(1)} %copy-done.23, s32[1,32]{1,0:T(1,128)S(1)} %copy-done.24, s32[1,32]{1,0:T(1,128)S(1)} %copy-done.25, s32[1]{0:T(128)S(6)} %copy.26.count_ref), custom_call_target="tpu_custom_call" | custom-call | flops 335544320 | bytes 8388608 | tf_op jit(solution)/shard_map/pallas_call | solution.py:350
  42.9 1.5 copy-done.1
  45.2 1.1 copy-done.7
  46.3 2.7 %shard_map.192 = (bf16[512,128]{1,0:T(8,128)(2,1)S(1)}, bf16[1536,128]{1,0:T(8,128)(2,1)S(1)}) custom-call(bf16[512,128]{1,0:T(8,128)(2,1)S(1)} %copy-done.3, bf16[1024,128]{1,0:T(8,128)(2,1)S(1)} %bitcast.21, bf16[1536,128]{1,0:T(8,128)(2,1)S(1)} %bitcast.15, bf16[512,2560]{1,0:T(8,128)(2,1)S(1)} %get-tuple-element.21.dense_ref, f32[512,128]{1,0:T(8,128)S(1)} %copy-done.7, ...), custom_call_target="tpu_custom_call" | custom-call | tf_op jit(solution)/shard_map/pallas_call | solution.py:360
  49.1 17.0 %all_to_all.41 = bf16[32,48,128]{2,1,0:T(8,128)(2,1)S(1)} all-to-all(bf16[32,48,128]{2,1,0:T(8,128)(2,1)S(1)} %bitcast.25), channel_id=1, replica_groups=mesh['grp'=8,'dev'=32] {'dev'}, dimensions={0} | all-to-all | bytes 786432 | tf_op jit(solution)/shard_map/all_to_all | solution.py:312
  66.1 1.0 shard_map.193
  67.1 7.7 %all-to-all-start.3 = ((bf16[8,128,128]{2,1,0:T(8,128)(2,1)}), bf16[8,128,128]{2,1,0:T(8,128)(2,1)S(1)}, u32[]{:S(2)}, u32[]{:S(2)}) async-start(bf16[8,128,128]{2,1,0:T(8,128)(2,1)} %shard_map.193), calls=%async_computation.3 | async-start | bytes 524288 | tf_op jit(solution)/shard_map/all_to_all | solution.py:312
  75.1 6.2 %all-to-all-done.3 = bf16[8,128,128]{2,1,0:T(8,128)(2,1)S(1)} async-done(((bf16[8,128,128]{2,1,0:T(8,128)(2,1)}), bf16[8,128,128]{2,1,0:T(8,128)(2,1)S(1)}, u32[]{:S(2)}, u32[]{:S(2)}) %all-to-all-start.3) | async-done | bytes 262176 | tf_op jit(solution)/shard_map/all_to_all | solution.py:312
  84.4 14.0 %shard_map.194 = (bf16[512,512]{1,0:T(8,128)(2,1)}, f32[512,512]{1,0:T(8,128)S(1)}, bf16[1024,256]{1,0:T(8,128)(2,1)S(1)}, bf16[8,288,256]{2,1,0:T(8,128)(2,1)S(1)}) custom-call(bf16[512,128]{1,0:T(8,128)(2,1)S(1)} %copy-done.3, bf16[1024,128]{1,0:T(8,128)(2,1)S(1)} %bitcast.22, bf16[1536,128]{1,0:T(8,128)(2,1)S(1)} %bitcast.16, ...), custom_call_target="tpu_custom_call" | custom-call | tf_op jit(solution)/shard_map/pallas_call | solution.py:370
  98.5 20.1 %all_to_all.42.arrived_ref = bf16[8,288,256]{2,1,0:T(8,128)(2,1)S(1)} all-to-all(bf16[8,288,256]{2,1,0:T(8,128)(2,1)S(1)} %get-tuple-element.28), channel_id=1, replica_groups=mesh['grp'=8,'dev'=32] {'grp'}, dimensions={0} | all-to-all | bytes 2359296 | tf_op jit(solution)/shard_map/all_to_all | solution.py:312
  119.0 24.8 %all_to_all.43 = bf16[32,48,256]{2,1,0:T(8,128)(2,1)S(1)} all-to-all(bf16[32,48,256]{2,1,0:T(8,128)(2,1)S(1)} %bitcast.20), channel_id=1, replica_groups=mesh['grp'=8,'dev'=32] {'dev'}, dimensions={0} | all-to-all | bytes 1572864 | tf_op jit(solution)/shard_map/all_to_all | solution.py:312
  143.8 17.4 %all_to_all.44.arrived_ref = f32[32,16,128]{2,1,0:T(8,128)S(1)} all-to-all(f32[32,16,128]{2,1,0:T(8,128)S(1)} %shard_map.197), channel_id=1, replica_groups=mesh['grp'=8,'dev'=32] {'dev'}, dimensions={0} | all-to-all | bytes 524288 | tf_op jit(solution)/shard_map/all_to_all | solution.py:312
  161.2 1.2 shard_map.198
  162.4 7.2 %all-to-all-start.7 = ((f32[8,80,512]{2,1,0:T(8,128)}), f32[8,80,512]{2,1,0:T(8,128)S(1)}, u32[]{:S(2)}, u32[]{:S(2)}) async-start(f32[8,80,512]{2,1,0:T(8,128)} %shard_map.198), calls=%async_computation.7 | async-start | bytes 2621440 | tf_op jit(solution)/shard_map/all_to_all | solution.py:312
  169.6 3.1 %shard_map.196 = f32[512,512]{1,0:T(8,128)} custom-call(f32[512,512]{1,0:T(8,128)S(1)} %copy-done.5, bf16[1536,256]{1,0:T(8,128)(2,1)S(1)} %bitcast.13, s32[32,32]{1,0:T(8,128)S(1)} %bitcast.28, s32[1,32]{1,0:T(1,128)S(1)} %copy-done.17, s32[1,4]{1,0:T(1,128)S(1)} %copy-done.20, bf16[512,172]{1,0:T(8,128)(2,1)S(1)} %copy.22.second_mean_ref.mean_ref), custom_call_target="tpu_custom_call" | custom-call | flops 671088640 | bytes 6291456 | tf_op jit(solution)/shard_map/pallas_call | solution.py:403
  172.7 14.8 %all-to-all-done.7 = f32[8,80,512]{2,1,0:T(8,128)S(1)} async-done(((f32[8,80,512]{2,1,0:T(8,128)}), f32[8,80,512]{2,1,0:T(8,128)S(1)}, u32[]{:S(2)}, u32[]{:S(2)}) %all-to-all-start.7) | async-done | bytes 1310752 | tf_op jit(solution)/shard_map/all_to_all | solution.py:312
  187.5 1.1 shard_map.199
  188.6 0.9 copy.24
  189.5 0.9 copy.25
  (58 shorter events, 7.6 us)
Async XLA Ops:
  0.6 37.5 %copy-start.25 = (s32[1,32]{1,0:T(1,128)S(1)}, s32[1,32]{1,0:T(1,128)}, u32[]{:S(2)}) copy-start(s32[1,32]{1,0:T(1,128)} %src_ref.1) | copy-start | bytes 388
  0.6 37.5 %copy-start.24 = (s32[1,32]{1,0:T(1,128)S(1)}, s32[1,32]{1,0:T(1,128)}, u32[]{:S(2)}) copy-start(s32[1,32]{1,0:T(1,128)} %dst_ref.1) | copy-start | bytes 388
  0.7 0.9 copy-start.2
  28.3 16.8 %copy-start.3 = (bf16[512,128]{1,0:T(8,128)(2,1)S(1)}, bf16[512,128]{1,0:T(8,128)(2,1)}, u32[]{:S(2)}) copy-start(bf16[512,128]{1,0:T(8,128)(2,1)} %features_ref.5) | copy-start | bytes 393220
  28.3 16.8 %copy-start.10 = (s32[1,32,32]{2,1,0:T(8,128)S(1)}, s32[1,32,32]{2,1,0:T(8,128)}, u32[]{:S(2)}) copy-start(s32[1,32,32]{2,1,0:T(8,128)} %param.16) | copy-start | bytes 12292
  28.3 16.8 %copy-start.16 = (s32[1,32]{1,0:T(1,128)S(1)}, s32[1,32]{1,0:T(1,128)}, u32[]{:S(2)}) copy-start(s32[1,32]{1,0:T(1,128)} %count_ref.6) | copy-start | bytes 388
  28.3 16.8 %copy-start.19 = (s32[1,4]{1,0:T(1,128)S(1)}, s32[1,4]{1,0:T(1,128)}, u32[]{:S(2)}) copy-start(s32[1,4]{1,0:T(1,128)} %hub_ref.3) | copy-start | bytes 52
  29.3 15.8 %all-to-all-start.1 = ((bf16[8,128,128]{2,1,0:T(8,128)(2,1)}), bf16[8,128,128]{2,1,0:T(8,128)(2,1)S(1)}, u32[]{:S(2)}, u32[]{:S(2)}) async-start(bf16[8,128,128]{2,1,0:T(8,128)(2,1)} %shard_map.190), calls=%async_computation.1 | async-start | bytes 524288 | tf_op jit(solution)/shard_map/all_to_all | solution.py:312
  38.1 1.2 copy-start.23
  42.9 1.5 copy-start.1
  45.1 3.9 %copy-start = (bf16[512,2560]{1,0:T(8,128)(2,1)}, bf16[512,2560]{1,0:T(8,128)(2,1)S(1)}, u32[]{:S(2)}) copy-start(bf16[512,2560]{1,0:T(8,128)(2,1)S(1)} %get-tuple-element.21.dense_ref) | copy-start | bytes 7864324
  45.2 1.2 copy-start.7
  49.0 17.1 %copy-start.13 = (bf16[512,128]{1,0:T(8,128)(2,1)}, bf16[512,128]{1,0:T(8,128)(2,1)S(1)}, u32[]{:S(2)}) copy-start(bf16[512,128]{1,0:T(8,128)(2,1)S(1)} %get-tuple-element.23.mean_ref) | copy-start | bytes 393220
  49.0 25.7 %copy-start.26 = (bf16[512,172]{0,1:T(8,128)(2,1)S(1)}, bf16[512,172]{0,1:T(8,128)(2,1)}, u32[]{:S(2)}) copy-start(bf16[512,172]{0,1:T(8,128)(2,1)} %param.27) | copy-start | bytes 528388
  49.0 25.9 %copy-start.27 = (bf16[512,172]{0,1:T(8,128)(2,1)S(1)}, bf16[512,172]{0,1:T(8,128)(2,1)}, u32[]{:S(2)}) copy-start(bf16[512,172]{0,1:T(8,128)(2,1)} %param.26) | copy-start | bytes 528388
  49.1 32.2 %copy-start.8 = (f32[512,128]{1,0:T(8,128)S(1)}, f32[512,128]{1,0:T(8,128)}, u32[]{:S(2)}) copy-start(f32[512,128]{1,0:T(8,128)} %copy-done.6) | copy-start | bytes 786436
  49.1 32.2 %copy-start.11 = (bf16[128,512]{1,0:T(8,128)(2,1)S(1)}, bf16[128,512]{1,0:T(8,128)(2,1)}, u32[]{:S(2)}) copy-start(bf16[128,512]{1,0:T(8,128)(2,1)} %first_self_ref.1) | copy-start | bytes 393220
  67.1 14.2 %all-to-all-start.3 = ((bf16[8,128,128]{2,1,0:T(8,128)(2,1)}), bf16[8,128,128]{2,1,0:T(8,128)(2,1)S(1)}, u32[]{:S(2)}, u32[]{:S(2)}) async-start(bf16[8,128,128]{2,1,0:T(8,128)(2,1)} %shard_map.193), calls=%async_computation.3 | async-start | bytes 524288 | tf_op jit(solution)/shard_map/all_to_all | solution.py:312
  81.3 0.9 copy-start.12
  98.5 20.5 %copy-start.4 = (f32[512,512]{1,0:T(8,128)}, f32[512,512]{1,0:T(8,128)S(1)}, u32[]{:S(2)}) copy-start(f32[512,512]{1,0:T(8,128)S(1)} %get-tuple-element.27.base_ref) | copy-start | bytes 3145732
  162.4 7.2 %copy-start.5 = (f32[512,512]{1,0:T(8,128)S(1)}, f32[512,512]{1,0:T(8,128)}, u32[]{:S(2)}) copy-start(f32[512,512]{1,0:T(8,128)} %copy-done.4) | copy-start | bytes 3145732
  162.4 7.2 %copy-start.17 = (s32[1,32]{1,0:T(1,128)S(1)}, s32[1,32]{1,0:T(1,128)}, u32[]{:S(2)}) copy-start(s32[1,32]{1,0:T(1,128)} %count_ref.6) | copy-start | bytes 388
  162.4 7.2 %copy-start.20 = (s32[1,4]{1,0:T(1,128)S(1)}, s32[1,4]{1,0:T(1,128)}, u32[]{:S(2)}) copy-start(s32[1,4]{1,0:T(1,128)} %hub_ref.3) | copy-start | bytes 52
  162.4 25.1 %all-to-all-start.7 = ((f32[8,80,512]{2,1,0:T(8,128)}), f32[8,80,512]{2,1,0:T(8,128)S(1)}, u32[]{:S(2)}, u32[]{:S(2)}) async-start(f32[8,80,512]{2,1,0:T(8,128)} %shard_map.198), calls=%async_computation.7 | async-start | bytes 2621440 | tf_op jit(solution)/shard_map/all_to_all | solution.py:312
  (7 other events, 5.0 us)

commit v2 on v1

v2 whole, which is shorter than its diff:
```python
import functools

import jax
import jax.numpy as jnp
from jax import lax
from jax.experimental import pallas as pl
from jax.experimental.pallas import tpu as pltpu
from jax.sharding import PartitionSpec as P

F32 = jnp.float32
BF16 = jnp.bfloat16
I32 = jnp.int32
MIB = 1 << 20
TILE = 128
HALF = 64
PEERS = 32
CHIPS = 4
CORES = 2
HUBS_EACH = 4
CAPACITY = 32
PEER_HUBS = CORES * CHIPS * HUBS_EACH
FORWARD_ROWS = CAPACITY + PEER_HUBS
EDGE_ROWS = CAPACITY + CAPACITY // 2
HUB_ROWS = CHIPS * HUBS_EACH
HUB_PACKED = HUB_ROWS + HUB_ROWS // 2
STACK_ROWS = 640
SELF_AT = 256
LOSS_AT = 440
MEAN_AT = 448
CLASS_ROWS = 176
PIECE = STACK_ROWS // CORES * 4 // PEERS
SUM_ROWS = HUB_PACKED + PIECE
BACK_ROWS = EDGE_ROWS + SUM_ROWS
PIECE_ROWS = PIECE + 8

VM = pl.BlockSpec(memory_space=pltpu.VMEM)
SM = pl.BlockSpec(memory_space=pltpu.SMEM)
ANY = pl.BlockSpec(memory_space=pl.ANY)


def nn(left, right):
    return jnp.dot(left, right, preferred_element_type=F32)


def nt(left, right):
    return lax.dot_general(left, right, (((1,), (1,)), ((), ())), preferred_element_type=F32)


def tn(left, right):
    return lax.dot_general(left, right, (((0,), (0,)), ((), ())), preferred_element_type=F32)


def split(values):
    high = values.astype(BF16)
    low = (values - high.astype(F32)).astype(BF16)
    return high, low


def one_hot(hit):
    return jnp.where(hit, 1.0, 0.0).astype(BF16)


def iota(dims, axis):
    return lax.broadcasted_iota(I32, dims, axis)


def kernel_call(body, outs, scratch=(), in_specs=None, limit=24, flops=0, moved=0):
    placed = {} if in_specs is None else {"in_specs": in_specs}
    return pl.pallas_call(
        body,
        out_shape=outs,
        **placed,
        scratch_shapes=list(scratch),
        compiler_params=pltpu.CompilerParams(vmem_limit_bytes=limit * MIB),
        cost_estimate=pl.CostEstimate(flops=flops, bytes_accessed=moved, transcendentals=0),
    )


def position():
    group = lax.axis_index("grp")
    return group // CORES, group % CORES


def hub_picks(hub_ref, core, nodes):
    row = iota((16, nodes), 0)
    found = jnp.full((16, nodes), -1, I32)
    for k in range(HUBS_EACH):
        found = jnp.where(row == core * HUBS_EACH + k, hub_ref[0, k], found)
    return one_hot(found == iota((16, nodes), 1))


def hub_features(features_ref, hub_ref, out_ref):
    unused, core = position()
    out_ref[...] = nn(hub_picks(hub_ref, core, features_ref.shape[0]), features_ref[...]).astype(BF16)


def edge_picks(send_ref, count_ref, pick_ref):
    nodes = pick_ref.shape[1]
    send = jnp.transpose(send_ref[...])
    send = jnp.where(iota(send.shape, 0) < count_ref[...], send, -1)
    lane = iota((CAPACITY, nodes), 1)
    for n in range(PEERS):
        pick_ref[n * CAPACITY : (n + 1) * CAPACITY, :] = one_hot(send[:, n : n + 1] == lane)


def build_dense(adj_ref, dst_ref, src_ref, count_ref, hub_ref, dense_ref, turned_ref, degree_ref, hub_dense_ref, order_ref):
    nodes = dense_ref.shape[0]
    hubs = order_ref.shape[0]
    dense_ref[...] = jnp.zeros_like(dense_ref)
    turned_ref[...] = jnp.zeros_like(turned_ref)

    def add(t, carry):
        rows = pl.ds(pl.multiple_of(dst_ref[0, t] * TILE, TILE), TILE)
        columns = pl.ds(pl.multiple_of(src_ref[0, t] * TILE, TILE), TILE)
        tile = adj_ref[t]
        dense_ref[rows, columns] += tile
        turned_ref[columns, rows] += jnp.transpose(tile)
        return carry

    lax.fori_loop(0, count_ref[0], add, 0)
    new = iota((hubs, 1), 0)
    member, core, chip, k = new >> 5, (new >> 4) & 1, (new >> 2) & 3, new & 3
    old = (chip * CORES + core) * (PEERS * HUBS_EACH) + member * HUBS_EACH + k
    order_ref[...] = one_hot(old == iota((hubs, hubs), 1))
    spot = slice(nodes, nodes + hubs)
    dense_ref[:, spot] = nt(dense_ref[:, spot], order_ref[...]).astype(BF16)
    turned_ref[spot, :] = nn(order_ref[...], turned_ref[spot, :]).astype(BF16)
    ones = jnp.ones((dense_ref.shape[1], TILE), BF16)
    degree_ref[...] = jnp.maximum(nn(dense_ref[...], ones), 1.0)
    unused, core = position()
    hub_dense_ref[...] = nn(hub_picks(hub_ref, core, nodes), dense_ref[...]).astype(BF16)


def fill(pick_ref, values_ref, *refs):
    *pair_refs, out_ref = refs
    chip, unused = position()
    hubs = jnp.zeros((PEER_HUBS, TILE), F32)
    row = iota((PEER_HUBS, 16), 0)
    i = iota((PEER_HUBS, 16), 1)
    for shift, pair_ref in enumerate(pair_refs):
        other = (chip + CHIPS - shift) % CHIPS
        place = one_hot((i < CORES * HUBS_EACH) & (row == (i >> 2) * HUB_ROWS + other * HUBS_EACH + (i & 3)))
        hubs += nn(place, pair_ref[...])
    hubs = hubs.astype(BF16)
    edges = nn(pick_ref[...], values_ref[...]).astype(BF16)
    for n in range(PEERS):
        at = n * FORWARD_ROWS
        out_ref[at : at + CAPACITY, :] = edges[n * CAPACITY : (n + 1) * CAPACITY]
        out_ref[at + CAPACITY : at + FORWARD_ROWS, :] = hubs


def assemble(table_ref, own_ref, arrived_ref, lanes):
    own = own_ref.shape[0]
    table_ref[0:own, lanes] = own_ref[...]
    for n in range(PEERS):
        at = n * FORWARD_ROWS
        hub_at = own + n * PEER_HUBS
        edge_at = own + PEERS * PEER_HUBS + n * CAPACITY
        table_ref[hub_at : hub_at + PEER_HUBS, lanes] = arrived_ref[at + CAPACITY : at + FORWARD_ROWS, :]
        table_ref[edge_at : edge_at + CAPACITY, lanes] = arrived_ref[at : at + CAPACITY, :]


def hub_means(features_ref, arrived_ref, hub_dense_ref, out_ref, table_ref):
    assemble(table_ref, features_ref, arrived_ref, slice(0, TILE))
    counts = hub_dense_ref[...]
    degree = jnp.maximum(nn(counts, jnp.ones((counts.shape[1], TILE), BF16)), 1.0)
    out_ref[...] = (nn(counts, table_ref[...]) / degree).astype(BF16)


def all_means(table_ref, dense_ref, degree_ref, out_ref):
    out_ref[...] = (nn(dense_ref[...], table_ref[...]) / degree_ref[...]).astype(BF16)


def join_rests(first, second):
    return first + pltpu.roll(second, HALF, 1)


def part_rests(packed):
    low = iota(packed.shape, 1) < HALF
    return jnp.where(low, packed, 0.0), jnp.where(low, pltpu.roll(packed, HALF, 1), 0.0)


def main_part(
    samples_all,
    feature_table_ref, mean_ref, mean_arrived_ref, dense_ref, turned_ref, degree_ref,
    sample_any, label_any, first_self_any, first_mean_any, second_self_any, second_mean_any,
    hidden_ref, base_ref, edge_ref, mine_ref, theirs_ref,
    table_ref, source_ref, scaled_ref, stack_ref, pay_ref,
    sample_ref, label_ref, first_ref, raw_self_ref, raw_mean_ref, self_ref, second_ref, sems,
):
    loads = [
        pltpu.make_async_copy(source, target, sems.at[i])
        for i, (source, target) in enumerate(
            (
                (first_self_any, first_ref.at[pl.ds(0, TILE)]),
                (first_mean_any, first_ref.at[pl.ds(TILE, TILE)]),
                (second_self_any, raw_self_ref),
                (second_mean_any, raw_mean_ref),
                (sample_any, sample_ref),
                (label_any, label_ref),
            )
        )
    ]
    for load in loads:
        load.start()
    nodes, width = hidden_ref.shape
    classes = raw_self_ref.shape[0]
    padded = self_ref.shape[0]
    chunks = table_ref.shape[0] // nodes
    table_ref[:, 0:TILE] = feature_table_ref[...]
    assemble(table_ref, mean_ref, mean_arrived_ref, slice(TILE, 2 * TILE))
    self_ref[...] = jnp.zeros_like(self_ref)
    second_ref[...] = jnp.zeros_like(second_ref)
    for load in loads:
        load.wait()
    self_ref[0:classes, :] = raw_self_ref[...]
    second_ref[0:classes, :] = raw_mean_ref[...]

    def rows_of(i):
        return pl.ds(pl.multiple_of(i * nodes, nodes), nodes)

    def forward(i, carry):
        rows = rows_of(i)
        linear = nn(table_ref[rows, :], first_ref[...])
        source_ref[rows, :] = jnp.maximum(linear, 0.0).astype(BF16)
        return carry

    lax.fori_loop(0, chunks, forward, 0)
    hidden = source_ref[0:nodes, :]
    hidden_ref[...] = hidden
    degree = degree_ref[:, 0:1]
    mean = (nn(dense_ref[...], source_ref[...]) / degree).astype(BF16)
    logits = nt(hidden, self_ref[...]) + nt(mean, second_ref[...])

    lane = iota((nodes, padded), 1)
    real = lane < classes
    node = iota((nodes, sample_ref.shape[1]), 0)
    hits = jnp.where(node == sample_ref[...], 1.0, 0.0)
    times = jnp.sum(hits, axis=1, keepdims=True)
    label = jnp.transpose(jnp.broadcast_to(label_ref[...], (8, nodes)))[:, 0:1]
    onehot = jnp.where(lane == label, 1.0, 0.0)
    top = jnp.max(jnp.where(real, logits, -jnp.inf), axis=1, keepdims=True)
    shifted = logits - top
    powers = jnp.where(real, jnp.exp(shifted), 0.0)
    total = jnp.sum(powers, axis=1, keepdims=True)
    chosen = jnp.sum(onehot * shifted, axis=1, keepdims=True)
    loss = jnp.sum(times * (jnp.log(total) - chosen), axis=0, keepdims=True)
    upstream = times * ((powers / total - onehot) / samples_all)
    upstream = upstream.astype(BF16)
    high, low = split(upstream.astype(F32) / degree)
    scaled_ref[:, 0:padded] = high
    scaled_ref[:, padded : 2 * padded] = low

    stack_ref[SELF_AT:, :] = jnp.zeros((STACK_ROWS - SELF_AT, width), F32)
    stack_ref[SELF_AT : SELF_AT + CLASS_ROWS, :] = tn(upstream, hidden)[0:CLASS_ROWS]
    stack_ref[MEAN_AT : MEAN_AT + CLASS_ROWS, :] = tn(upstream, mean)[0:CLASS_ROWS]
    loss_high = loss.astype(BF16).astype(F32)
    place = iota((8, width), 0)
    marks = jnp.where(place == 0, loss_high, 0.0)
    stack_ref[LOSS_AT : LOSS_AT + 8, :] = jnp.where(place == 1, loss - loss_high, marks)

    def back(rows):
        pair = nn(turned_ref[rows, :], scaled_ref[...])
        found = pair[:, 0:padded] + pair[:, padded : 2 * padded]
        high, low = split(found)
        return found, nn(high, second_ref[...]) + nn(low, second_ref[...])

    def weights(rows, grad):
        masked = jnp.where(source_ref[rows, :] > 0, grad, 0.0).astype(BF16)
        return tn(table_ref[rows, :], masked)

    own = rows_of(0)
    unused, spread = back(own)
    base = nt(upstream, jnp.transpose(self_ref[...])) + spread
    base_ref[...] = base
    stack_ref[0 : 2 * TILE, :] = weights(own, base)
    each = nodes // CAPACITY

    def hub_chunk(i, carry):
        rows = rows_of(i + 1)
        found, spread = back(rows)
        stack_ref[0 : 2 * TILE, :] += weights(rows, spread)
        for p in range(each):
            for core in range(CORES):
                at = p * PEER_HUBS + core * HUB_ROWS
                rest = found[at : at + HUB_ROWS, TILE:]
                pay_ref[core, i * each + p, 0:HUB_ROWS, :] = found[at : at + HUB_ROWS, 0:TILE]
                pay_ref[core, i * each + p, HUB_ROWS:HUB_PACKED, :] = join_rests(
                    rest[0 : HUB_ROWS // 2], rest[HUB_ROWS // 2 :]
                )
        return carry

    lax.fori_loop(0, PEERS // each, hub_chunk, 0)

    def edge_chunk(i, carry):
        rows = rows_of(i + 1 + PEERS // each)
        found, spread = back(rows)
        stack_ref[0 : 2 * TILE, :] += weights(rows, spread)
        for p in range(each):
            at = p * CAPACITY
            rest = found[at : at + CAPACITY, TILE:]
            edge_ref[i * each + p, 0:CAPACITY, :] = found[at : at + CAPACITY, 0:TILE].astype(BF16)
            edge_ref[i * each + p, CAPACITY:EDGE_ROWS, :] = join_rests(
                rest[0 : CAPACITY // 2], rest[CAPACITY // 2 :]
            ).astype(BF16)
        return carry

    lax.fori_loop(0, PEERS // each, edge_chunk, 0)
    for core in range(CORES):
        for n in range(PEERS):
            at = core * (STACK_ROWS // CORES) + PIECE * (n % 8)
            lanes = slice(TILE * (n // 8), TILE * (n // 8 + 1))
            pay_ref[core, n, HUB_PACKED:SUM_ROWS, :] = stack_ref[at : at + PIECE, lanes]
    unused, core = position()
    mine_ref[...] = pay_ref[core].astype(BF16)
    theirs_ref[...] = pay_ref[1 - core].astype(BF16)


def sum_cores(mine_ref, arrived_ref, edge_ref, out_ref):
    out_ref[:, 0:EDGE_ROWS, :] = edge_ref[...]
    total = mine_ref[...].astype(F32) + arrived_ref[...].astype(F32)
    out_ref[:, EDGE_ROWS:BACK_ROWS, :] = total.astype(BF16)


def sum_peers(arrived_ref, out_ref):
    total = jnp.zeros((SUM_ROWS, TILE), F32)
    for n in range(PEERS):
        total += arrived_ref[n, EDGE_ROWS:BACK_ROWS, :].astype(F32)
    out_ref[...] = total


def sum_chips(*refs):
    *sum_refs, out_ref, total_ref = refs
    total = sum_refs[0][...]
    for sum_ref in sum_refs[1:]:
        total += sum_ref[...]
    total_ref[...] = total
    piece = total[HUB_PACKED:SUM_ROWS]
    rest = piece[0:8] - piece[0:8].astype(BF16).astype(F32)
    piece = jnp.concatenate([piece, rest], axis=0).astype(BF16)
    for n in range(PEERS):
        out_ref[n] = piece


def return_rows(base_ref, arrived_ref, total_ref, pick_ref, hub_ref, mean_any, out_ref, found_ref, raw_ref, second_ref, sem):
    load = pltpu.make_async_copy(mean_any, raw_ref, sem)
    load.start()
    nodes = out_ref.shape[0]
    for n in range(PEERS):
        at = n * CAPACITY
        found_ref[at : at + CAPACITY, 0:TILE] = arrived_ref[n, 0:CAPACITY, :]
        first, second = part_rests(arrived_ref[n, CAPACITY:EDGE_ROWS, :].astype(F32))
        found_ref[at : at + CAPACITY // 2, TILE:] = first.astype(BF16)
        found_ref[at + CAPACITY // 2 : at + CAPACITY, TILE:] = second.astype(BF16)
    first, second = part_rests(total_ref[HUB_ROWS:HUB_PACKED, :])
    hubs = jnp.concatenate([total_ref[0:HUB_ROWS, :], jnp.concatenate([first, second], axis=0)], axis=1)
    chip, unused = position()
    lane = iota((nodes, HUB_ROWS), 1)
    owner = jnp.full((nodes, HUB_ROWS), -1, I32)
    for k in range(HUBS_EACH):
        owner = jnp.where(lane == chip * HUBS_EACH + k, hub_ref[0, k], owner)
    owner = one_hot(owner == iota((nodes, HUB_ROWS), 0))
    high, low = split(hubs)
    rows = tn(pick_ref[...], found_ref[...]) + nn(owner, high) + nn(owner, low)
    second_ref[...] = jnp.zeros_like(second_ref)
    load.wait()
    second_ref[0 : raw_ref.shape[0], :] = raw_ref[...]
    high, low = split(rows)
    out_ref[...] = base_ref[...] + nn(high, second_ref[...]) + nn(low, second_ref[...])


def weight_outputs(samples_all, mine_ref, theirs_ref, first_self_ref, first_mean_ref, self_ref, mean_ref, loss_ref, stack_ref):
    unused, core = position()
    half = STACK_ROWS // CORES
    for n in range(PEERS):
        mine = mine_ref[n].astype(F32)
        theirs = theirs_ref[n].astype(F32)
        lanes = slice(TILE * (n // 8), TILE * (n // 8 + 1))
        at = PIECE * (n % 8)
        first = jnp.where(core == 0, mine, theirs)
        second = jnp.where(core == 0, theirs, mine)
        stack_ref[at : at + PIECE, lanes] = first[0:PIECE]
        stack_ref[half + at : half + at + PIECE, lanes] = second[0:PIECE]
        if lanes.start == 0 and half + at == LOSS_AT:
            loss = second[0:1, 0:1] + second[1:2, 0:1] + second[PIECE : PIECE + 1, 0:1]
            loss_ref[...] = loss / samples_all
    classes = self_ref.shape[0]
    first_self_ref[...] = stack_ref[0:TILE, :]
    first_mean_ref[...] = stack_ref[TILE : 2 * TILE, :]
    self_ref[...] = stack_ref[SELF_AT : SELF_AT + classes, :]
    mean_ref[...] = stack_ref[MEAN_AT : MEAN_AT + classes, :]


def shape(dims, dtype):
    return jax.ShapeDtypeStruct(dims, dtype)


def swap(values):
    return lax.all_to_all(values, "dev", split_axis=0, concat_axis=0, tiled=True)


def to_core(values):
    return lax.ppermute(values, "grp", [(i, i ^ 1) for i in range(CHIPS * CORES)])


def to_chips(values):
    every = CHIPS * CORES
    return [
        lax.ppermute(values, "grp", [(i, (i + CORES * shift) % every) for i in range(every)])
        for shift in range(1, CHIPS)
    ]


def on_device(
    features,
    hub_list,
    send_list,
    send_count,
    tile_dst,
    tile_src,
    tile_count,
    tile_adj,
    sample_ids,
    labels,
    first_self,
    first_mean,
    second_self,
    second_mean,
):
    nodes, inputs = features.shape
    width, classes = second_self.shape
    hubs = CHIPS * CORES * PEERS * HUBS_EACH
    edges = PEERS * CAPACITY
    table = nodes + hubs + edges
    padded = 2 * TILE
    samples_all = float(sample_ids.shape[1] * CHIPS * CORES * PEERS)
    second_self = second_self.T
    second_mean = second_mean.T

    def exchange(own, values):
        pair = own + to_core(own)
        rows = kernel_call(fill, shape((PEERS * FORWARD_ROWS, inputs), BF16), moved=2 * MIB)(
            picks, values(), pair, *to_chips(pair)
        )
        return swap(rows.reshape(PEERS, FORWARD_ROWS, inputs)).reshape(PEERS * FORWARD_ROWS, inputs)

    own = kernel_call(hub_features, shape((16, inputs), BF16), in_specs=[VM, SM])(features, hub_list)
    picks = kernel_call(edge_picks, shape((edges, nodes), BF16), moved=2 * MIB)(send_list[0], send_count)
    feature_arrived = exchange(own, lambda: features)
    dense, turned, degree, hub_dense = kernel_call(
        build_dense,
        (
            shape((nodes, table), BF16),
            shape((table, nodes), BF16),
            shape((nodes, TILE), F32),
            shape((16, table), BF16),
        ),
        [pltpu.VMEM((hubs, hubs), BF16)],
        [VM, SM, SM, SM, SM],
        flops=4 * nodes * hubs * hubs,
        moved=16 * MIB,
    )(tile_adj, tile_dst, tile_src, tile_count, hub_list)
    own, feature_table = kernel_call(
        hub_means, (shape((16, inputs), BF16), shape((table, inputs), BF16))
    )(features, feature_arrived, hub_dense)
    mean_rows = kernel_call(
        all_means, shape((nodes, inputs), BF16), flops=2 * nodes * table * inputs, moved=4 * MIB
    )(feature_table, dense, degree)
    mean_arrived = exchange(own, lambda: mean_rows)

    hidden, base, edge_rows, mine, theirs = kernel_call(
        functools.partial(main_part, samples_all),
        (
            shape((nodes, width), BF16),
            shape((nodes, width), F32),
            shape((PEERS, EDGE_ROWS, TILE), BF16),
            shape((PEERS, SUM_ROWS, TILE), BF16),
            shape((PEERS, SUM_ROWS, TILE), BF16),
        ),
        [
            pltpu.VMEM((table, 2 * inputs), BF16),
            pltpu.VMEM((table, width), BF16),
            pltpu.VMEM((nodes, 2 * padded), BF16),
            pltpu.VMEM((STACK_ROWS, width), F32),
            pltpu.VMEM((CORES, PEERS, SUM_ROWS, TILE), F32),
            pltpu.VMEM(sample_ids.shape, I32),
            pltpu.VMEM((1, nodes), I32),
            pltpu.VMEM((2 * inputs, width), BF16),
            pltpu.VMEM((classes, width), BF16),
            pltpu.VMEM((classes, width), BF16),
            pltpu.VMEM((padded, width), BF16),
            pltpu.VMEM((padded, width), BF16),
            pltpu.SemaphoreType.DMA((6,)),
        ],
        [VM] * 6 + [ANY] * 6,
        limit=44,
    )(
        feature_table, mean_rows, mean_arrived, dense, turned, degree,
        sample_ids, labels.reshape(1, nodes), first_self, first_mean, second_self, second_mean,
    )
    rows = kernel_call(sum_cores, shape((PEERS, BACK_ROWS, TILE), BF16))(mine, to_core(theirs), edge_rows)
    arrived = swap(rows)
    sums = kernel_call(sum_peers, shape((SUM_ROWS, TILE), F32))(arrived)
    pieces, total = kernel_call(
        sum_chips, (shape((PEERS, PIECE_ROWS, TILE), BF16), shape((SUM_ROWS, TILE), F32))
    )(sums, *to_chips(sums))
    pieces = swap(pieces)
    grad_hidden = kernel_call(
        return_rows,
        shape((nodes, width), F32),
        [
            pltpu.VMEM((edges, padded), BF16),
            pltpu.VMEM((classes, width), BF16),
            pltpu.VMEM((padded, width), BF16),
            pltpu.SemaphoreType.DMA,
        ],
        [VM, VM, VM, VM, SM, ANY],
        flops=2 * nodes * (edges * padded + 2 * width * padded),
        moved=8 * MIB,
    )(base, arrived, total, picks, hub_list, second_mean)
    first_self_sum, first_mean_sum, self_sum, mean_sum, loss = kernel_call(
        functools.partial(weight_outputs, samples_all),
        (
            shape(first_self.shape, F32),
            shape(first_mean.shape, F32),
            shape((classes, width), F32),
            shape((classes, width), F32),
            shape((1, 1), F32),
        ),
        [pltpu.VMEM((STACK_ROWS, width), F32)],
    )(pieces, to_core(pieces))
    return hidden, grad_hidden, loss[0, 0], first_self_sum, first_mean_sum, self_sum.T, mean_sum.T


def solution(mesh):
    both = ("grp", "dev")
    placed = (
        P(both, None),
        P(both, None),
        P(both, None, None),
        P(both, None),
        P(both, None),
        P(both, None),
        P(both),
        P(both, None, None),
        P(both, None),
        P(both),
        P(),
        P(),
        P(),
        P(),
    )
    return jax.shard_map(
        on_device,
        mesh=mesh,
        in_specs=placed,
        out_specs=(P(both, None), P(both, None), P(), P(), P(), P(), P()),
        check_vma=False,
    )
```

time: 191 us -> 151 us (0.79)
  blocking collectives: 103 us -> 63 us
  starting transfers between devices: 23 us -> 37.9 us
  waiting for transfers between devices: 21 us -> 12.3 us
  local copies, waits for them, and re-layouts: 12.9 us -> 8.63 us
    all_to_all x5 -> x3, blocking collectives: 103 us -> 63 us  [swap(): lax.all_to_all(values, 'dev', split_axis=0, concat_axis=0, tiled=True)]
    ppermute x0 -> x13, starting transfers between devices: none -> 26.7 us  [the longest x4 19.3 us: to_core(): lax.ppermute(values, 'grp', [(i, i ^ 1) for i in range(CHIPS * CORES)])]
    all_to_all x3 -> x1, waiting for transfers between devices: 21 us -> 3.4 us  [swap(): lax.all_to_all(values, 'dev', split_axis=0, concat_axis=0, tiled=True)]
    all_to_all x3 -> x1, starting transfers between devices: 23 us -> 11.2 us  [swap(): lax.all_to_all(values, 'dev', split_axis=0, concat_axis=0, tiled=True)]
    ppermute x0 -> x13, waiting for transfers between devices: none -> 8.95 us  [the longest x9 5.77 us: to_chips(): lax.ppermute(values, 'grp', [(i, (i + CORES * shift) % every) for i in ra...]
    unnamed x60 -> x42, local copies, waits for them, and re-layouts: 12.9 us -> 8.63 us
    pallas_call x8 -> x10, Pallas kernels: 10.6 us -> 7.52 us  [the longest x1 3.35 us: on_device(): kernel_call(return_rows, shape((nodes, width), F32), [pltpu.VMEM((edges,...]
    pallas_call x1, Pallas kernels: 3.53 us -> 5.55 us  [on_device(): kernel_call(build_dense, (shape((nodes, table), BF16), shape((table, node...]
  transfers between devices with their start and end apart: 3 -> 14, of which waited for: 2 -> 10; matrix products, arithmetic and copies ran while one was open for 0% -> 0% of each run, Pallas kernels for 4% -> 7%
where the time goes in v2:
time: 151 us
  blocking collectives  63 us (42%)
  starting transfers between devices  37.9 us (25%)
  Pallas kernels  27.4 us (18%)
  waiting for transfers between devices  12.3 us (8%)
  local copies, waits for them, and re-layouts  8.63 us (6%)
  between operations  1.53 us (1%)
    all_to_all x3, blocking collectives, swap(): lax.all_to_all(values, 'dev', split_axis=0, concat_axis=0, tiled=True)  63 us
    ppermute x4, starting transfers between devices, to_core(): lax.ppermute(values, 'grp', [(i, i ^ 1) for i in range(CHIPS * CORES)])  19.3 us
    pallas_call x1, Pallas kernels, on_device(): kernel_call(functools.partial(main_part, samples_all), (shape((nodes, wid...  13.2 us
    all_to_all x1, starting transfers between devices, swap(): lax.all_to_all(values, 'dev', split_axis=0, concat_axis=0, tiled=True)  11.2 us
    unnamed x42, local copies, waits for them, and re-layouts  8.63 us
    ppermute x9, starting transfers between devices, to_chips(): lax.ppermute(values, 'grp', [(i, (i + CORES * shift) % every) for i in ra...  7.38 us
    ppermute x9, waiting for transfers between devices, to_chips(): lax.ppermute(values, 'grp', [(i, (i + CORES * shift) % every) for i in ra...  5.77 us
    pallas_call x1, Pallas kernels, on_device(): kernel_call(build_dense, (shape((nodes, table), BF16), shape((table, node...  5.55 us
  transfers between devices with their start and end apart: 14, of which 10 were waited for; matrix products, arithmetic and copies ran while one was open for 0% of the time, Pallas kernels for 7%

profile of v2, /device:TPU:1, one launch (start us, length us, event | category | flops | bytes accessed | tf_op | source)
XLA Modules:
  0.0 150.8 jit_solution(8932211574687935694)
XLA Ops:
  2.9 3.2 %collective-permute-start = (bf16[16,128]{1,0:T(8,128)(2,1)S(1)}, bf16[16,128]{1,0:T(8,128)(2,1)S(1)}, u32[]{:S(2)}, u32[]{:S(2)}) collective-permute-start(bf16[16,128]{1,0:T(8,128)(2,1)S(1)} %shard_map.190), channel_id=1, source_target_pairs={{0,32},{32,0},{64,96},{96,64},{128,160},{160,128},{192,224},{224,1... | collective-permute-start | bytes 12296 | tf_op jit(solution)/shard_map/ppermute | solution.py:403
  10.6 1.1 collective-permute-done.2.refs_2_
  12.8 1.3 shard_map.191
  14.1 11.2 %all-to-all-start = ((bf16[32,64,128]{2,1,0:T(8,128)(2,1)}), bf16[32,64,128]{2,1,0:T(8,128)(2,1)S(1)}, u32[]{:S(2)}, u32[]{:S(2)}) async-start(bf16[32,64,128]{2,1,0:T(8,128)(2,1)} %bitcast.1), calls=%async_computation | async-start | bytes 1048576 | tf_op jit(solution)/shard_map/all_to_all | solution.py:399
  26.0 5.5 %shard_map.192 = (bf16[512,2560]{1,0:T(8,128)(2,1)S(1)}, bf16[2560,512]{1,0:T(8,128)(2,1)S(1)}, f32[512,128]{1,0:T(8,128)S(1)}, bf16[16,2560]{1,0:T(8,128)(2,1)S(1)}) custom-call(bf16[32,128,128]{2,1,0:T(8,128)(2,1)S(1)} %copy-done.18, s32[1,32]{1,0:T(1,128)S(1)} %copy-done.19, s32[1,32]{1,0:T(1,128)S(1)} %copy-done.20, s32[1]{0:T(128)S(6)} %copy.21.count_ref, ...), custom_call_target="tpu_custom_call" | custom-call | flops 2147483648 | bytes 16777216 | tf_op jit(solution)/shard_map/pallas_call | solution.py:450
  31.5 1.5 copy-done
  33.0 1.5 %copy-done.3 = bf16[2560,512]{1,0:T(8,128)(2,1)} copy-done((bf16[2560,512]{1,0:T(8,128)(2,1)}, bf16[2560,512]{1,0:T(8,128)(2,1)S(1)}, u32[]{:S(2)}) %copy-start.3) | copy-done | bytes 2621464
  34.6 3.4 %all-to-all-done = bf16[32,64,128]{2,1,0:T(8,128)(2,1)S(1)} async-done(((bf16[32,64,128]{2,1,0:T(8,128)(2,1)}), bf16[32,64,128]{2,1,0:T(8,128)(2,1)S(1)}, u32[]{:S(2)}, u32[]{:S(2)}) %all-to-all-start) | async-done | bytes 524320 | tf_op jit(solution)/shard_map/all_to_all | solution.py:399
  38.2 5.3 %collective-permute-start.4 = (bf16[16,128]{1,0:T(8,128)(2,1)S(1)}, bf16[16,128]{1,0:T(8,128)(2,1)S(1)}, u32[]{:S(2)}, u32[]{:S(2)}) collective-permute-start(bf16[16,128]{1,0:T(8,128)(2,1)S(1)} %get-tuple-element.29), channel_id=1, source_target_pairs={{0,32},{32,0},{64,96},{96,64},{128,160},{160,128},{192,224},{224,1... | collective-permute-start | bytes 12296 | tf_op jit(solution)/shard_map/ppermute | solution.py:403
  44.3 1.1 collective-permute-start.7
  45.4 1.3 collective-permute-start.6
  47.0 1.7 %copy-done.1 = bf16[512,2560]{1,0:T(8,128)(2,1)S(1)} copy-done((bf16[512,2560]{1,0:T(8,128)(2,1)S(1)}, bf16[512,2560]{1,0:T(8,128)(2,1)}, u32[]{:S(2)}) %copy-start.1) | copy-done | bytes 2621464
  49.7 1.0 collective-permute-done.5.refs_1_
  51.2 17.7 %all_to_all.20 = bf16[32,64,128]{2,1,0:T(8,128)(2,1)S(1)} all-to-all(bf16[32,64,128]{2,1,0:T(8,128)(2,1)S(1)} %bitcast.13), channel_id=1, replica_groups=mesh['grp'=8,'dev'=32] {'dev'}, dimensions={0} | all-to-all | bytes 1048576 | tf_op jit(solution)/shard_map/all_to_all | solution.py:399
  69.0 13.2 %shard_map.196 = (bf16[512,512]{1,0:T(8,128)(2,1)}, f32[512,512]{1,0:T(8,128)S(1)}, bf16[32,48,128]{2,1,0:T(8,128)(2,1)S(1)}, bf16[32,64,128]{2,1,0:T(8,128)(2,1)S(1)}, bf16[32,64,128]{2,1,0:T(8,128)(2,1)S(1)}) custom-call(bf16[2560,128]{1,0:T(8,128)(2,1)S(1)} %get-tuple-element.26.table_ref.feature_table_ref, ...), custom_call_target="tpu_custom_call" | custom-call | tf_op jit(solution)/shard_map/pallas_call | solution.py:471
  82.2 5.2 %collective-permute-start.8 = (bf16[32,64,128]{2,1,0:T(8,128)(2,1)S(1)}, bf16[32,64,128]{2,1,0:T(8,128)(2,1)S(1)}, u32[]{:S(2)}, u32[]{:S(2)}) collective-permute-start(bf16[32,64,128]{2,1,0:T(8,128)(2,1)S(1)} %get-tuple-element.34), channel_id=1, source_target_pairs={{0,32},{32,0},{64,96},{96,64},{128,160},{160,128},{192,224},{224,1... | collective-permute-start | bytes 1572872 | tf_op jit(solution)/shard_map/ppermute | solution.py:403
  87.4 1.5 %collective-permute-done.8.arrived_ref = bf16[32,64,128]{2,1,0:T(8,128)(2,1)S(1)} collective-permute-done((bf16[32,64,128]{2,1,0:T(8,128)(2,1)S(1)}, bf16[32,64,128]{2,1,0:T(8,128)(2,1)S(1)}, u32[]{:S(2)}, u32[]{:S(2)}) %collective-permute-start.8) | collective-permute-done | bytes 524320 | tf_op jit(solution)/shard_map/ppermute | solution.py:403
  89.1 27.1 %all_to_all.21.arrived_ref = bf16[32,112,128]{2,1,0:T(8,128)(2,1)S(1)} all-to-all(bf16[32,112,128]{2,1,0:T(8,128)(2,1)S(1)} %shard_map.197), channel_id=1, replica_groups=mesh['grp'=8,'dev'=32] {'dev'}, dimensions={0} | all-to-all | bytes 1835008 | tf_op jit(solution)/shard_map/all_to_all | solution.py:399
  116.3 1.6 %collective-permute-start.11 = (f32[64,128]{1,0:T(8,128)S(1)}, f32[64,128]{1,0:T(8,128)S(1)}, u32[]{:S(2)}, u32[]{:S(2)}) collective-permute-start(f32[64,128]{1,0:T(8,128)S(1)} %shard_map.198.refs_0_), channel_id=1, source_target_pairs={{0,192},{32,224},{64,0},{96,32},{128,64},{160,96},{192,128},{224,1... | collective-permute-start | bytes 98312 | tf_op jit(solution)/shard_map/ppermute | solution.py:409
  119.4 2.8 %collective-permute-done.10.refs_2_ = f32[64,128]{1,0:T(8,128)S(1)} collective-permute-done((f32[64,128]{1,0:T(8,128)S(1)}, f32[64,128]{1,0:T(8,128)S(1)}, u32[]{:S(2)}, u32[]{:S(2)}) %collective-permute-start.10) | collective-permute-done | bytes 32800 | tf_op jit(solution)/shard_map/ppermute | solution.py:409
  122.6 18.2 %all_to_all.22.mine_ref = bf16[32,48,128]{2,1,0:T(8,128)(2,1)S(1)} all-to-all(bf16[32,48,128]{2,1,0:T(8,128)(2,1)S(1)} %get-tuple-element.37), channel_id=1, replica_groups=mesh['grp'=8,'dev'=32] {'dev'}, dimensions={0} | all-to-all | bytes 786432 | tf_op jit(solution)/shard_map/all_to_all | solution.py:399
  140.8 5.6 %collective-permute-start.12 = (bf16[32,48,128]{2,1,0:T(8,128)(2,1)S(1)}, bf16[32,48,128]{2,1,0:T(8,128)(2,1)S(1)}, u32[]{:S(2)}, u32[]{:S(2)}) collective-permute-start(bf16[32,48,128]{2,1,0:T(8,128)(2,1)S(1)} %all_to_all.22.mine_ref), channel_id=1, source_target_pairs={{0,32},{32,0},{64,96},{96,64},{128,160},{160,128},{192,224},{224,1... | collective-permute-start | bytes 1179656 | tf_op jit(solution)/shard_map/ppermute | solution.py:403
  146.4 3.4 %shard_map.200 = f32[512,512]{1,0:T(8,128)} custom-call(f32[512,512]{1,0:T(8,128)S(1)} %get-tuple-element.32.base_ref, bf16[32,112,128]{2,1,0:T(8,128)(2,1)S(1)} %all_to_all.21.arrived_ref, f32[64,128]{1,0:T(8,128)S(1)} %get-tuple-element.36.total_ref, bf16[1024,512]{1,0:T(8,128)(2,1)S(1)} %shard_map.189.pick_ref, s32[1,4]{1,0:T(1,128)S(1)} %copy-done.15, ...), custom_call_target="tpu_custom_call" | custom-call | flops 536870912 | bytes 8388608 | tf_op jit(solution)/shard_map/pallas_call | solution.py:508
  149.7 1.1 shard_map.201
  (64 shorter events, 12.7 us)
Async XLA Ops:
  2.2 23.7 %copy-start.15 = (s32[1,4]{1,0:T(1,128)S(1)}, s32[1,4]{1,0:T(1,128)}, u32[]{:S(2)}) copy-start(s32[1,4]{1,0:T(1,128)} %hub_ref.5) | copy-start | bytes 52
  2.2 23.7 %copy-start.19 = (s32[1,32]{1,0:T(1,128)S(1)}, s32[1,32]{1,0:T(1,128)}, u32[]{:S(2)}) copy-start(s32[1,32]{1,0:T(1,128)} %dst_ref.1) | copy-start | bytes 388
  2.2 23.8 %copy-start.20 = (s32[1,32]{1,0:T(1,128)S(1)}, s32[1,32]{1,0:T(1,128)}, u32[]{:S(2)}) copy-start(s32[1,32]{1,0:T(1,128)} %src_ref.1) | copy-start | bytes 388
  2.9 4.1 %collective-permute-start = (bf16[16,128]{1,0:T(8,128)(2,1)S(1)}, bf16[16,128]{1,0:T(8,128)(2,1)S(1)}, u32[]{:S(2)}, u32[]{:S(2)}) collective-permute-start(bf16[16,128]{1,0:T(8,128)(2,1)S(1)} %shard_map.190), channel_id=1, source_target_pairs={{0,32},{32,0},{64,96},{96,64},{128,160},{160,128},{192,224},{224,1... | collective-permute-start | bytes 12296 | tf_op jit(solution)/shard_map/ppermute | solution.py:403
  7.0 3.6 %collective-permute-start.3 = (bf16[16,128]{1,0:T(8,128)(2,1)S(1)}, bf16[16,128]{1,0:T(8,128)(2,1)S(1)}, u32[]{:S(2)}, u32[]{:S(2)}) collective-permute-start(bf16[16,128]{1,0:T(8,128)(2,1)S(1)} %add.6.refs_0_), channel_id=1, source_target_pairs={{0,192},{32,224},{64,0},{96,32},{128,64},{160,96},{192,128},{224,1... | collective-permute-start | bytes 12296 | tf_op jit(solution)/shard_map/ppermute | solution.py:409
  7.7 4.0 %collective-permute-start.2 = (bf16[16,128]{1,0:T(8,128)(2,1)S(1)}, bf16[16,128]{1,0:T(8,128)(2,1)S(1)}, u32[]{:S(2)}, u32[]{:S(2)}) collective-permute-start(bf16[16,128]{1,0:T(8,128)(2,1)S(1)} %add.6.refs_0_), channel_id=1, source_target_pairs={{0,128},{32,160},{64,192},{96,224},{128,0},{160,32},{192,64},{224,... | collective-permute-start | bytes 12296 | tf_op jit(solution)/shard_map/ppermute | solution.py:409
  8.2 3.7 %collective-permute-start.1 = (bf16[16,128]{1,0:T(8,128)(2,1)S(1)}, bf16[16,128]{1,0:T(8,128)(2,1)S(1)}, u32[]{:S(2)}, u32[]{:S(2)}) collective-permute-start(bf16[16,128]{1,0:T(8,128)(2,1)S(1)} %add.6.refs_0_), channel_id=1, source_target_pairs={{0,64},{32,96},{64,128},{96,160},{128,192},{160,224},{192,0},{224,... | collective-permute-start | bytes 12296 | tf_op jit(solution)/shard_map/ppermute | solution.py:409
  14.1 23.9 %all-to-all-start = ((bf16[32,64,128]{2,1,0:T(8,128)(2,1)}), bf16[32,64,128]{2,1,0:T(8,128)(2,1)S(1)}, u32[]{:S(2)}, u32[]{:S(2)}) async-start(bf16[32,64,128]{2,1,0:T(8,128)(2,1)} %bitcast.1), calls=%async_computation | async-start | bytes 1048576 | tf_op jit(solution)/shard_map/all_to_all | solution.py:399
  38.2 6.1 %collective-permute-start.4 = (bf16[16,128]{1,0:T(8,128)(2,1)S(1)}, bf16[16,128]{1,0:T(8,128)(2,1)S(1)}, u32[]{:S(2)}, u32[]{:S(2)}) collective-permute-start(bf16[16,128]{1,0:T(8,128)(2,1)S(1)} %get-tuple-element.29), channel_id=1, source_target_pairs={{0,32},{32,0},{64,96},{96,64},{128,160},{160,128},{192,224},{224,1... | collective-permute-start | bytes 12296 | tf_op jit(solution)/shard_map/ppermute | solution.py:403
  44.3 5.3 %collective-permute-start.7 = (bf16[16,128]{1,0:T(8,128)(2,1)S(1)}, bf16[16,128]{1,0:T(8,128)(2,1)S(1)}, u32[]{:S(2)}, u32[]{:S(2)}) collective-permute-start(bf16[16,128]{1,0:T(8,128)(2,1)S(1)} %add.7.refs_0_), channel_id=1, source_target_pairs={{0,192},{32,224},{64,0},{96,32},{128,64},{160,96},{192,128},{224,1... | collective-permute-start | bytes 12296 | tf_op jit(solution)/shard_map/ppermute | solution.py:409
  45.4 4.2 %collective-permute-start.6 = (bf16[16,128]{1,0:T(8,128)(2,1)S(1)}, bf16[16,128]{1,0:T(8,128)(2,1)S(1)}, u32[]{:S(2)}, u32[]{:S(2)}) collective-permute-start(bf16[16,128]{1,0:T(8,128)(2,1)S(1)} %add.7.refs_0_), channel_id=1, source_target_pairs={{0,128},{32,160},{64,192},{96,224},{128,0},{160,32},{192,64},{224,... | collective-permute-start | bytes 12296 | tf_op jit(solution)/shard_map/ppermute | solution.py:409
  46.8 4.0 %collective-permute-start.5 = (bf16[16,128]{1,0:T(8,128)(2,1)S(1)}, bf16[16,128]{1,0:T(8,128)(2,1)S(1)}, u32[]{:S(2)}, u32[]{:S(2)}) collective-permute-start(bf16[16,128]{1,0:T(8,128)(2,1)S(1)} %add.7.refs_0_), channel_id=1, source_target_pairs={{0,64},{32,96},{64,128},{96,160},{128,192},{160,224},{192,0},{224,... | collective-permute-start | bytes 12296 | tf_op jit(solution)/shard_map/ppermute | solution.py:409
  48.8 20.2 %copy-start.4 = (bf16[2560,512]{1,0:T(8,128)(2,1)S(1)}, bf16[2560,512]{1,0:T(8,128)(2,1)}, u32[]{:S(2)}) copy-start(bf16[2560,512]{1,0:T(8,128)(2,1)} %copy-done.3) | copy-start | bytes 7864324
  48.8 20.2 %copy-start.8 = (bf16[512,172]{0,1:T(8,128)(2,1)S(1)}, bf16[512,172]{0,1:T(8,128)(2,1)}, u32[]{:S(2)}) copy-start(bf16[512,172]{0,1:T(8,128)(2,1)} %param.27) | copy-start | bytes 528388
  48.8 20.2 %copy-start.9 = (bf16[512,172]{0,1:T(8,128)(2,1)S(1)}, bf16[512,172]{0,1:T(8,128)(2,1)}, u32[]{:S(2)}) copy-start(bf16[512,172]{0,1:T(8,128)(2,1)} %param.26) | copy-start | bytes 528388
  48.8 20.2 %copy-start.10 = (bf16[128,512]{1,0:T(8,128)(2,1)S(1)}, bf16[128,512]{1,0:T(8,128)(2,1)}, u32[]{:S(2)}) copy-start(bf16[128,512]{1,0:T(8,128)(2,1)} %first_self_any.1) | copy-start | bytes 393220
  48.8 20.2 %copy-start.11 = (bf16[128,512]{1,0:T(8,128)(2,1)S(1)}, bf16[128,512]{1,0:T(8,128)(2,1)}, u32[]{:S(2)}) copy-start(bf16[128,512]{1,0:T(8,128)(2,1)} %first_mean_any.1) | copy-start | bytes 393220
  48.8 20.2 %copy-start.13 = (s32[512]{0:T(512)S(1)}, s32[512]{0:T(512)}, u32[]{:S(2)}) copy-start(s32[512]{0:T(512)} %param.23) | copy-start | bytes 6148
  48.8 20.2 %copy-start.16 = (s32[1,256]{1,0:T(1,128)S(1)}, s32[1,256]{1,0:T(1,128)}, u32[]{:S(2)}) copy-start(s32[1,256]{1,0:T(1,128)} %sample_any.1) | copy-start | bytes 3076
  82.2 6.7 %collective-permute-start.8 = (bf16[32,64,128]{2,1,0:T(8,128)(2,1)S(1)}, bf16[32,64,128]{2,1,0:T(8,128)(2,1)S(1)}, u32[]{:S(2)}, u32[]{:S(2)}) collective-permute-start(bf16[32,64,128]{2,1,0:T(8,128)(2,1)S(1)} %get-tuple-element.34), channel_id=1, source_target_pairs={{0,32},{32,0},{64,96},{96,64},{128,160},{160,128},{192,224},{224,1... | collective-permute-start | bytes 1572872 | tf_op jit(solution)/shard_map/ppermute | solution.py:403
  116.3 3.1 %collective-permute-start.11 = (f32[64,128]{1,0:T(8,128)S(1)}, f32[64,128]{1,0:T(8,128)S(1)}, u32[]{:S(2)}, u32[]{:S(2)}) collective-permute-start(f32[64,128]{1,0:T(8,128)S(1)} %shard_map.198.refs_0_), channel_id=1, source_target_pairs={{0,192},{32,224},{64,0},{96,32},{128,64},{160,96},{192,128},{224,1... | collective-permute-start | bytes 98312 | tf_op jit(solution)/shard_map/ppermute | solution.py:409
  117.9 4.3 %collective-permute-start.10 = (f32[64,128]{1,0:T(8,128)S(1)}, f32[64,128]{1,0:T(8,128)S(1)}, u32[]{:S(2)}, u32[]{:S(2)}) collective-permute-start(f32[64,128]{1,0:T(8,128)S(1)} %shard_map.198.refs_0_), channel_id=1, source_target_pairs={{0,128},{32,160},{64,192},{96,224},{128,0},{160,32},{192,64},{224,... | collective-permute-start | bytes 98312 | tf_op jit(solution)/shard_map/ppermute | solution.py:409
  118.4 4.1 %collective-permute-start.9 = (f32[64,128]{1,0:T(8,128)S(1)}, f32[64,128]{1,0:T(8,128)S(1)}, u32[]{:S(2)}, u32[]{:S(2)}) collective-permute-start(f32[64,128]{1,0:T(8,128)S(1)} %shard_map.198.refs_0_), channel_id=1, source_target_pairs={{0,64},{32,96},{64,128},{96,160},{128,192},{160,224},{192,0},{224,... | collective-permute-start | bytes 98312 | tf_op jit(solution)/shard_map/ppermute | solution.py:409
  140.8 9.0 %collective-permute-start.12 = (bf16[32,48,128]{2,1,0:T(8,128)(2,1)S(1)}, bf16[32,48,128]{2,1,0:T(8,128)(2,1)S(1)}, u32[]{:S(2)}, u32[]{:S(2)}) collective-permute-start(bf16[32,48,128]{2,1,0:T(8,128)(2,1)S(1)} %all_to_all.22.mine_ref), channel_id=1, source_target_pairs={{0,32},{32,0},{64,96},{96,64},{128,160},{160,128},{192,224},{224,1... | collective-permute-start | bytes 1179656 | tf_op jit(solution)/shard_map/ppermute | solution.py:403
  (11 other events, 56.5 us)

commit v3 on v2

v3 whole, which is shorter than its diff:
```python
import functools

import jax
import jax.numpy as jnp
from jax import lax
from jax.experimental import pallas as pl
from jax.experimental.pallas import tpu as pltpu
from jax.sharding import PartitionSpec as P

F32 = jnp.float32
BF16 = jnp.bfloat16
I32 = jnp.int32
MIB = 1 << 20
TILE = 128
HALF = 64
PEERS = 32
CHIPS = 4
CORES = 2
HUBS_EACH = 4
CAPACITY = 32
GROUP_HUBS = PEERS * HUBS_EACH
FORWARD_ROWS = CAPACITY + 8
PEER_HUBS = CORES * CHIPS * HUBS_EACH
EDGE_ROWS = CAPACITY + CAPACITY // 2
HUB_ROWS = CHIPS * HUBS_EACH
HUB_PACKED = HUB_ROWS + HUB_ROWS // 2
STACK_ROWS = 640
SELF_AT = 256
LOSS_AT = 440
MEAN_AT = 448
CLASS_ROWS = 176
PIECE = STACK_ROWS // CORES * 4 // PEERS
SUM_ROWS = HUB_PACKED + PIECE
BACK_ROWS = EDGE_ROWS + SUM_ROWS

VM = pl.BlockSpec(memory_space=pltpu.VMEM)
SM = pl.BlockSpec(memory_space=pltpu.SMEM)
ANY = pl.BlockSpec(memory_space=pl.ANY)
HBM = pl.BlockSpec(memory_space=pltpu.HBM)


def nn(left, right):
    return jnp.dot(left, right, preferred_element_type=F32)


def nt(left, right):
    return lax.dot_general(left, right, (((1,), (1,)), ((), ())), preferred_element_type=F32)


def tn(left, right):
    return lax.dot_general(left, right, (((0,), (0,)), ((), ())), preferred_element_type=F32)


def split(values):
    high = values.astype(BF16)
    low = (values - high.astype(F32)).astype(BF16)
    return high, low


def one_hot(hit):
    return jnp.where(hit, 1.0, 0.0).astype(BF16)


def iota(dims, axis):
    return lax.broadcasted_iota(I32, dims, axis)


def kernel_call(body, outs, scratch=(), in_specs=None, limit=5, flops=0, moved=0):
    placed = {} if in_specs is None else {"in_specs": in_specs}
    return pl.pallas_call(
        body,
        out_shape=outs,
        **placed,
        scratch_shapes=list(scratch),
        compiler_params=pltpu.CompilerParams(vmem_limit_bytes=limit * MIB),
        cost_estimate=pl.CostEstimate(flops=flops, bytes_accessed=moved, transcendentals=0),
    )


def position():
    group = lax.axis_index("grp")
    return group // CORES, group % CORES


def fetch(pairs, sems):
    loads = [pltpu.make_async_copy(source, target, sems.at[i]) for i, (source, target) in enumerate(pairs)]
    for load in loads:
        load.start()
    return loads


def wanted_rows(send, counts, hub_ref):
    send = jnp.transpose(send)
    send = jnp.where(iota(send.shape, 0) < counts, send, -1)
    row = iota((FORWARD_ROWS - CAPACITY, PEERS), 0)
    hubs = jnp.full(row.shape, -1, I32)
    for k in range(HUBS_EACH):
        hubs = jnp.where(row == k, hub_ref[0, k], hubs)
    return jnp.concatenate([send, hubs], axis=0)


def pick_matrix(wanted, pick_ref):
    lane = iota((2 * FORWARD_ROWS, pick_ref.shape[1]), 1)
    for n in range(0, PEERS, 2):
        pair = jnp.concatenate([wanted[:, n : n + 1], wanted[:, n + 1 : n + 2]], axis=0)
        pick_ref[n * FORWARD_ROWS : (n + 2) * FORWARD_ROWS, :] = one_hot(pair == lane)


def send_features(
    features_any, send_any, count_any, hub_any, out_ref, pick_ref, features_ref, send_ref, count_ref, hub_ref, sems
):
    loads = fetch(
        (
            (send_any.at[0], send_ref),
            (count_any, count_ref),
            (hub_any, hub_ref),
            (features_any, features_ref),
        ),
        sems,
    )
    for load in loads[:-1]:
        load.wait()
    pick_matrix(wanted_rows(send_ref[...], count_ref[...], hub_ref), pick_ref)
    loads[-1].wait()
    out_ref[...] = nn(pick_ref[...], features_ref[...]).astype(BF16)


def build_dense(*refs):
    count = 13
    sources, refs = refs[:count], refs[count + 1 :]
    dense_ref, numbers_ref, weights_ref, wanted_ref, pick_ref, *places, sems = refs
    (
        adj_ref, dst_ref, src_ref, live_ref, send_ref, count_ref, hub_ref,
        sample_ref, label_ref, raw_self_ref, raw_mean_ref,
    ) = places
    targets = (
        adj_ref, dst_ref, src_ref, live_ref, send_ref, count_ref, hub_ref, sample_ref, label_ref,
        weights_ref.at[pl.ds(0, TILE)], weights_ref.at[pl.ds(TILE, TILE)], raw_self_ref, raw_mean_ref,
    )
    loads = fetch(zip(sources, targets), sems)
    dense_ref[...] = jnp.zeros_like(dense_ref)
    weights_ref[SELF_AT:, :] = jnp.zeros((weights_ref.shape[0] - SELF_AT, weights_ref.shape[1]), BF16)
    for load in loads:
        load.wait()

    def add(t, carry):
        rows = pl.ds(pl.multiple_of(dst_ref[0, t] * TILE, TILE), TILE)
        columns = pl.ds(pl.multiple_of(src_ref[0, t] * TILE, TILE), TILE)
        dense_ref[rows, columns] += adj_ref[t]
        return carry

    lax.fori_loop(0, live_ref[0], add, 0)
    classes = raw_self_ref.shape[0]
    weights_ref[SELF_AT : SELF_AT + classes, :] = raw_self_ref[...]
    weights_ref[2 * SELF_AT : 2 * SELF_AT + classes, :] = raw_mean_ref[...]
    wanted = wanted_rows(send_ref[...], count_ref[...], hub_ref)
    wanted_ref[...] = wanted
    pick_matrix(wanted, pick_ref)
    nodes = dense_ref.shape[0]
    node = iota((nodes, sample_ref.shape[1]), 0)
    times = jnp.sum(jnp.where(node == sample_ref[...], 1.0, 0.0), axis=1, keepdims=True)
    label = jnp.transpose(jnp.broadcast_to(label_ref[...], (8, nodes)))[:, 0:1]
    degree = jnp.maximum(nn(dense_ref[...], jnp.ones((dense_ref.shape[1], TILE), BF16)), 1.0)
    lane = iota(degree.shape, 1)
    numbers_ref[...] = jnp.where(lane == 0, degree, jnp.where(lane == 1, times, label.astype(F32)))


def group_hubs(arrived_ref, out_ref):
    low = iota((8, TILE), 0) < HUBS_EACH
    rows = []
    for n in range(0, PEERS, 2):
        first = arrived_ref[n, CAPACITY:FORWARD_ROWS, :].astype(F32)
        second = arrived_ref[n + 1, CAPACITY:FORWARD_ROWS, :].astype(F32)
        rows.append(jnp.where(low, first, pltpu.roll(second, HUBS_EACH, 0)))
    out_ref[...] = jnp.concatenate(rows, axis=0).astype(BF16)


def join_blocks(*refs):
    out_ref = refs[-1]
    for i in range(CHIPS):
        out_ref[i * GROUP_HUBS : (i + 1) * GROUP_HUBS, :] = refs[i][...]


def place_hubs(table_ref, start, hub_refs, lanes):
    chip, core = position()
    for there, hub_ref in zip((core, 1 - core), hub_refs):
        for i in range(CHIPS):
            other = (chip + CHIPS - i) % CHIPS
            at = start + (other * CORES + there) * GROUP_HUBS
            block = hub_ref[i * GROUP_HUBS : (i + 1) * GROUP_HUBS, :]
            table_ref[pl.ds(pl.multiple_of(at, GROUP_HUBS), GROUP_HUBS), lanes] = block


def first_means(
    features_ref, arrived_ref, dense_ref, numbers_ref, pick_ref, own_hub_ref, other_hub_ref,
    mean_ref, table_ref, out_ref,
):
    nodes = features_ref.shape[0]
    table_ref[0:nodes, :] = features_ref[...]
    place_hubs(table_ref, nodes, (own_hub_ref, other_hub_ref), slice(0, TILE))
    edge_at = nodes + CORES * CHIPS * GROUP_HUBS
    for n in range(PEERS):
        at = edge_at + n * CAPACITY
        table_ref[at : at + CAPACITY, :] = arrived_ref[n, 0:CAPACITY, :]
    mean = (nn(dense_ref[...], table_ref[...]) / numbers_ref[:, 0:1]).astype(BF16)
    mean_ref[...] = mean
    out_ref[...] = nn(pick_ref[...], mean).astype(BF16)


def join_rests(first, second):
    return first + pltpu.roll(second, HALF, 1)


def part_rests(packed):
    low = iota(packed.shape, 1) < HALF
    return jnp.where(low, packed, 0.0), jnp.where(low, pltpu.roll(packed, HALF, 1), 0.0)


def early_part(
    feature_table_ref, mean_ref, arrived_ref, dense_ref, weights_ref,
    hidden_ref, table_ref, source_ref, part_ref, logits_ref,
):
    nodes, width = hidden_ref.shape
    edges = PEERS * CAPACITY
    edge_at = feature_table_ref.shape[0] - edges
    table_ref[0:nodes, 0:TILE] = feature_table_ref[0:nodes, :]
    table_ref[nodes:, 0:TILE] = feature_table_ref[edge_at:, :]
    table_ref[0:nodes, TILE:] = mean_ref[...]
    for n in range(PEERS):
        at = nodes + n * CAPACITY
        table_ref[at : at + CAPACITY, TILE:] = arrived_ref[n, 0:CAPACITY, :]

    def forward(i, carry):
        rows = pl.ds(pl.multiple_of(i * nodes, nodes), nodes)
        source_ref[rows, :] = jnp.maximum(nn(table_ref[rows, :], weights_ref[0:SELF_AT, :]), 0.0).astype(BF16)
        return carry

    lax.fori_loop(0, table_ref.shape[0] // nodes, forward, 0)
    hidden = source_ref[0:nodes, :]
    hidden_ref[...] = hidden
    part_ref[...] = nn(dense_ref[:, 0:nodes], hidden) + nn(dense_ref[:, edge_at:], source_ref[nodes:, :])
    logits_ref[...] = nt(hidden, weights_ref[SELF_AT : 2 * SELF_AT, :])


def main_part(
    samples_all, classes,
    feature_table_ref, early_table_ref, early_source_ref, part_ref, logits_ref,
    dense_ref, numbers_ref, weights_ref, own_hub_ref, other_hub_ref,
    base_ref, edge_ref, mine_ref, theirs_ref,
    table_ref, source_ref, turned_ref, stack_ref, pay_ref,
):
    nodes, width = base_ref.shape
    padded = SELF_AT
    hubs = table_ref.shape[0]
    self_rows = slice(SELF_AT, 2 * SELF_AT)
    mean_rows = slice(2 * SELF_AT, 3 * SELF_AT)
    table_ref[:, 0:TILE] = feature_table_ref[nodes : nodes + hubs, :]
    place_hubs(table_ref, 0, (own_hub_ref, other_hub_ref), slice(TILE, 2 * TILE))

    def rows_of(i):
        return pl.ds(pl.multiple_of(i * nodes, nodes), nodes)

    def forward(i, carry):
        rows = rows_of(i)
        source_ref[rows, :] = jnp.maximum(nn(table_ref[rows, :], weights_ref[0:SELF_AT, :]), 0.0).astype(BF16)
        return carry

    lax.fori_loop(0, hubs // nodes, forward, 0)
    hidden = early_source_ref[0:nodes, :]
    degree = numbers_ref[:, 0:1]
    times = numbers_ref[:, 1:2]
    label = numbers_ref[:, 2:3].astype(I32)
    mean = part_ref[...] + nn(dense_ref[:, nodes : nodes + hubs], source_ref[...])
    mean = (mean / degree).astype(BF16)
    logits = logits_ref[...] + nt(mean, weights_ref[mean_rows, :])

    lane = iota((nodes, padded), 1)
    real = lane < classes
    onehot = jnp.where(lane == label, 1.0, 0.0)
    top = jnp.max(jnp.where(real, logits, -jnp.inf), axis=1, keepdims=True)
    shifted = logits - top
    powers = jnp.where(real, jnp.exp(shifted), 0.0)
    total = jnp.sum(powers, axis=1, keepdims=True)
    chosen = jnp.sum(onehot * shifted, axis=1, keepdims=True)
    loss = jnp.sum(times * (jnp.log(total) - chosen), axis=0, keepdims=True)
    upstream = times * ((powers / total - onehot) / samples_all)
    upstream = upstream.astype(BF16)
    turned_ref[...] = jnp.transpose((upstream.astype(F32) / degree).astype(BF16))

    stack_ref[SELF_AT:, :] = jnp.zeros((STACK_ROWS - SELF_AT, width), F32)
    upstream_turned = jnp.transpose(upstream)
    stack_ref[SELF_AT : SELF_AT + CLASS_ROWS, :] = nn(upstream_turned, hidden)[0:CLASS_ROWS]
    stack_ref[MEAN_AT : MEAN_AT + CLASS_ROWS, :] = nn(upstream_turned, mean)[0:CLASS_ROWS]
    loss_high = loss.astype(BF16).astype(F32)
    place = iota((8, width), 0)
    marks = jnp.where(place == 0, loss_high, 0.0)
    stack_ref[LOSS_AT : LOSS_AT + 8, :] = jnp.where(place == 1, loss - loss_high, marks)

    def back(at):
        found = nn(turned_ref[...], dense_ref[:, pl.ds(pl.multiple_of(at, nodes), nodes)])
        found = jnp.transpose(found.astype(BF16))
        return found, nn(found, weights_ref[mean_rows, :])

    def weights(table, source, grad):
        masked = jnp.where(source > 0, grad, 0.0).astype(BF16)
        return tn(table, masked)

    unused, spread = back(0)
    base = nn(upstream, weights_ref[self_rows, :]) + spread
    base_ref[...] = base
    stack_ref[0 : 2 * TILE, :] = weights(early_table_ref[0:nodes, :], hidden, base)
    each = nodes // CAPACITY

    low = iota((8, padded), 0) < HUBS_EACH
    for i in range(hubs // nodes):
        rows = slice(i * nodes, (i + 1) * nodes)
        found, spread = back(nodes + i * nodes)
        stack_ref[0 : 2 * TILE, :] += weights(table_ref[rows, :], source_ref[rows, :], spread)
        found = found.astype(F32)
        for core in range(CORES):
            for n in range(0, PEERS, 2):
                at = core * GROUP_HUBS + n * HUBS_EACH
                first = found[at : at + 8]
                second = found[at + CORES * GROUP_HUBS : at + CORES * GROUP_HUBS + 8]
                for member, rows_here in (
                    (n, jnp.where(low, first, pltpu.roll(second, HUBS_EACH, 0))),
                    (n + 1, jnp.where(low, pltpu.roll(first, HUBS_EACH, 0), second)),
                ):
                    pay_ref[core, member, 8 * i : 8 * i + 8, :] = rows_here[:, 0:TILE]
                    rest = rows_here[:, TILE:]
                    if i == 0:
                        pay_ref[core, member, HUB_ROWS:HUB_PACKED, :] = rest
                    else:
                        pay_ref[core, member, HUB_ROWS:HUB_PACKED, :] += pltpu.roll(rest, HALF, 1)

    def edge_chunk(i, carry):
        rows = rows_of(i + 1)
        found, spread = back(nodes + hubs + i * nodes)
        stack_ref[0 : 2 * TILE, :] += weights(early_table_ref[rows, :], early_source_ref[rows, :], spread)
        for p in range(each):
            at = p * CAPACITY
            rest = found[at : at + CAPACITY, TILE:].astype(F32)
            edge_ref[i * each + p, 0:CAPACITY, :] = found[at : at + CAPACITY, 0:TILE]
            edge_ref[i * each + p, CAPACITY:EDGE_ROWS, :] = join_rests(
                rest[0 : CAPACITY // 2], rest[CAPACITY // 2 :]
            ).astype(BF16)
        return carry

    lax.fori_loop(0, PEERS // each, edge_chunk, 0)
    for core in range(CORES):
        for n in range(PEERS):
            at = core * (STACK_ROWS // CORES) + PIECE * (n % 8)
            lanes = slice(TILE * (n // 8), TILE * (n // 8 + 1))
            pay_ref[core, n, HUB_PACKED:SUM_ROWS, :] = stack_ref[at : at + PIECE, lanes]
    unused, core = position()
    mine_ref[...] = pay_ref[core].astype(BF16)
    theirs_ref[...] = pay_ref[1 - core].astype(BF16)


def sum_cores(mine_ref, arrived_ref, edge_ref, out_ref):
    out_ref[:, 0:EDGE_ROWS, :] = edge_ref[...]
    total = mine_ref[...].astype(F32) + arrived_ref[...].astype(F32)
    out_ref[:, EDGE_ROWS:BACK_ROWS, :] = total.astype(BF16)


def sum_peers(arrived_ref, out_ref):
    total = arrived_ref[0, EDGE_ROWS:BACK_ROWS, :].astype(F32)
    for n in range(1, PEERS):
        total += arrived_ref[n, EDGE_ROWS:BACK_ROWS, :].astype(F32)
    out_ref[...] = total


def return_edges(base_ref, arrived_ref, wanted_ref, weights_ref, out_ref, found_ref, pick_ref):
    pick_matrix(wanted_ref[...], pick_ref)
    found_ref[...] = jnp.zeros_like(found_ref)
    for n in range(PEERS):
        at = n * FORWARD_ROWS
        first, second = part_rests(arrived_ref[n, CAPACITY:EDGE_ROWS, :].astype(F32))
        rest = jnp.concatenate([first, second], axis=0).astype(BF16)
        found_ref[at : at + CAPACITY, 0:TILE] = arrived_ref[n, 0:CAPACITY, :]
        found_ref[at : at + CAPACITY, TILE:] = rest
    rows = tn(pick_ref[...], found_ref[...])
    out_ref[...] = base_ref[...] + nn(rows.astype(BF16), weights_ref[2 * SELF_AT :, :])


def sum_chips(*refs):
    sum_refs, out_ref, total_ref = refs[:CHIPS], refs[-2], refs[-1]
    total = sum_refs[0][...]
    for sum_ref in sum_refs[1:]:
        total += sum_ref[...]
    total_ref[...] = total
    piece = total[HUB_PACKED:SUM_ROWS]
    unused, core = position()
    holder = (core == LOSS_AT * CORES // STACK_ROWS) & (lax.axis_index("dev") == LOSS_AT % (STACK_ROWS // CORES) // PIECE)
    rest = piece[0:1] - piece[0:1].astype(BF16).astype(F32)
    row = iota(piece.shape, 0)
    piece = jnp.where((row == 2) & holder, rest, piece).astype(BF16)
    for n in range(PEERS):
        out_ref[n] = piece


def return_hubs(base_ref, total_ref, wanted_ref, weights_ref, out_ref):
    nodes = out_ref.shape[0]
    chip, unused = position()
    mains = (total_ref[0:8, :], total_ref[8:16, :])
    rests = part_rests(total_ref[HUB_ROWS:HUB_PACKED, :])
    own = jnp.zeros((8, 2 * TILE), F32)
    for other in range(CHIPS):
        rows = jnp.concatenate([mains[other // 2], rests[other // 2]], axis=1)
        if other % 2:
            rows = pltpu.roll(rows, HUBS_EACH, 0)
        own += jnp.where(chip == other, rows, 0.0)
    high, low = split(nn(own.astype(BF16), weights_ref[2 * SELF_AT :, :]))
    owner = one_hot(wanted_ref[CAPACITY:FORWARD_ROWS, 0:1] == iota((8, nodes), 1))
    out_ref[...] = base_ref[...] + tn(owner, high) + tn(owner, low)


def weight_outputs(samples_all, mine_ref, theirs_ref, first_self_ref, first_mean_ref, self_ref, mean_ref, loss_ref, stack_ref):
    unused, core = position()
    half = STACK_ROWS // CORES
    for n in range(PEERS):
        mine = mine_ref[n].astype(F32)
        theirs = theirs_ref[n].astype(F32)
        lanes = slice(TILE * (n // 8), TILE * (n // 8 + 1))
        at = PIECE * (n % 8)
        stack_ref[at : at + PIECE, lanes] = jnp.where(core == 0, mine, theirs)
        stack_ref[half + at : half + at + PIECE, lanes] = jnp.where(core == 0, theirs, mine)
    classes = self_ref.shape[0]
    first_self_ref[...] = stack_ref[0:TILE, :]
    first_mean_ref[...] = stack_ref[TILE : 2 * TILE, :]
    self_ref[...] = stack_ref[SELF_AT : SELF_AT + classes, :]
    mean_ref[...] = stack_ref[MEAN_AT : MEAN_AT + classes, :]
    parts = stack_ref[LOSS_AT : LOSS_AT + 8, 0:1]
    loss_ref[...] = (parts[0:1] + parts[1:2] + parts[2:3]) / samples_all


def shape(dims, dtype):
    return jax.ShapeDtypeStruct(dims, dtype)


def swap(values):
    return lax.all_to_all(values, "dev", split_axis=0, concat_axis=0, tiled=True)


def to_core(values):
    return lax.ppermute(values, "grp", [(i, i ^ 1) for i in range(CHIPS * CORES)])


def to_chips(values):
    every = CHIPS * CORES
    return [
        lax.ppermute(values, "grp", [(i, (i + CORES * shift) % every) for i in range(every)])
        for shift in range(1, CHIPS)
    ]


def on_device(
    features,
    hub_list,
    send_list,
    send_count,
    tile_dst,
    tile_src,
    tile_count,
    tile_adj,
    sample_ids,
    labels,
    first_self,
    first_mean,
    second_self,
    second_mean,
):
    nodes, inputs = features.shape
    width, classes = second_self.shape
    hubs = CHIPS * CORES * PEERS * HUBS_EACH
    edges = PEERS * CAPACITY
    table = nodes + hubs + edges
    padded = 2 * TILE
    samples_all = float(sample_ids.shape[1] * CHIPS * CORES * PEERS)

    slots = PEERS * FORWARD_ROWS

    def gather_hubs(arrived, beside):
        own = kernel_call(group_hubs, shape((GROUP_HUBS, inputs), BF16))(arrived)
        blocks = kernel_call(
            join_blocks,
            shape((CHIPS * GROUP_HUBS, inputs), BF16),
            in_specs=[VM] * CHIPS + [ANY] * len(beside),
        )(own, *to_chips(own), *beside)
        return blocks, to_core(blocks)

    rows = kernel_call(
        send_features,
        shape((slots, inputs), BF16),
        [
            pltpu.VMEM((slots, nodes), BF16),
            pltpu.VMEM((nodes, inputs), BF16),
            pltpu.VMEM(send_list.shape[1:], I32),
            pltpu.VMEM(send_count.shape, I32),
            pltpu.SMEM(hub_list.shape, I32),
            pltpu.SemaphoreType.DMA((4,)),
        ],
        [HBM] * 4,
        limit=60,
    )(features, send_list, send_count, hub_list)
    feature_arrived = swap(rows.reshape(PEERS, FORWARD_ROWS, inputs))
    raw = (second_self.T, second_mean.T)
    operands = (
        tile_adj, tile_dst, tile_src, tile_count, send_list[0], send_count, hub_list,
        sample_ids, labels.reshape(1, nodes), first_self, first_mean, *raw,
    )
    dense, numbers, weights, wanted, picks = kernel_call(
        build_dense,
        (
            shape((nodes, table), BF16),
            shape((nodes, TILE), F32),
            shape((3 * padded, width), BF16),
            shape((FORWARD_ROWS, PEERS), I32),
            shape((slots, nodes), BF16),
        ),
        [
            pltpu.VMEM(tile_adj.shape, BF16),
            pltpu.SMEM(tile_dst.shape, I32),
            pltpu.SMEM(tile_src.shape, I32),
            pltpu.SMEM(tile_count.shape, I32),
            pltpu.VMEM(send_list.shape[1:], I32),
            pltpu.VMEM(send_count.shape, I32),
            pltpu.SMEM(hub_list.shape, I32),
            pltpu.VMEM(sample_ids.shape, I32),
            pltpu.VMEM((1, nodes), I32),
            pltpu.VMEM(raw[0].shape, BF16),
            pltpu.VMEM(raw[1].shape, BF16),
            pltpu.SemaphoreType.DMA((len(operands),)),
        ],
        [HBM] * len(operands) + [ANY],
        flops=2 * nodes * table * TILE,
        moved=8 * MIB,
    )(
        *(
            operand if operand is tile_count else pltpu.with_memory_space_constraint(operand, pltpu.HBM)
            for operand in operands
        ),
        feature_arrived,
    )
    feature_hubs = gather_hubs(feature_arrived, [numbers])
    mean_rows, feature_table, rows = kernel_call(
        first_means,
        (shape((nodes, inputs), BF16), shape((table, inputs), BF16), shape((slots, inputs), BF16)),
    )(features, feature_arrived, dense, numbers, picks, *feature_hubs)
    mean_arrived = swap(rows.reshape(PEERS, FORWARD_ROWS, inputs))

    hidden, early_table, early_source, part, own_logits = kernel_call(
        early_part,
        (
            shape((nodes, width), BF16),
            shape((nodes + edges, 2 * inputs), BF16),
            shape((nodes + edges, width), BF16),
            shape((nodes, width), F32),
            shape((nodes, padded), F32),
        ),
        limit=8,
        flops=6 * nodes * edges * width,
        moved=8 * MIB,
    )(feature_table, mean_rows, mean_arrived, dense, weights)
    mean_hubs = gather_hubs(mean_arrived, [own_logits])
    base, edge_rows, mine, theirs = kernel_call(
        functools.partial(main_part, samples_all, classes),
        (
            shape((nodes, width), F32),
            shape((PEERS, EDGE_ROWS, TILE), BF16),
            shape((PEERS, SUM_ROWS, TILE), BF16),
            shape((PEERS, SUM_ROWS, TILE), BF16),
        ),
        [
            pltpu.VMEM((hubs, 2 * inputs), BF16),
            pltpu.VMEM((hubs, width), BF16),
            pltpu.VMEM((padded, nodes), BF16),
            pltpu.VMEM((STACK_ROWS, width), F32),
            pltpu.VMEM((CORES, PEERS, SUM_ROWS, TILE), F32),
        ],
        limit=16,
    )(
        feature_table, early_table, early_source, part, own_logits, dense, numbers, weights, *mean_hubs,
    )
    rows = kernel_call(sum_cores, shape((PEERS, BACK_ROWS, TILE), BF16))(mine, to_core(theirs), edge_rows)
    arrived = swap(rows)
    sums = kernel_call(sum_peers, shape((SUM_ROWS, TILE), F32))(arrived)
    base = kernel_call(
        return_edges,
        shape((nodes, width), F32),
        [pltpu.VMEM((slots, padded), BF16), pltpu.VMEM((slots, nodes), BF16)],
        limit=6,
        flops=2 * nodes * (edges * padded + width * padded),
        moved=4 * MIB,
    )(base, arrived, wanted, weights)
    pieces, total = kernel_call(
        sum_chips,
        (shape((PEERS, PIECE, TILE), BF16), shape((SUM_ROWS, TILE), F32)),
        in_specs=[VM] * CHIPS + [ANY],
    )(sums, *to_chips(sums), base)
    pieces = swap(pieces)
    grad_hidden = kernel_call(
        return_hubs,
        shape((nodes, width), F32),
        flops=4 * nodes * padded * width,
        moved=4 * MIB,
    )(base, total, wanted, weights)
    first_self_sum, first_mean_sum, self_sum, mean_sum, loss = kernel_call(
        functools.partial(weight_outputs, samples_all),
        (
            shape(first_self.shape, F32),
            shape(first_mean.shape, F32),
            shape((classes, width), F32),
            shape((classes, width), F32),
            shape((1, 1), F32),
        ),
        [pltpu.VMEM((STACK_ROWS, width), F32)],
    )(pieces, to_core(pieces))
    return hidden, grad_hidden, loss[0, 0], first_self_sum, first_mean_sum, self_sum.T, mean_sum.T


def solution(mesh):
    both = ("grp", "dev")
    placed = (
        P(both, None),
        P(both, None),
        P(both, None, None),
        P(both, None),
        P(both, None),
        P(both, None),
        P(both),
        P(both, None, None),
        P(both, None),
        P(both),
        P(),
        P(),
        P(),
        P(),
    )
    return jax.shard_map(
        on_device,
        mesh=mesh,
        in_specs=placed,
        out_specs=(P(both, None), P(both, None), P(), P(), P(), P(), P()),
        check_vma=False,
    )
```

time: 151 us -> 137 us (0.907)
  blocking collectives: 63 us -> 81.6 us
  starting transfers between devices: 37.9 us -> 25.9 us
  local copies, waits for them, and re-layouts: 8.63 us -> 0.01 us
  Pallas kernels: 27.4 us -> 20.6 us
  waiting for transfers between devices: 12.3 us -> 7.26 us
    all_to_all x3 -> x4, blocking collectives: 63 us -> 81.6 us  [swap(): lax.all_to_all(values, 'dev', split_axis=0, concat_axis=0, tiled=True)]
    all_to_all x1 -> x0, starting transfers between devices: 11.2 us -> none  [swap(): lax.all_to_all(values, 'dev', split_axis=0, concat_axis=0, tiled=True)]
    unnamed x42 -> x2, local copies, waits for them, and re-layouts: 8.63 us -> 0.01 us
    pallas_call x10 -> x12, Pallas kernels: 26.1 us -> 19.2 us  [the longest x1 6.47 us: on_device(): kernel_call(functools.partial(main_part, samples_all, classes), (shape((n...]
    all_to_all x1 -> x0, waiting for transfers between devices: 3.4 us -> none  [swap(): lax.all_to_all(values, 'dev', split_axis=0, concat_axis=0, tiled=True)]
    ppermute x9, waiting for transfers between devices: 5.77 us -> 3.73 us  [to_chips(): lax.ppermute(values, 'grp', [(i, (i + CORES * shift) % every) for i in ra...]
  transfers between devices with their start and end apart: 14 -> 13, of which waited for: 10 -> 9; matrix products, arithmetic and copies ran while one was open for 0% -> 0% of each run, Pallas kernels for 7% -> 6%
where the time goes in v3:
time: 137 us
  blocking collectives  81.6 us (60%)
  starting transfers between devices  25.9 us (19%)
  Pallas kernels  20.6 us (15%)
  waiting for transfers between devices  7.26 us (5%)
  between operations  1.37 us (1%)
    all_to_all x4, blocking collectives, swap(): lax.all_to_all(values, 'dev', split_axis=0, concat_axis=0, tiled=True)  81.6 us
    ppermute x4, starting transfers between devices, to_core(): lax.ppermute(values, 'grp', [(i, i ^ 1) for i in range(CHIPS * CORES)])  17.9 us
    ppermute x9, starting transfers between devices, to_chips(): lax.ppermute(values, 'grp', [(i, (i + CORES * shift) % every) for i in ra...  8.02 us
    pallas_call x1, Pallas kernels, on_device(): kernel_call(functools.partial(main_part, samples_all, classes), (shape((n...  6.47 us
    ppermute x9, waiting for transfers between devices, to_chips(): lax.ppermute(values, 'grp', [(i, (i + CORES * shift) % every) for i in ra...  3.73 us
    ppermute x4, waiting for transfers between devices, to_core(): lax.ppermute(values, 'grp', [(i, i ^ 1) for i in range(CHIPS * CORES)])  3.52 us
    pallas_call x1, Pallas kernels, on_device(): kernel_call(build_dense, (shape((nodes, table), BF16), shape((nodes, TILE...  2.76 us
  transfers between devices with their start and end apart: 13, of which 9 were waited for; matrix products, arithmetic and copies ran while one was open for 0% of the time, Pallas kernels for 6%

profile of v3, /device:TPU:1, one launch (start us, length us, event | category | flops | bytes accessed | tf_op | source)
XLA Modules:
  0.0 136.7 jit_solution(2318675518352734103)
XLA Ops:
  0.6 2.5 %shard_map.189 = bf16[1280,128]{1,0:T(8,128)(2,1)} custom-call(bf16[512,128]{1,0:T(8,128)(2,1)} %features_ref.1, s32[1,32,32]{2,1,0:T(8,128)} %send_any.1, s32[1,32]{1,0:T(1,128)} %refs_5_.1, s32[1,4]{1,0:T(1,128)} %refs_6_.1), custom_call_target="tpu_custom_call" | custom-call | tf_op jit(solution)/shard_map/pallas_call | solution.py:492
  3.1 22.2 %all_to_all.20.refs_13_.arrived_ref = bf16[32,40,128]{2,1,0:T(8,128)(2,1)S(1)} all-to-all(bf16[32,40,128]{2,1,0:T(8,128)(2,1)} %bitcast.10), channel_id=1, replica_groups=mesh['grp'=8,'dev'=32] {'dev'}, dimensions={0} | all-to-all | bytes 655360 | tf_op jit(solution)/shard_map/all_to_all | solution.py:442
  25.3 2.6 %collective-permute-start.2 = (bf16[128,128]{1,0:T(8,128)(2,1)S(1)}, bf16[128,128]{1,0:T(8,128)(2,1)S(1)}, u32[]{:S(2)}, u32[]{:S(2)}) collective-permute-start(bf16[128,128]{1,0:T(8,128)(2,1)S(1)} %shard_map.191.refs_0_), channel_id=1, source_target_pairs={{0,192},{32,224},{64,0},{96,32},{128,64},{160,96},{192,128},{224,1... | collective-permute-start | bytes 98312 | tf_op jit(solution)/shard_map/ppermute | solution.py:452
  29.7 2.8 %shard_map.190 = (bf16[512,2560]{1,0:T(8,128)(2,1)S(1)}, f32[512,128]{1,0:T(8,128)S(1)}, bf16[768,512]{1,0:T(8,128)(2,1)S(1)}, s32[40,32]{1,0:T(8,128)S(1)}, bf16[1280,512]{1,0:T(8,128)(2,1)S(1)}) custom-call(bf16[32,128,128]{2,1,0:T(8,128)(2,1)} %refs_0_.1, s32[1,32]{1,0:T(1,128)} %refs_1_.1, s32[1,32]{1,0:T(1,128)} %refs_2_.1, s32[1]{0:T(128)S(6)} %copy.21.refs_3_, ...), custom_call_target="tpu_custom_call" | custom-call | flops 335544320 | bytes 8388608 | tf_op jit(solution)/shard_map/pallas_call | solution.py:512
  32.5 6.0 %collective-permute-start.3 = (bf16[512,128]{1,0:T(8,128)(2,1)S(1)}, bf16[512,128]{1,0:T(8,128)(2,1)S(1)}, u32[]{:S(2)}, u32[]{:S(2)}) collective-permute-start(bf16[512,128]{1,0:T(8,128)(2,1)S(1)} %shard_map.192.own_hub_ref), channel_id=1, source_target_pairs={{0,32},{32,0},{64,96},{96,64},{128,160},{160,128},{192,224},{224,1... | collective-permute-start | bytes 393224 | tf_op jit(solution)/shard_map/ppermute | solution.py:446
  38.5 1.0 collective-permute-done.3.other_hub_ref
  39.5 2.0 %shard_map.193 = (bf16[512,128]{1,0:T(8,128)(2,1)S(1)}, bf16[2560,128]{1,0:T(8,128)(2,1)S(1)}, bf16[1280,128]{1,0:T(8,128)(2,1)S(1)}) custom-call(bf16[512,128]{1,0:T(8,128)(2,1)S(1)} %copy-done, bf16[32,40,128]{2,1,0:T(8,128)(2,1)S(1)} %all_to_all.20.refs_13_.arrived_ref, bf16[512,2560]{1,0:T(8,128)(2,1)S(1)} %get-tuple-element.31.dense_ref, ...), custom_call_target="tpu_custom_call" | custom-call | tf_op jit(solution)/shard_map/pallas_call | solution.py:546
  41.5 14.7 %all_to_all.21.arrived_ref = bf16[32,40,128]{2,1,0:T(8,128)(2,1)S(1)} all-to-all(bf16[32,40,128]{2,1,0:T(8,128)(2,1)S(1)} %bitcast.9), channel_id=1, replica_groups=mesh['grp'=8,'dev'=32] {'dev'}, dimensions={0} | all-to-all | bytes 655360 | tf_op jit(solution)/shard_map/all_to_all | solution.py:442
  56.2 1.7 %collective-permute-start.6 = (bf16[128,128]{1,0:T(8,128)(2,1)S(1)}, bf16[128,128]{1,0:T(8,128)(2,1)S(1)}, u32[]{:S(2)}, u32[]{:S(2)}) collective-permute-start(bf16[128,128]{1,0:T(8,128)(2,1)S(1)} %shard_map.195.refs_0_), channel_id=1, source_target_pairs={{0,192},{32,224},{64,0},{96,32},{128,64},{160,96},{192,128},{224,1... | collective-permute-start | bytes 98312 | tf_op jit(solution)/shard_map/ppermute | solution.py:452
  57.9 1.1 collective-permute-start.5
  59.0 2.6 %shard_map.194 = (bf16[512,512]{1,0:T(8,128)(2,1)}, bf16[1536,256]{1,0:T(8,128)(2,1)S(1)}, bf16[1536,512]{1,0:T(8,128)(2,1)S(1)}, f32[512,512]{1,0:T(8,128)S(1)}, f32[512,256]{1,0:T(8,128)S(1)}) custom-call(bf16[2560,128]{1,0:T(8,128)(2,1)S(1)} %get-tuple-element.34.feature_table_ref, bf16[512,128]{1,0:T(8,128)(2,1)S(1)} %get-tuple-element.35.mean_ref, ...), custom_call_target="tpu_custom_call" | custom-call | flops 1610612736 | bytes 8388608 | tf_op jit(solution)/shard_map/pallas_call | solution.py:552
  62.1 0.8 collective-permute-done.4.refs_1_
  63.0 5.8 %collective-permute-start.7 = (bf16[512,128]{1,0:T(8,128)(2,1)S(1)}, bf16[512,128]{1,0:T(8,128)(2,1)S(1)}, u32[]{:S(2)}, u32[]{:S(2)}) collective-permute-start(bf16[512,128]{1,0:T(8,128)(2,1)S(1)} %shard_map.196.own_hub_ref), channel_id=1, source_target_pairs={{0,32},{32,0},{64,96},{96,64},{128,160},{160,128},{192,224},{224,1... | collective-permute-start | bytes 393224 | tf_op jit(solution)/shard_map/ppermute | solution.py:446
  68.7 1.0 collective-permute-done.7.other_hub_ref
  69.7 6.5 %shard_map.197 = (f32[512,512]{1,0:T(8,128)S(1)}, bf16[32,48,128]{2,1,0:T(8,128)(2,1)S(1)}, bf16[32,64,128]{2,1,0:T(8,128)(2,1)S(1)}, bf16[32,64,128]{2,1,0:T(8,128)(2,1)S(1)}) custom-call(bf16[2560,128]{1,0:T(8,128)(2,1)S(1)} %get-tuple-element.34.feature_table_ref, bf16[1536,256]{1,0:T(8,128)(2,1)S(1)} %get-tuple-element.39.early_table_ref, ...), custom_call_target="tpu_custom_call" | custom-call | tf_op jit(solution)/shard_map/pallas_call | solution.py:566
  76.7 1.5 %collective-permute-done.8.arrived_ref = bf16[32,64,128]{2,1,0:T(8,128)(2,1)S(1)} collective-permute-done((bf16[32,64,128]{2,1,0:T(8,128)(2,1)S(1)}, bf16[32,64,128]{2,1,0:T(8,128)(2,1)S(1)}, u32[]{:S(2)}, u32[]{:S(2)}) %collective-permute-start.8) | collective-permute-done | bytes 524320 | tf_op jit(solution)/shard_map/ppermute | solution.py:446
  78.4 26.7 %all_to_all.22.arrived_ref = bf16[32,112,128]{2,1,0:T(8,128)(2,1)S(1)} all-to-all(bf16[32,112,128]{2,1,0:T(8,128)(2,1)S(1)} %shard_map.198), channel_id=1, replica_groups=mesh['grp'=8,'dev'=32] {'dev'}, dimensions={0} | all-to-all | bytes 1835008 | tf_op jit(solution)/shard_map/all_to_all | solution.py:442
  105.7 0.7 collective-permute-start.10
  106.7 1.3 shard_map.199.refs_4_.base_ref
  108.3 1.7 %collective-permute-done.10.refs_2_ = f32[64,128]{1,0:T(8,128)S(1)} collective-permute-done((f32[64,128]{1,0:T(8,128)S(1)}, f32[64,128]{1,0:T(8,128)S(1)}, u32[]{:S(2)}, u32[]{:S(2)}) %collective-permute-start.10) | collective-permute-done | bytes 32800 | tf_op jit(solution)/shard_map/ppermute | solution.py:452
  110.4 18.0 %all_to_all.23.mine_ref = bf16[32,40,128]{2,1,0:T(8,128)(2,1)S(1)} all-to-all(bf16[32,40,128]{2,1,0:T(8,128)(2,1)S(1)} %get-tuple-element.49), channel_id=1, replica_groups=mesh['grp'=8,'dev'=32] {'dev'}, dimensions={0} | all-to-all | bytes 655360 | tf_op jit(solution)/shard_map/all_to_all | solution.py:442
  128.4 5.6 %collective-permute-start.12 = (bf16[32,40,128]{2,1,0:T(8,128)(2,1)S(1)}, bf16[32,40,128]{2,1,0:T(8,128)(2,1)S(1)}, u32[]{:S(2)}, u32[]{:S(2)}) collective-permute-start(bf16[32,40,128]{2,1,0:T(8,128)(2,1)S(1)} %all_to_all.23.mine_ref), channel_id=1, source_target_pairs={{0,32},{32,0},{64,96},{96,64},{128,160},{160,128},{192,224},{224,1... | collective-permute-start | bytes 983048 | tf_op jit(solution)/shard_map/ppermute | solution.py:446
  134.0 1.6 %shard_map.202 = f32[512,512]{1,0:T(8,128)} custom-call(f32[512,512]{1,0:T(8,128)S(1)} %shard_map.199.refs_4_.base_ref, f32[64,128]{1,0:T(8,128)S(1)} %get-tuple-element.48.total_ref, s32[40,32]{1,0:T(8,128)S(1)} %get-tuple-element.47.wanted_ref, bf16[768,512]{1,0:T(8,128)(2,1)S(1)} %get-tuple-element.37.weights_ref), custom_call_target="tpu_custom_call" | custom-call | flops 268435456 | bytes 4194304 | tf_op jit(solution)/shard_map/pallas_call | solution.py:602
  135.6 1.1 shard_map.203
  (23 shorter events, 4.1 us)
Async XLA Ops:
  25.3 14.2 %copy-start = (bf16[512,128]{1,0:T(8,128)(2,1)S(1)}, bf16[512,128]{1,0:T(8,128)(2,1)}, u32[]{:S(2)}) copy-start(bf16[512,128]{1,0:T(8,128)(2,1)} %features_ref.1) | copy-start | bytes 393220
  25.3 7.1 %collective-permute-start.2 = (bf16[128,128]{1,0:T(8,128)(2,1)S(1)}, bf16[128,128]{1,0:T(8,128)(2,1)S(1)}, u32[]{:S(2)}, u32[]{:S(2)}) collective-permute-start(bf16[128,128]{1,0:T(8,128)(2,1)S(1)} %shard_map.191.refs_0_), channel_id=1, source_target_pairs={{0,192},{32,224},{64,0},{96,32},{128,64},{160,96},{192,128},{224,1... | collective-permute-start | bytes 98312 | tf_op jit(solution)/shard_map/ppermute | solution.py:452
  27.9 4.6 %collective-permute-start.1 = (bf16[128,128]{1,0:T(8,128)(2,1)S(1)}, bf16[128,128]{1,0:T(8,128)(2,1)S(1)}, u32[]{:S(2)}, u32[]{:S(2)}) collective-permute-start(bf16[128,128]{1,0:T(8,128)(2,1)S(1)} %shard_map.191.refs_0_), channel_id=1, source_target_pairs={{0,128},{32,160},{64,192},{96,224},{128,0},{160,32},{192,64},{224,... | collective-permute-start | bytes 98312 | tf_op jit(solution)/shard_map/ppermute | solution.py:452
  28.4 4.1 %collective-permute-start = (bf16[128,128]{1,0:T(8,128)(2,1)S(1)}, bf16[128,128]{1,0:T(8,128)(2,1)S(1)}, u32[]{:S(2)}, u32[]{:S(2)}) collective-permute-start(bf16[128,128]{1,0:T(8,128)(2,1)S(1)} %shard_map.191.refs_0_), channel_id=1, source_target_pairs={{0,64},{32,96},{64,128},{96,160},{128,192},{160,224},{192,0},{224,... | collective-permute-start | bytes 98312 | tf_op jit(solution)/shard_map/ppermute | solution.py:452
  32.5 7.0 %collective-permute-start.3 = (bf16[512,128]{1,0:T(8,128)(2,1)S(1)}, bf16[512,128]{1,0:T(8,128)(2,1)S(1)}, u32[]{:S(2)}, u32[]{:S(2)}) collective-permute-start(bf16[512,128]{1,0:T(8,128)(2,1)S(1)} %shard_map.192.own_hub_ref), channel_id=1, source_target_pairs={{0,32},{32,0},{64,96},{96,64},{128,160},{160,128},{192,224},{224,1... | collective-permute-start | bytes 393224 | tf_op jit(solution)/shard_map/ppermute | solution.py:446
  56.2 5.4 %collective-permute-start.6 = (bf16[128,128]{1,0:T(8,128)(2,1)S(1)}, bf16[128,128]{1,0:T(8,128)(2,1)S(1)}, u32[]{:S(2)}, u32[]{:S(2)}) collective-permute-start(bf16[128,128]{1,0:T(8,128)(2,1)S(1)} %shard_map.195.refs_0_), channel_id=1, source_target_pairs={{0,192},{32,224},{64,0},{96,32},{128,64},{160,96},{192,128},{224,1... | collective-permute-start | bytes 98312 | tf_op jit(solution)/shard_map/ppermute | solution.py:452
  57.9 4.3 %collective-permute-start.5 = (bf16[128,128]{1,0:T(8,128)(2,1)S(1)}, bf16[128,128]{1,0:T(8,128)(2,1)S(1)}, u32[]{:S(2)}, u32[]{:S(2)}) collective-permute-start(bf16[128,128]{1,0:T(8,128)(2,1)S(1)} %shard_map.195.refs_0_), channel_id=1, source_target_pairs={{0,128},{32,160},{64,192},{96,224},{128,0},{160,32},{192,64},{224,... | collective-permute-start | bytes 98312 | tf_op jit(solution)/shard_map/ppermute | solution.py:452
  59.0 4.0 %collective-permute-start.4 = (bf16[128,128]{1,0:T(8,128)(2,1)S(1)}, bf16[128,128]{1,0:T(8,128)(2,1)S(1)}, u32[]{:S(2)}, u32[]{:S(2)}) collective-permute-start(bf16[128,128]{1,0:T(8,128)(2,1)S(1)} %shard_map.195.refs_0_), channel_id=1, source_target_pairs={{0,64},{32,96},{64,128},{96,160},{128,192},{160,224},{192,0},{224,... | collective-permute-start | bytes 98312 | tf_op jit(solution)/shard_map/ppermute | solution.py:452
  63.0 6.8 %collective-permute-start.7 = (bf16[512,128]{1,0:T(8,128)(2,1)S(1)}, bf16[512,128]{1,0:T(8,128)(2,1)S(1)}, u32[]{:S(2)}, u32[]{:S(2)}) collective-permute-start(bf16[512,128]{1,0:T(8,128)(2,1)S(1)} %shard_map.196.own_hub_ref), channel_id=1, source_target_pairs={{0,32},{32,0},{64,96},{96,64},{128,160},{160,128},{192,224},{224,1... | collective-permute-start | bytes 393224 | tf_op jit(solution)/shard_map/ppermute | solution.py:446
  76.2 2.0 %collective-permute-start.8 = (bf16[32,64,128]{2,1,0:T(8,128)(2,1)S(1)}, bf16[32,64,128]{2,1,0:T(8,128)(2,1)S(1)}, u32[]{:S(2)}, u32[]{:S(2)}) collective-permute-start(bf16[32,64,128]{2,1,0:T(8,128)(2,1)S(1)} %get-tuple-element.45), channel_id=1, source_target_pairs={{0,32},{32,0},{64,96},{96,64},{128,160},{160,128},{192,224},{224,1... | collective-permute-start | bytes 1572872 | tf_op jit(solution)/shard_map/ppermute | solution.py:446
  105.2 3.1 %collective-permute-start.11 = (f32[64,128]{1,0:T(8,128)S(1)}, f32[64,128]{1,0:T(8,128)S(1)}, u32[]{:S(2)}, u32[]{:S(2)}) collective-permute-start(f32[64,128]{1,0:T(8,128)S(1)} %shard_map.200.refs_0_), channel_id=1, source_target_pairs={{0,192},{32,224},{64,0},{96,32},{128,64},{160,96},{192,128},{224,1... | collective-permute-start | bytes 98312 | tf_op jit(solution)/shard_map/ppermute | solution.py:452
  105.7 4.3 %collective-permute-start.10 = (f32[64,128]{1,0:T(8,128)S(1)}, f32[64,128]{1,0:T(8,128)S(1)}, u32[]{:S(2)}, u32[]{:S(2)}) collective-permute-start(f32[64,128]{1,0:T(8,128)S(1)} %shard_map.200.refs_0_), channel_id=1, source_target_pairs={{0,128},{32,160},{64,192},{96,224},{128,0},{160,32},{192,64},{224,... | collective-permute-start | bytes 98312 | tf_op jit(solution)/shard_map/ppermute | solution.py:452
  106.3 4.0 %collective-permute-start.9 = (f32[64,128]{1,0:T(8,128)S(1)}, f32[64,128]{1,0:T(8,128)S(1)}, u32[]{:S(2)}, u32[]{:S(2)}) collective-permute-start(f32[64,128]{1,0:T(8,128)S(1)} %shard_map.200.refs_0_), channel_id=1, source_target_pairs={{0,64},{32,96},{64,128},{96,160},{128,192},{160,224},{192,0},{224,... | collective-permute-start | bytes 98312 | tf_op jit(solution)/shard_map/ppermute | solution.py:452
  128.4 7.2 %collective-permute-start.12 = (bf16[32,40,128]{2,1,0:T(8,128)(2,1)S(1)}, bf16[32,40,128]{2,1,0:T(8,128)(2,1)S(1)}, u32[]{:S(2)}, u32[]{:S(2)}) collective-permute-start(bf16[32,40,128]{2,1,0:T(8,128)(2,1)S(1)} %all_to_all.23.mine_ref), channel_id=1, source_target_pairs={{0,32},{32,0},{64,96},{96,64},{128,160},{160,128},{192,224},{224,1... | collective-permute-start | bytes 983048 | tf_op jit(solution)/shard_map/ppermute | solution.py:446

commit v4 on v3

--- a/solution.py
+++ b/solution.py
@@ -191,18 +191,28 @@
             table_ref[pl.ds(pl.multiple_of(at, GROUP_HUBS), GROUP_HUBS), lanes] = block
 
 
-def first_means(
-    features_ref, arrived_ref, dense_ref, numbers_ref, pick_ref, own_hub_ref, other_hub_ref,
-    mean_ref, table_ref, out_ref,
-):
+def early_means(features_ref, arrived_ref, dense_ref, own_hub_ref, part_ref, table_ref):
     nodes = features_ref.shape[0]
+    edge_at = nodes + CORES * CHIPS * GROUP_HUBS
     table_ref[0:nodes, :] = features_ref[...]
-    place_hubs(table_ref, nodes, (own_hub_ref, other_hub_ref), slice(0, TILE))
-    edge_at = nodes + CORES * CHIPS * GROUP_HUBS
+    table_ref[nodes:edge_at, :] = jnp.zeros((edge_at - nodes, TILE), BF16)
+    place_hubs(table_ref, nodes, (own_hub_ref,), slice(0, TILE))
     for n in range(PEERS):
         at = edge_at + n * CAPACITY
         table_ref[at : at + CAPACITY, :] = arrived_ref[n, 0:CAPACITY, :]
-    mean = (nn(dense_ref[...], table_ref[...]) / numbers_ref[:, 0:1]).astype(BF16)
+    part_ref[...] = nn(dense_ref[...], table_ref[...])
+
+
+def first_means(part_ref, dense_ref, numbers_ref, pick_ref, other_hub_ref, mean_ref, out_ref):
+    nodes = part_ref.shape[0]
+    chip, core = position()
+    total = part_ref[...]
+    for i in range(CHIPS):
+        other = (chip + CHIPS - i) % CHIPS
+        at = nodes + (other * CORES + 1 - core) * GROUP_HUBS
+        columns = dense_ref[:, pl.ds(pl.multiple_of(at, GROUP_HUBS), GROUP_HUBS)]
+        total += nn(columns, other_hub_ref[i * GROUP_HUBS : (i + 1) * GROUP_HUBS, :])
+    mean = (total / numbers_ref[:, 0:1]).astype(BF16)
     mean_ref[...] = mean
     out_ref[...] = nn(pick_ref[...], mean).astype(BF16)
 
@@ -217,61 +227,75 @@
 
 
 def early_part(
-    feature_table_ref, mean_ref, arrived_ref, dense_ref, weights_ref,
-    hidden_ref, table_ref, source_ref, part_ref, logits_ref,
+    features_ref, feature_arrived_ref, mean_ref, arrived_ref, dense_ref, weights_ref,
+    hidden_ref, turned_ref, source_ref, part_ref, logits_ref, table_ref,
 ):
     nodes, width = hidden_ref.shape
     edges = PEERS * CAPACITY
-    edge_at = feature_table_ref.shape[0] - edges
-    table_ref[0:nodes, 0:TILE] = feature_table_ref[0:nodes, :]
-    table_ref[nodes:, 0:TILE] = feature_table_ref[edge_at:, :]
+    edge_at = dense_ref.shape[1] - edges
+    table_ref[0:nodes, 0:TILE] = features_ref[...]
     table_ref[0:nodes, TILE:] = mean_ref[...]
     for n in range(PEERS):
         at = nodes + n * CAPACITY
+        table_ref[at : at + CAPACITY, 0:TILE] = feature_arrived_ref[n, 0:CAPACITY, :]
         table_ref[at : at + CAPACITY, TILE:] = arrived_ref[n, 0:CAPACITY, :]
-
-    def forward(i, carry):
-        rows = pl.ds(pl.multiple_of(i * nodes, nodes), nodes)
-        source_ref[rows, :] = jnp.maximum(nn(table_ref[rows, :], weights_ref[0:SELF_AT, :]), 0.0).astype(BF16)
-        return carry
-
-    lax.fori_loop(0, table_ref.shape[0] // nodes, forward, 0)
+    for at in range(0, nodes + edges, nodes):
+        rows = slice(at, at + nodes)
+        linear = nn(table_ref[rows, :], weights_ref[0:SELF_AT, :])
+        source_ref[rows, :] = jnp.maximum(linear, 0.0).astype(BF16)
+        turned_ref[:, rows] = jnp.transpose(table_ref[rows, :])
     hidden = source_ref[0:nodes, :]
     hidden_ref[...] = hidden
     part_ref[...] = nn(dense_ref[:, 0:nodes], hidden) + nn(dense_ref[:, edge_at:], source_ref[nodes:, :])
     logits_ref[...] = nt(hidden, weights_ref[SELF_AT : 2 * SELF_AT, :])
 
 
+def hub_part(
+    dense_ref, weights_ref, features, means, others, turned_ref, source_ref, columns_ref
+):
+    nodes = dense_ref.shape[0]
+    chip, core = position()
+    there = 1 - core if others else core
+    table = jnp.concatenate([features, means], axis=1)
+    turned_ref[...] = jnp.transpose(table)
+    source_ref[...] = jnp.maximum(nn(table, weights_ref[0:SELF_AT, :]), 0.0).astype(BF16)
+    for i in range(CHIPS):
+        other = (chip + CHIPS - i) % CHIPS
+        at = pl.multiple_of(nodes + (other * CORES + there) * GROUP_HUBS, GROUP_HUBS)
+        columns_ref[:, i * GROUP_HUBS : (i + 1) * GROUP_HUBS] = dense_ref[:, pl.ds(at, GROUP_HUBS)]
+    return nn(columns_ref[...], source_ref[...])
+
+
+def own_hub_part(
+    dense_ref, weights_ref, part_ref, feature_ref, mean_ref, turned_ref, source_ref, columns_ref, out_ref
+):
+    total = hub_part(
+        dense_ref, weights_ref, feature_ref[...], mean_ref[...], False, turned_ref, source_ref, columns_ref
+    )
+    out_ref[...] = part_ref[...] + total
+
+
 def main_part(
     samples_all, classes,
-    feature_table_ref, early_table_ref, early_source_ref, part_ref, logits_ref,
-    dense_ref, numbers_ref, weights_ref, own_hub_ref, other_hub_ref,
+    early_turned_ref, early_source_ref, logits_ref, own_turned_ref, own_source_ref, own_columns_ref, part_ref,
+    dense_ref, numbers_ref, weights_ref, feature_ref, mean_ref,
     base_ref, edge_ref, mine_ref, theirs_ref,
-    table_ref, source_ref, turned_ref, stack_ref, pay_ref,
+    other_turned_ref, other_source_ref, other_columns_ref, scaled_ref, masked_ref, stack_ref, rest_ref,
 ):
     nodes, width = base_ref.shape
     padded = SELF_AT
-    hubs = table_ref.shape[0]
     self_rows = slice(SELF_AT, 2 * SELF_AT)
     mean_rows = slice(2 * SELF_AT, 3 * SELF_AT)
-    table_ref[:, 0:TILE] = feature_table_ref[nodes : nodes + hubs, :]
-    place_hubs(table_ref, 0, (own_hub_ref, other_hub_ref), slice(TILE, 2 * TILE))
-
-    def rows_of(i):
-        return pl.ds(pl.multiple_of(i * nodes, nodes), nodes)
-
-    def forward(i, carry):
-        rows = rows_of(i)
-        source_ref[rows, :] = jnp.maximum(nn(table_ref[rows, :], weights_ref[0:SELF_AT, :]), 0.0).astype(BF16)
-        return carry
-
-    lax.fori_loop(0, hubs // nodes, forward, 0)
+    edge_at = dense_ref.shape[1] - PEERS * CAPACITY
+    total = hub_part(
+        dense_ref, weights_ref, feature_ref[...], mean_ref[...], True,
+        other_turned_ref, other_source_ref, other_columns_ref,
+    )
     hidden = early_source_ref[0:nodes, :]
     degree = numbers_ref[:, 0:1]
     times = numbers_ref[:, 1:2]
     label = numbers_ref[:, 2:3].astype(I32)
-    mean = part_ref[...] + nn(dense_ref[:, nodes : nodes + hubs], source_ref[...])
-    mean = (mean / degree).astype(BF16)
+    mean = ((part_ref[...] + total) / degree).astype(BF16)
     logits = logits_ref[...] + nt(mean, weights_ref[mean_rows, :])
 
     lane = iota((nodes, padded), 1)
@@ -285,7 +309,53 @@
     loss = jnp.sum(times * (jnp.log(total) - chosen), axis=0, keepdims=True)
     upstream = times * ((powers / total - onehot) / samples_all)
     upstream = upstream.astype(BF16)
-    turned_ref[...] = jnp.transpose((upstream.astype(F32) / degree).astype(BF16))
+    scaled_ref[...] = jnp.transpose((upstream.astype(F32) / degree).astype(BF16))
+
+    def back(columns):
+        found = nn(scaled_ref[...], columns)
+        found = jnp.transpose(found.astype(BF16))
+        return found, nn(found, weights_ref[mean_rows, :])
+
+    def mask(at, source, grad):
+        masked_ref[at : at + nodes, :] = jnp.where(source > 0, grad, 0.0).astype(BF16)
+
+    low = iota((8, padded), 0) < HUBS_EACH
+    hub_at = nodes + PEERS * CAPACITY
+    for i, (columns_ref, source_ref, out_ref) in enumerate(
+        ((own_columns_ref, own_source_ref, mine_ref), (other_columns_ref, other_source_ref, theirs_ref))
+    ):
+        found, spread = back(columns_ref[...])
+        mask(hub_at + i * nodes, source_ref[...], spread)
+        found = found.astype(F32)
+        for n in range(0, PEERS, 2):
+            first, second = [], []
+            for pair in range(CHIPS // 2):
+                at = 2 * pair * GROUP_HUBS + n * HUBS_EACH
+                even = found[at : at + 8]
+                odd = found[at + GROUP_HUBS : at + GROUP_HUBS + 8]
+                first.append(jnp.where(low, even, pltpu.roll(odd, HUBS_EACH, 0)))
+                second.append(jnp.where(low, pltpu.roll(even, HUBS_EACH, 0), odd))
+            for member, blocks in ((n, first), (n + 1, second)):
+                rows = jnp.concatenate([block[:, 0:TILE] for block in blocks], axis=0)
+                out_ref[member, 0:HUB_ROWS, :] = rows.astype(BF16)
+                rest_ref[i, member] = join_rests(blocks[0][:, TILE:], blocks[1][:, TILE:])
+
+    unused, spread = back(dense_ref[:, 0:nodes])
+    base = nn(upstream, weights_ref[self_rows, :]) + spread
+    base_ref[...] = base
+    mask(0, hidden, base)
+    each = nodes // CAPACITY
+    for i in range(PEERS // each):
+        found, spread = back(dense_ref[:, edge_at + i * nodes : edge_at + (i + 1) * nodes])
+        at = (i + 1) * nodes
+        mask(at, early_source_ref[at : at + nodes, :], spread)
+        for p in range(each):
+            at = p * CAPACITY
+            rest = found[at : at + CAPACITY, TILE:].astype(F32)
+            edge_ref[i * each + p, 0:CAPACITY, :] = found[at : at + CAPACITY, 0:TILE]
+            edge_ref[i * each + p, CAPACITY:EDGE_ROWS, :] = join_rests(
+                rest[0 : CAPACITY // 2], rest[CAPACITY // 2 :]
+            ).astype(BF16)
 
     stack_ref[SELF_AT:, :] = jnp.zeros((STACK_ROWS - SELF_AT, width), F32)
     upstream_turned = jnp.transpose(upstream)
@@ -295,66 +365,19 @@
     place = iota((8, width), 0)
     marks = jnp.where(place == 0, loss_high, 0.0)
     stack_ref[LOSS_AT : LOSS_AT + 8, :] = jnp.where(place == 1, loss - loss_high, marks)
-
-    def back(at):
-        found = nn(turned_ref[...], dense_ref[:, pl.ds(pl.multiple_of(at, nodes), nodes)])
-        found = jnp.transpose(found.astype(BF16))
-        return found, nn(found, weights_ref[mean_rows, :])
-
-    def weights(table, source, grad):
-        masked = jnp.where(source > 0, grad, 0.0).astype(BF16)
-        return tn(table, masked)
-
-    unused, spread = back(0)
-    base = nn(upstream, weights_ref[self_rows, :]) + spread
-    base_ref[...] = base
-    stack_ref[0 : 2 * TILE, :] = weights(early_table_ref[0:nodes, :], hidden, base)
-    each = nodes // CAPACITY
-
-    low = iota((8, padded), 0) < HUBS_EACH
-    for i in range(hubs // nodes):
-        rows = slice(i * nodes, (i + 1) * nodes)
-        found, spread = back(nodes + i * nodes)
-        stack_ref[0 : 2 * TILE, :] += weights(table_ref[rows, :], source_ref[rows, :], spread)
-        found = found.astype(F32)
-        for core in range(CORES):
-            for n in range(0, PEERS, 2):
-                at = core * GROUP_HUBS + n * HUBS_EACH
-                first = found[at : at + 8]
-                second = found[at + CORES * GROUP_HUBS : at + CORES * GROUP_HUBS + 8]
-                for member, rows_here in (
-                    (n, jnp.where(low, first, pltpu.roll(second, HUBS_EACH, 0))),
-                    (n + 1, jnp.where(low, pltpu.roll(first, HUBS_EACH, 0), second)),
-                ):
-                    pay_ref[core, member, 8 * i : 8 * i + 8, :] = rows_here[:, 0:TILE]
-                    rest = rows_here[:, TILE:]
-                    if i == 0:
-                        pay_ref[core, member, HUB_ROWS:HUB_PACKED, :] = rest
-                    else:
-                        pay_ref[core, member, HUB_ROWS:HUB_PACKED, :] += pltpu.roll(rest, HALF, 1)
-
-    def edge_chunk(i, carry):
-        rows = rows_of(i + 1)
-        found, spread = back(nodes + hubs + i * nodes)
-        stack_ref[0 : 2 * TILE, :] += weights(early_table_ref[rows, :], early_source_ref[rows, :], spread)
-        for p in range(each):
-            at = p * CAPACITY
-            rest = found[at : at + CAPACITY, TILE:].astype(F32)
-            edge_ref[i * each + p, 0:CAPACITY, :] = found[at : at + CAPACITY, 0:TILE]
-            edge_ref[i * each + p, CAPACITY:EDGE_ROWS, :] = join_rests(
-                rest[0 : CAPACITY // 2], rest[CAPACITY // 2 :]
-            ).astype(BF16)
-        return carry
-
-    lax.fori_loop(0, PEERS // each, edge_chunk, 0)
-    for core in range(CORES):
+    stack_ref[0:SELF_AT, :] = (
+        nn(early_turned_ref[...], masked_ref[0:hub_at, :])
+        + nn(own_turned_ref[...], masked_ref[hub_at : hub_at + nodes, :])
+        + nn(other_turned_ref[...], masked_ref[hub_at + nodes :, :])
+    )
+    unused, core = position()
+    for i, (there, out_ref) in enumerate(((core, mine_ref), (1 - core, theirs_ref))):
         for n in range(PEERS):
-            at = core * (STACK_ROWS // CORES) + PIECE * (n % 8)
+            at = there * (STACK_ROWS // CORES) + PIECE * (n % 8)
             lanes = slice(TILE * (n // 8), TILE * (n // 8 + 1))
-            pay_ref[core, n, HUB_PACKED:SUM_ROWS, :] = stack_ref[at : at + PIECE, lanes]
-    unused, core = position()
-    mine_ref[...] = pay_ref[core].astype(BF16)
-    theirs_ref[...] = pay_ref[1 - core].astype(BF16)
+            piece = stack_ref[pl.ds(pl.multiple_of(at, 8), PIECE), lanes]
+            rows = jnp.concatenate([rest_ref[i, n], piece], axis=0)
+            out_ref[n, HUB_ROWS:SUM_ROWS, :] = rows.astype(BF16)
 
 
 def sum_cores(mine_ref, arrived_ref, edge_ref, out_ref):
@@ -384,12 +407,18 @@
 
 
 def sum_chips(*refs):
-    sum_refs, out_ref, total_ref = refs[:CHIPS], refs[-2], refs[-1]
-    total = sum_refs[0][...]
+    sum_refs, out_ref, hub_ref = refs[:CHIPS], refs[-2], refs[-1]
+    piece = sum_refs[0][HUB_PACKED:SUM_ROWS, :]
     for sum_ref in sum_refs[1:]:
-        total += sum_ref[...]
-    total_ref[...] = total
-    piece = total[HUB_PACKED:SUM_ROWS]
+        piece += sum_ref[HUB_PACKED:SUM_ROWS, :]
+    hubs = jnp.zeros((8, 2 * TILE), F32)
+    for shift, sum_ref in enumerate(sum_refs):
+        i = (CHIPS - shift) % CHIPS
+        main = sum_ref[8 * (i // 2) : 8 * (i // 2) + 8, :]
+        rest = part_rests(sum_ref[HUB_ROWS:HUB_PACKED, :])[i // 2]
+        rows = jnp.concatenate([main, rest], axis=1)
+        hubs += pltpu.roll(rows, HUBS_EACH, 0) if i % 2 else rows
+    hub_ref[...] = hubs
     unused, core = position()
     holder = (core == LOSS_AT * CORES // STACK_ROWS) & (lax.axis_index("dev") == LOSS_AT % (STACK_ROWS // CORES) // PIECE)
     rest = piece[0:1] - piece[0:1].astype(BF16).astype(F32)
@@ -399,18 +428,9 @@
         out_ref[n] = piece
 
 
-def return_hubs(base_ref, total_ref, wanted_ref, weights_ref, out_ref):
+def return_hubs(base_ref, hub_ref, wanted_ref, weights_ref, out_ref):
     nodes = out_ref.shape[0]
-    chip, unused = position()
-    mains = (total_ref[0:8, :], total_ref[8:16, :])
-    rests = part_rests(total_ref[HUB_ROWS:HUB_PACKED, :])
-    own = jnp.zeros((8, 2 * TILE), F32)
-    for other in range(CHIPS):
-        rows = jnp.concatenate([mains[other // 2], rests[other // 2]], axis=1)
-        if other % 2:
-            rows = pltpu.roll(rows, HUBS_EACH, 0)
-        own += jnp.where(chip == other, rows, 0.0)
-    high, low = split(nn(own.astype(BF16), weights_ref[2 * SELF_AT :, :]))
+    high, low = split(nn(hub_ref[...].astype(BF16), weights_ref[2 * SELF_AT :, :]))
     owner = one_hot(wanted_ref[CAPACITY:FORWARD_ROWS, 0:1] == iota((8, nodes), 1))
     out_ref[...] = base_ref[...] + tn(owner, high) + tn(owner, low)
 
@@ -501,8 +521,7 @@
             pltpu.SemaphoreType.DMA((4,)),
         ],
         [HBM] * 4,
-        limit=60,
-    )(features, send_list, send_count, hub_list)
+    )(*(pltpu.with_memory_space_constraint(operand, pltpu.HBM) for operand in (features, send_list, send_count, hub_list)))
     feature_arrived = swap(rows.reshape(PEERS, FORWARD_ROWS, inputs))
     raw = (second_self.T, second_mean.T)
     operands = (
@@ -543,26 +562,46 @@
         feature_arrived,
     )
     feature_hubs = gather_hubs(feature_arrived, [numbers])
-    mean_rows, feature_table, rows = kernel_call(
-        first_means,
-        (shape((nodes, inputs), BF16), shape((table, inputs), BF16), shape((slots, inputs), BF16)),
-    )(features, feature_arrived, dense, numbers, picks, *feature_hubs)
+    part = kernel_call(
+        early_means,
+        shape((nodes, inputs), F32),
+        [pltpu.VMEM((table, inputs), BF16)],
+        flops=2 * nodes * table * inputs,
+        moved=4 * MIB,
+    )(features, feature_arrived, dense, feature_hubs[0])
+    mean_rows, rows = kernel_call(
+        first_means, (shape((nodes, inputs), BF16), shape((slots, inputs), BF16))
+    )(part, dense, numbers, picks, feature_hubs[1])
     mean_arrived = swap(rows.reshape(PEERS, FORWARD_ROWS, inputs))
 
-    hidden, early_table, early_source, part, own_logits = kernel_call(
+    hidden, early_turned, early_source, part, own_logits = kernel_call(
         early_part,
         (
             shape((nodes, width), BF16),
-            shape((nodes + edges, 2 * inputs), BF16),
+            shape((2 * inputs, nodes + edges), BF16),
             shape((nodes + edges, width), BF16),
             shape((nodes, width), F32),
             shape((nodes, padded), F32),
         ),
+        [pltpu.VMEM((nodes + edges, 2 * inputs), BF16)],
         limit=8,
         flops=6 * nodes * edges * width,
         moved=8 * MIB,
-    )(feature_table, mean_rows, mean_arrived, dense, weights)
+    )(features, feature_arrived, mean_rows, mean_arrived, dense, weights)
     mean_hubs = gather_hubs(mean_arrived, [own_logits])
+    half = CHIPS * GROUP_HUBS
+    own_turned, own_source, own_columns, part = kernel_call(
+        own_hub_part,
+        (
+            shape((2 * inputs, half), BF16),
+            shape((half, width), BF16),
+            shape((nodes, half), BF16),
+            shape((nodes, width), F32),
+        ),
+        limit=6,
+        flops=4 * nodes * half * width,
+        moved=4 * MIB,
+    )(dense, weights, part, feature_hubs[0], mean_hubs[0])
     base, edge_rows, mine, theirs = kernel_call(
         functools.partial(main_part, samples_all, classes),
         (
@@ -572,15 +611,18 @@
             shape((PEERS, SUM_ROWS, TILE), BF16),
         ),
         [
-            pltpu.VMEM((hubs, 2 * inputs), BF16),
-            pltpu.VMEM((hubs, width), BF16),
+            pltpu.VMEM((2 * inputs, half), BF16),
+            pltpu.VMEM((half, width), BF16),
+            pltpu.VMEM((nodes, half), BF16),
             pltpu.VMEM((padded, nodes), BF16),
+            pltpu.VMEM((table, width), BF16),
             pltpu.VMEM((STACK_ROWS, width), F32),
-            pltpu.VMEM((CORES, PEERS, SUM_ROWS, TILE), F32),
+            pltpu.VMEM((CORES, PEERS, HUB_PACKED - HUB_ROWS, TILE), F32),
         ],
-        limit=16,
+        limit=20,
     )(
-        feature_table, early_table, early_source, part, own_logits, dense, numbers, weights, *mean_hubs,
+        early_turned, early_source, own_logits, own_turned, own_source, own_columns, part,
+        dense, numbers, weights, feature_hubs[1], mean_hubs[1],
     )
     rows = kernel_call(sum_cores, shape((PEERS, BACK_ROWS, TILE), BF16))(mine, to_core(theirs), edge_rows)
     arrived = swap(rows)
@@ -593,9 +635,9 @@
         flops=2 * nodes * (edges * padded + width * padded),
         moved=4 * MIB,
     )(base, arrived, wanted, weights)
-    pieces, total = kernel_call(
+    pieces, own_hubs = kernel_call(
         sum_chips,
-        (shape((PEERS, PIECE, TILE), BF16), shape((SUM_ROWS, TILE), F32)),
+        (shape((PEERS, PIECE, TILE), BF16), shape((8, padded), F32)),
         in_specs=[VM] * CHIPS + [ANY],
     )(sums, *to_chips(sums), base)
     pieces = swap(pieces)
@@ -604,7 +646,7 @@
         shape((nodes, width), F32),
         flops=4 * nodes * padded * width,
         moved=4 * MIB,
-    )(base, total, wanted, weights)
+    )(base, own_hubs, wanted, weights)
     first_self_sum, first_mean_sum, self_sum, mean_sum, loss = kernel_call(
         functools.partial(weight_outputs, samples_all),
         (

time: 137 us -> 133 us (0.971)
  Pallas kernels: 20.6 us -> 18.6 us
  starting transfers between devices: 25.9 us -> 24.4 us
    ppermute x4, waiting for transfers between devices: 3.52 us -> 1.91 us  [to_core(): lax.ppermute(values, 'grp', [(i, i ^ 1) for i in range(CHIPS * CORES)])]
    ppermute x4, starting transfers between devices: 17.9 us -> 16.4 us  [to_core(): lax.ppermute(values, 'grp', [(i, i ^ 1) for i in range(CHIPS * CORES)])]
    pallas_call x3 -> x5, Pallas kernels: 4.6 us -> 4.24 us  [the longest x1 1.61 us: on_device(): kernel_call(early_part, (shape((nodes, width), BF16), shape((2 * inputs,...]
  transfers between devices with their start and end apart: 13 -> 13, of which waited for: 9 -> 8; matrix products, arithmetic and copies ran while one was open for 0% -> 0% of each run, Pallas kernels for 6% -> 7%
where the time goes in v4:
time: 133 us
  blocking collectives  81.6 us (61%)
  starting transfers between devices  24.4 us (18%)
  Pallas kernels  18.6 us (14%)
  waiting for transfers between devices  6.58 us (5%)
  between operations  1.41 us (1%)
    all_to_all x4, blocking collectives, swap(): lax.all_to_all(values, 'dev', split_axis=0, concat_axis=0, tiled=True)  81.6 us
    ppermute x4, starting transfers between devices, to_core(): lax.ppermute(values, 'grp', [(i, i ^ 1) for i in range(CHIPS * CORES)])  16.4 us
    ppermute x9, starting transfers between devices, to_chips(): lax.ppermute(values, 'grp', [(i, (i + CORES * shift) % every) for i in ra...  8.01 us
    pallas_call x1, Pallas kernels, on_device(): kernel_call(functools.partial(main_part, samples_all, classes), (shape((n...  5.31 us
    ppermute x9, waiting for transfers between devices, to_chips(): lax.ppermute(values, 'grp', [(i, (i + CORES * shift) % every) for i in ra...  4.67 us
    pallas_call x1, Pallas kernels, on_device(): kernel_call(build_dense, (shape((nodes, table), BF16), shape((nodes, TILE...  3.06 us
  transfers between devices with their start and end apart: 13, of which 8 were waited for; matrix products, arithmetic and copies ran while one was open for 0% of the time, Pallas kernels for 7%

profile of v4, /device:TPU:1, one launch (start us, length us, event | category | flops | bytes accessed | tf_op | source)
XLA Modules:
  0.0 132.6 jit_solution(14562502879990282357)
XLA Ops:
  0.6 1.7 %shard_map.189 = bf16[1280,128]{1,0:T(8,128)(2,1)S(1)} custom-call(bf16[512,128]{1,0:T(8,128)(2,1)} %features_ref.3, s32[1,32,32]{2,1,0:T(8,128)} %send_any.1, s32[1,32]{1,0:T(1,128)} %refs_5_.1, s32[1,4]{1,0:T(1,128)} %refs_6_.1), custom_call_target="tpu_custom_call" | custom-call | tf_op jit(solution)/shard_map/pallas_call | solution.py:512
  2.4 22.0 %all_to_all.20.refs_13_.arrived_ref.feature_arrived_ref = bf16[32,40,128]{2,1,0:T(8,128)(2,1)S(1)} all-to-all(bf16[32,40,128]{2,1,0:T(8,128)(2,1)S(1)} %bitcast.9), channel_id=1, replica_groups=mesh['grp'=8,'dev'=32] {'dev'}, dimensions={0} | all-to-all | bytes 655360 | tf_op jit(solution)/shard_map/all_to_all | solution.py:462
  24.4 2.6 %collective-permute-start.2 = (bf16[128,128]{1,0:T(8,128)(2,1)S(1)}, bf16[128,128]{1,0:T(8,128)(2,1)S(1)}, u32[]{:S(2)}, u32[]{:S(2)}) collective-permute-start(bf16[128,128]{1,0:T(8,128)(2,1)S(1)} %shard_map.191.refs_0_), channel_id=1, source_target_pairs={{0,192},{32,224},{64,0},{96,32},{128,64},{160,96},{192,128},{224,1... | collective-permute-start | bytes 98312 | tf_op jit(solution)/shard_map/ppermute | solution.py:472
  28.7 3.1 %shard_map.190 = (bf16[512,2560]{1,0:T(8,128)(2,1)S(1)}, f32[512,128]{1,0:T(8,128)S(1)}, bf16[768,512]{1,0:T(8,128)(2,1)S(1)}, s32[40,32]{1,0:T(8,128)S(1)}, bf16[1280,512]{1,0:T(8,128)(2,1)S(1)}) custom-call(bf16[32,128,128]{2,1,0:T(8,128)(2,1)} %refs_0_.1, s32[1,32]{1,0:T(1,128)} %refs_1_.1, s32[1,32]{1,0:T(1,128)} %refs_2_.1, s32[1]{0:T(128)S(6)} %copy.21.refs_3_, ...), custom_call_target="tpu_custom_call" | custom-call | flops 335544320 | bytes 8388608 | tf_op jit(solution)/shard_map/pallas_call | solution.py:531
  31.9 5.8 %collective-permute-start.3 = (bf16[512,128]{1,0:T(8,128)(2,1)S(1)}, bf16[512,128]{1,0:T(8,128)(2,1)S(1)}, u32[]{:S(2)}, u32[]{:S(2)}) collective-permute-start(bf16[512,128]{1,0:T(8,128)(2,1)S(1)} %shard_map.192.own_hub_ref.feature_ref), channel_id=1, source_target_pairs={{0,32},{32,0},{64,96},{96,64},{128,160},{160,128},{192,224},{224,1... | collective-permute-start | bytes 393224 | tf_op jit(solution)/shard_map/ppermute | solution.py:466
  37.6 0.9 shard_map.193.part_ref
  38.6 1.0 shard_map.194
  39.6 14.7 %all_to_all.21.arrived_ref = bf16[32,40,128]{2,1,0:T(8,128)(2,1)S(1)} all-to-all(bf16[32,40,128]{2,1,0:T(8,128)(2,1)S(1)} %bitcast.10), channel_id=1, replica_groups=mesh['grp'=8,'dev'=32] {'dev'}, dimensions={0} | all-to-all | bytes 655360 | tf_op jit(solution)/shard_map/all_to_all | solution.py:462
  54.3 1.6 %collective-permute-start.6 = (bf16[128,128]{1,0:T(8,128)(2,1)S(1)}, bf16[128,128]{1,0:T(8,128)(2,1)S(1)}, u32[]{:S(2)}, u32[]{:S(2)}) collective-permute-start(bf16[128,128]{1,0:T(8,128)(2,1)S(1)} %shard_map.196.refs_0_), channel_id=1, source_target_pairs={{0,192},{32,224},{64,0},{96,32},{128,64},{160,96},{192,128},{224,1... | collective-permute-start | bytes 98312 | tf_op jit(solution)/shard_map/ppermute | solution.py:472
  55.9 1.1 collective-permute-start.5
  57.0 1.6 %shard_map.195 = (bf16[512,512]{1,0:T(8,128)(2,1)}, bf16[256,1536]{1,0:T(8,128)(2,1)S(1)}, bf16[1536,512]{1,0:T(8,128)(2,1)S(1)}, f32[512,512]{1,0:T(8,128)S(1)}, f32[512,256]{1,0:T(8,128)S(1)}) custom-call(bf16[512,128]{1,0:T(8,128)(2,1)S(1)} %copy-done, bf16[32,40,128]{2,1,0:T(8,128)(2,1)S(1)} %all_to_all.20.refs_13_.arrived_ref.feature_arrived_ref, ...), custom_call_target="tpu_custom_call" | custom-call | flops 1610612736 | bytes 8388608 | tf_op jit(solution)/shard_map/pallas_call | solution.py:577
  58.7 1.5 %collective-permute-done.5.refs_2_ = bf16[128,128]{1,0:T(8,128)(2,1)S(1)} collective-permute-done((bf16[128,128]{1,0:T(8,128)(2,1)S(1)}, bf16[128,128]{1,0:T(8,128)(2,1)S(1)}, u32[]{:S(2)}, u32[]{:S(2)}) %collective-permute-start.5) | collective-permute-done | bytes 32800 | tf_op jit(solution)/shard_map/ppermute | solution.py:472
  60.2 0.8 collective-permute-done.4.refs_1_
  61.0 5.8 %collective-permute-start.7 = (bf16[512,128]{1,0:T(8,128)(2,1)S(1)}, bf16[512,128]{1,0:T(8,128)(2,1)S(1)}, u32[]{:S(2)}, u32[]{:S(2)}) collective-permute-start(bf16[512,128]{1,0:T(8,128)(2,1)S(1)} %shard_map.197.mean_ref), channel_id=1, source_target_pairs={{0,32},{32,0},{64,96},{96,64},{128,160},{160,128},{192,224},{224,1... | collective-permute-start | bytes 393224 | tf_op jit(solution)/shard_map/ppermute | solution.py:466
  67.8 5.3 %shard_map.199 = (f32[512,512]{1,0:T(8,128)S(1)}, bf16[32,48,128]{2,1,0:T(8,128)(2,1)S(1)}, bf16[32,64,128]{2,1,0:T(8,128)(2,1)S(1)}, bf16[32,64,128]{2,1,0:T(8,128)(2,1)S(1)}) custom-call(bf16[256,1536]{1,0:T(8,128)(2,1)S(1)} %get-tuple-element.41.early_turned_ref, bf16[1536,512]{1,0:T(8,128)(2,1)S(1)} %get-tuple-element.42.early_source_ref, ...), custom_call_target="tpu_custom_call" | custom-call | tf_op jit(solution)/shard_map/pallas_call | solution.py:605
  73.6 1.5 %collective-permute-done.8.arrived_ref = bf16[32,64,128]{2,1,0:T(8,128)(2,1)S(1)} collective-permute-done((bf16[32,64,128]{2,1,0:T(8,128)(2,1)S(1)}, bf16[32,64,128]{2,1,0:T(8,128)(2,1)S(1)}, u32[]{:S(2)}, u32[]{:S(2)}) %collective-permute-start.8) | collective-permute-done | bytes 524320 | tf_op jit(solution)/shard_map/ppermute | solution.py:466
  75.3 26.7 %all_to_all.22.arrived_ref = bf16[32,112,128]{2,1,0:T(8,128)(2,1)S(1)} all-to-all(bf16[32,112,128]{2,1,0:T(8,128)(2,1)S(1)} %shard_map.200), channel_id=1, replica_groups=mesh['grp'=8,'dev'=32] {'dev'}, dimensions={0} | all-to-all | bytes 1835008 | tf_op jit(solution)/shard_map/all_to_all | solution.py:462
  103.6 1.3 %shard_map.201.refs_4_.base_ref = f32[512,512]{1,0:T(8,128)S(1)} custom-call(f32[512,512]{1,0:T(8,128)S(1)} %get-tuple-element.49.base_ref, bf16[32,112,128]{2,1,0:T(8,128)(2,1)S(1)} %all_to_all.22.arrived_ref, s32[40,32]{1,0:T(8,128)S(1)} %get-tuple-element.53.wanted_ref, bf16[768,512]{1,0:T(8,128)(2,1)S(1)} %get-tuple-element.39.weights_ref), custom_call_target="tpu_custom_call" | custom-call | flops 402653184 | bytes 4194304 | tf_op jit(solution)/shard_map/pallas_call | solution.py:630
  105.2 1.3 collective-permute-done.10.refs_2_
  106.5 0.8 collective-permute-done.9.refs_1_
  107.4 18.2 %all_to_all.23.mine_ref = bf16[32,40,128]{2,1,0:T(8,128)(2,1)S(1)} all-to-all(bf16[32,40,128]{2,1,0:T(8,128)(2,1)S(1)} %get-tuple-element.55), channel_id=1, replica_groups=mesh['grp'=8,'dev'=32] {'dev'}, dimensions={0} | all-to-all | bytes 655360 | tf_op jit(solution)/shard_map/all_to_all | solution.py:462
  125.6 4.4 %collective-permute-start.12 = (bf16[32,40,128]{2,1,0:T(8,128)(2,1)S(1)}, bf16[32,40,128]{2,1,0:T(8,128)(2,1)S(1)}, u32[]{:S(2)}, u32[]{:S(2)}) collective-permute-start(bf16[32,40,128]{2,1,0:T(8,128)(2,1)S(1)} %all_to_all.23.mine_ref), channel_id=1, source_target_pairs={{0,32},{32,0},{64,96},{96,64},{128,160},{160,128},{192,224},{224,1... | collective-permute-start | bytes 983048 | tf_op jit(solution)/shard_map/ppermute | solution.py:466
  130.0 1.5 %shard_map.204 = f32[512,512]{1,0:T(8,128)} custom-call(f32[512,512]{1,0:T(8,128)S(1)} %shard_map.201.refs_4_.base_ref, f32[8,256]{1,0:T(8,128)S(1)} %get-tuple-element.54.hub_ref, s32[40,32]{1,0:T(8,128)S(1)} %get-tuple-element.53.wanted_ref, bf16[768,512]{1,0:T(8,128)(2,1)S(1)} %get-tuple-element.39.weights_ref), custom_call_target="tpu_custom_call" | custom-call | flops 268435456 | bytes 4194304 | tf_op jit(solution)/shard_map/pallas_call | solution.py:644
  131.5 1.1 shard_map.205
  (25 shorter events, 4.8 us)
Async XLA Ops:
  24.4 13.2 %copy-start = (bf16[512,128]{1,0:T(8,128)(2,1)S(1)}, bf16[512,128]{1,0:T(8,128)(2,1)}, u32[]{:S(2)}) copy-start(bf16[512,128]{1,0:T(8,128)(2,1)} %features_ref.3) | copy-start | bytes 393220
  24.4 7.4 %collective-permute-start.2 = (bf16[128,128]{1,0:T(8,128)(2,1)S(1)}, bf16[128,128]{1,0:T(8,128)(2,1)S(1)}, u32[]{:S(2)}, u32[]{:S(2)}) collective-permute-start(bf16[128,128]{1,0:T(8,128)(2,1)S(1)} %shard_map.191.refs_0_), channel_id=1, source_target_pairs={{0,192},{32,224},{64,0},{96,32},{128,64},{160,96},{192,128},{224,1... | collective-permute-start | bytes 98312 | tf_op jit(solution)/shard_map/ppermute | solution.py:472
  27.0 4.9 %collective-permute-start.1 = (bf16[128,128]{1,0:T(8,128)(2,1)S(1)}, bf16[128,128]{1,0:T(8,128)(2,1)S(1)}, u32[]{:S(2)}, u32[]{:S(2)}) collective-permute-start(bf16[128,128]{1,0:T(8,128)(2,1)S(1)} %shard_map.191.refs_0_), channel_id=1, source_target_pairs={{0,128},{32,160},{64,192},{96,224},{128,0},{160,32},{192,64},{224,... | collective-permute-start | bytes 98312 | tf_op jit(solution)/shard_map/ppermute | solution.py:472
  27.5 4.3 %collective-permute-start = (bf16[128,128]{1,0:T(8,128)(2,1)S(1)}, bf16[128,128]{1,0:T(8,128)(2,1)S(1)}, u32[]{:S(2)}, u32[]{:S(2)}) collective-permute-start(bf16[128,128]{1,0:T(8,128)(2,1)S(1)} %shard_map.191.refs_0_), channel_id=1, source_target_pairs={{0,64},{32,96},{64,128},{96,160},{128,192},{160,224},{192,0},{224,... | collective-permute-start | bytes 98312 | tf_op jit(solution)/shard_map/ppermute | solution.py:472
  31.9 6.7 %collective-permute-start.3 = (bf16[512,128]{1,0:T(8,128)(2,1)S(1)}, bf16[512,128]{1,0:T(8,128)(2,1)S(1)}, u32[]{:S(2)}, u32[]{:S(2)}) collective-permute-start(bf16[512,128]{1,0:T(8,128)(2,1)S(1)} %shard_map.192.own_hub_ref.feature_ref), channel_id=1, source_target_pairs={{0,32},{32,0},{64,96},{96,64},{128,160},{160,128},{192,224},{224,1... | collective-permute-start | bytes 393224 | tf_op jit(solution)/shard_map/ppermute | solution.py:466
  54.3 4.4 %collective-permute-start.6 = (bf16[128,128]{1,0:T(8,128)(2,1)S(1)}, bf16[128,128]{1,0:T(8,128)(2,1)S(1)}, u32[]{:S(2)}, u32[]{:S(2)}) collective-permute-start(bf16[128,128]{1,0:T(8,128)(2,1)S(1)} %shard_map.196.refs_0_), channel_id=1, source_target_pairs={{0,192},{32,224},{64,0},{96,32},{128,64},{160,96},{192,128},{224,1... | collective-permute-start | bytes 98312 | tf_op jit(solution)/shard_map/ppermute | solution.py:472
  55.9 4.3 %collective-permute-start.5 = (bf16[128,128]{1,0:T(8,128)(2,1)S(1)}, bf16[128,128]{1,0:T(8,128)(2,1)S(1)}, u32[]{:S(2)}, u32[]{:S(2)}) collective-permute-start(bf16[128,128]{1,0:T(8,128)(2,1)S(1)} %shard_map.196.refs_0_), channel_id=1, source_target_pairs={{0,128},{32,160},{64,192},{96,224},{128,0},{160,32},{192,64},{224,... | collective-permute-start | bytes 98312 | tf_op jit(solution)/shard_map/ppermute | solution.py:472
  57.0 4.0 %collective-permute-start.4 = (bf16[128,128]{1,0:T(8,128)(2,1)S(1)}, bf16[128,128]{1,0:T(8,128)(2,1)S(1)}, u32[]{:S(2)}, u32[]{:S(2)}) collective-permute-start(bf16[128,128]{1,0:T(8,128)(2,1)S(1)} %shard_map.196.refs_0_), channel_id=1, source_target_pairs={{0,64},{32,96},{64,128},{96,160},{128,192},{160,224},{192,0},{224,... | collective-permute-start | bytes 98312 | tf_op jit(solution)/shard_map/ppermute | solution.py:472
  61.0 6.8 %collective-permute-start.7 = (bf16[512,128]{1,0:T(8,128)(2,1)S(1)}, bf16[512,128]{1,0:T(8,128)(2,1)S(1)}, u32[]{:S(2)}, u32[]{:S(2)}) collective-permute-start(bf16[512,128]{1,0:T(8,128)(2,1)S(1)} %shard_map.197.mean_ref), channel_id=1, source_target_pairs={{0,32},{32,0},{64,96},{96,64},{128,160},{160,128},{192,224},{224,1... | collective-permute-start | bytes 393224 | tf_op jit(solution)/shard_map/ppermute | solution.py:466
  73.1 2.0 %collective-permute-start.8 = (bf16[32,64,128]{2,1,0:T(8,128)(2,1)S(1)}, bf16[32,64,128]{2,1,0:T(8,128)(2,1)S(1)}, u32[]{:S(2)}, u32[]{:S(2)}) collective-permute-start(bf16[32,64,128]{2,1,0:T(8,128)(2,1)S(1)} %get-tuple-element.51), channel_id=1, source_target_pairs={{0,32},{32,0},{64,96},{96,64},{128,160},{160,128},{192,224},{224,1... | collective-permute-start | bytes 1572872 | tf_op jit(solution)/shard_map/ppermute | solution.py:466
  102.1 3.1 %collective-permute-start.11 = (f32[64,128]{1,0:T(8,128)S(1)}, f32[64,128]{1,0:T(8,128)S(1)}, u32[]{:S(2)}, u32[]{:S(2)}) collective-permute-start(f32[64,128]{1,0:T(8,128)S(1)} %shard_map.202.refs_0_), channel_id=1, source_target_pairs={{0,192},{32,224},{64,0},{96,32},{128,64},{160,96},{192,128},{224,1... | collective-permute-start | bytes 98312 | tf_op jit(solution)/shard_map/ppermute | solution.py:472
  102.2 4.4 %collective-permute-start.10 = (f32[64,128]{1,0:T(8,128)S(1)}, f32[64,128]{1,0:T(8,128)S(1)}, u32[]{:S(2)}, u32[]{:S(2)}) collective-permute-start(f32[64,128]{1,0:T(8,128)S(1)} %shard_map.202.refs_0_), channel_id=1, source_target_pairs={{0,128},{32,160},{64,192},{96,224},{128,0},{160,32},{192,64},{224,... | collective-permute-start | bytes 98312 | tf_op jit(solution)/shard_map/ppermute | solution.py:472
  102.9 4.4 %collective-permute-start.9 = (f32[64,128]{1,0:T(8,128)S(1)}, f32[64,128]{1,0:T(8,128)S(1)}, u32[]{:S(2)}, u32[]{:S(2)}) collective-permute-start(f32[64,128]{1,0:T(8,128)S(1)} %shard_map.202.refs_0_), channel_id=1, source_target_pairs={{0,64},{32,96},{64,128},{96,160},{128,192},{160,224},{192,0},{224,... | collective-permute-start | bytes 98312 | tf_op jit(solution)/shard_map/ppermute | solution.py:472
  125.6 6.0 %collective-permute-start.12 = (bf16[32,40,128]{2,1,0:T(8,128)(2,1)S(1)}, bf16[32,40,128]{2,1,0:T(8,128)(2,1)S(1)}, u32[]{:S(2)}, u32[]{:S(2)}) collective-permute-start(bf16[32,40,128]{2,1,0:T(8,128)(2,1)S(1)} %all_to_all.23.mine_ref), channel_id=1, source_target_pairs={{0,32},{32,0},{64,96},{96,64},{128,160},{160,128},{192,224},{224,1... | collective-permute-start | bytes 983048 | tf_op jit(solution)/shard_map/ppermute | solution.py:466

commit v5 on v4

--- a/solution.py
+++ b/solution.py
@@ -82,6 +82,10 @@
     return group // CORES, group % CORES
 
 
+def before(place, step, size):
+    return (place + size - step) % size
+
+
 def fetch(pairs, sems):
     loads = [pltpu.make_async_copy(source, target, sems.at[i]) for i, (source, target) in enumerate(pairs)]
     for load in loads:
@@ -163,6 +167,21 @@
     degree = jnp.maximum(nn(dense_ref[...], jnp.ones((dense_ref.shape[1], TILE), BF16)), 1.0)
     lane = iota(degree.shape, 1)
     numbers_ref[...] = jnp.where(lane == 0, degree, jnp.where(lane == 1, times, label.astype(F32)))
+
+
+def build_turned(adj_any, dst_any, src_any, live_ref, unused, turned_ref, adj_ref, dst_ref, src_ref, sems):
+    loads = fetch(((dst_any, dst_ref), (src_any, src_ref), (adj_any, adj_ref)), sems)
+    turned_ref[...] = jnp.zeros_like(turned_ref)
+    for load in loads:
+        load.wait()
+
+    def add(t, carry):
+        rows = pl.ds(pl.multiple_of(src_ref[0, t] * TILE, TILE), TILE)
+        columns = pl.ds(pl.multiple_of(dst_ref[0, t] * TILE, TILE), TILE)
+        turned_ref[rows, columns] += jnp.transpose(adj_ref[t])
+        return carry
+
+    lax.fori_loop(0, live_ref[0], add, 0)
 
 
 def group_hubs(arrived_ref, out_ref):
@@ -267,7 +286,7 @@
 
 
 def own_hub_part(
-    dense_ref, weights_ref, part_ref, feature_ref, mean_ref, turned_ref, source_ref, columns_ref, out_ref
+    dense_ref, weights_ref, part_ref, feature_ref, mean_ref, turned_ref, source_ref, out_ref, columns_ref
 ):
     total = hub_part(
         dense_ref, weights_ref, feature_ref[...], mean_ref[...], False, turned_ref, source_ref, columns_ref
@@ -277,10 +296,10 @@
 
 def main_part(
     samples_all, classes,
-    early_turned_ref, early_source_ref, logits_ref, own_turned_ref, own_source_ref, own_columns_ref, part_ref,
-    dense_ref, numbers_ref, weights_ref, feature_ref, mean_ref,
+    early_turned_ref, early_source_ref, logits_ref, own_turned_ref, own_source_ref, part_ref,
+    dense_ref, adjoint_ref, numbers_ref, weights_ref, feature_ref, mean_ref,
     base_ref, edge_ref, mine_ref, theirs_ref,
-    other_turned_ref, other_source_ref, other_columns_ref, scaled_ref, masked_ref, stack_ref, rest_ref,
+    other_turned_ref, other_source_ref, other_columns_ref, order_ref, scaled_ref, masked_ref, stack_ref, rest_ref,
 ):
     nodes, width = base_ref.shape
     padded = SELF_AT
@@ -309,24 +328,27 @@
     loss = jnp.sum(times * (jnp.log(total) - chosen), axis=0, keepdims=True)
     upstream = times * ((powers / total - onehot) / samples_all)
     upstream = upstream.astype(BF16)
-    scaled_ref[...] = jnp.transpose((upstream.astype(F32) / degree).astype(BF16))
-
-    def back(columns):
-        found = nn(scaled_ref[...], columns)
-        found = jnp.transpose(found.astype(BF16))
-        return found, nn(found, weights_ref[mean_rows, :])
+    scaled_ref[...] = (upstream.astype(F32) / degree).astype(BF16)
+
+    def back(rows):
+        found = nn(rows, scaled_ref[...])
+        return found, nn(found.astype(BF16), weights_ref[mean_rows, :])
 
     def mask(at, source, grad):
         masked_ref[at : at + nodes, :] = jnp.where(source > 0, grad, 0.0).astype(BF16)
 
     low = iota((8, padded), 0) < HUBS_EACH
     hub_at = nodes + PEERS * CAPACITY
-    for i, (columns_ref, source_ref, out_ref) in enumerate(
-        ((own_columns_ref, own_source_ref, mine_ref), (other_columns_ref, other_source_ref, theirs_ref))
+    chip, core = position()
+    for i, (there, source_ref, out_ref) in enumerate(
+        ((core, own_source_ref, mine_ref), (1 - core, other_source_ref, theirs_ref))
     ):
-        found, spread = back(columns_ref[...])
+        for block in range(CHIPS):
+            at = nodes + (before(chip, block, CHIPS) * CORES + there) * GROUP_HUBS
+            rows = adjoint_ref[pl.ds(pl.multiple_of(at, GROUP_HUBS), GROUP_HUBS), :]
+            order_ref[block * GROUP_HUBS : (block + 1) * GROUP_HUBS, :] = rows
+        found, spread = back(order_ref[...])
         mask(hub_at + i * nodes, source_ref[...], spread)
-        found = found.astype(F32)
         for n in range(0, PEERS, 2):
             first, second = [], []
             for pair in range(CHIPS // 2):
@@ -340,19 +362,19 @@
                 out_ref[member, 0:HUB_ROWS, :] = rows.astype(BF16)
                 rest_ref[i, member] = join_rests(blocks[0][:, TILE:], blocks[1][:, TILE:])
 
-    unused, spread = back(dense_ref[:, 0:nodes])
+    unused, spread = back(adjoint_ref[0:nodes, :])
     base = nn(upstream, weights_ref[self_rows, :]) + spread
     base_ref[...] = base
     mask(0, hidden, base)
     each = nodes // CAPACITY
     for i in range(PEERS // each):
-        found, spread = back(dense_ref[:, edge_at + i * nodes : edge_at + (i + 1) * nodes])
+        found, spread = back(adjoint_ref[edge_at + i * nodes : edge_at + (i + 1) * nodes, :])
         at = (i + 1) * nodes
         mask(at, early_source_ref[at : at + nodes, :], spread)
         for p in range(each):
             at = p * CAPACITY
-            rest = found[at : at + CAPACITY, TILE:].astype(F32)
-            edge_ref[i * each + p, 0:CAPACITY, :] = found[at : at + CAPACITY, 0:TILE]
+            rest = found[at : at + CAPACITY, TILE:]
+            edge_ref[i * each + p, 0:CAPACITY, :] = found[at : at + CAPACITY, 0:TILE].astype(BF16)
             edge_ref[i * each + p, CAPACITY:EDGE_ROWS, :] = join_rests(
                 rest[0 : CAPACITY // 2], rest[CAPACITY // 2 :]
             ).astype(BF16)
@@ -370,7 +392,6 @@
         + nn(own_turned_ref[...], masked_ref[hub_at : hub_at + nodes, :])
         + nn(other_turned_ref[...], masked_ref[hub_at + nodes :, :])
     )
-    unused, core = position()
     for i, (there, out_ref) in enumerate(((core, mine_ref), (1 - core, theirs_ref))):
         for n in range(PEERS):
             at = there * (STACK_ROWS // CORES) + PIECE * (n % 8)
@@ -588,16 +609,32 @@
         flops=6 * nodes * edges * width,
         moved=8 * MIB,
     )(features, feature_arrived, mean_rows, mean_arrived, dense, weights)
-    mean_hubs = gather_hubs(mean_arrived, [own_logits])
+    turned = kernel_call(
+        build_turned,
+        shape((table, nodes), BF16),
+        [
+            pltpu.VMEM(tile_adj.shape, BF16),
+            pltpu.SMEM(tile_dst.shape, I32),
+            pltpu.SMEM(tile_src.shape, I32),
+            pltpu.SemaphoreType.DMA((3,)),
+        ],
+        [HBM, HBM, HBM, SM, ANY],
+        moved=4 * MIB,
+    )(
+        *(pltpu.with_memory_space_constraint(operand, pltpu.HBM) for operand in (tile_adj, tile_dst, tile_src)),
+        tile_count,
+        mean_arrived,
+    )
+    mean_hubs = gather_hubs(mean_arrived, [own_logits, turned])
     half = CHIPS * GROUP_HUBS
-    own_turned, own_source, own_columns, part = kernel_call(
+    own_turned, own_source, part = kernel_call(
         own_hub_part,
         (
             shape((2 * inputs, half), BF16),
             shape((half, width), BF16),
-            shape((nodes, half), BF16),
             shape((nodes, width), F32),
         ),
+        [pltpu.VMEM((nodes, half), BF16)],
         limit=6,
         flops=4 * nodes * half * width,
         moved=4 * MIB,
@@ -614,15 +651,16 @@
             pltpu.VMEM((2 * inputs, half), BF16),
             pltpu.VMEM((half, width), BF16),
             pltpu.VMEM((nodes, half), BF16),
-            pltpu.VMEM((padded, nodes), BF16),
+            pltpu.VMEM((half, nodes), BF16),
+            pltpu.VMEM((nodes, padded), BF16),
             pltpu.VMEM((table, width), BF16),
             pltpu.VMEM((STACK_ROWS, width), F32),
             pltpu.VMEM((CORES, PEERS, HUB_PACKED - HUB_ROWS, TILE), F32),
         ],
         limit=20,
     )(
-        early_turned, early_source, own_logits, own_turned, own_source, own_columns, part,
-        dense, numbers, weights, feature_hubs[1], mean_hubs[1],
+        early_turned, early_source, own_logits, own_turned, own_source, part,
+        dense, turned, numbers, weights, feature_hubs[1], mean_hubs[1],
     )
     rows = kernel_call(sum_cores, shape((PEERS, BACK_ROWS, TILE), BF16))(mine, to_core(theirs), edge_rows)
     arrived = swap(rows)

time: 133 us -> 135 us (1.015)
  starting transfers between devices: 24.4 us -> 26.6 us
  Pallas kernels: 18.6 us -> 20.7 us
  waiting for transfers between devices: 6.58 us -> 4.49 us
    pallas_call x0 -> x1, Pallas kernels: none -> 3.12 us  [on_device(): kernel_call(build_turned, shape((table, nodes), BF16), [pltpu.VMEM(tile_a...]
    ppermute x9, waiting for transfers between devices: 4.67 us -> 2.58 us  [to_chips(): lax.ppermute(values, 'grp', [(i, (i + CORES * shift) % every) for i in ra...]
    ppermute x9, starting transfers between devices: 8.01 us -> 10 us  [to_chips(): lax.ppermute(values, 'grp', [(i, (i + CORES * shift) % every) for i in ra...]
  transfers between devices with their start and end apart: 13 -> 13, of which waited for: 8 -> 5; matrix products, arithmetic and copies ran while one was open for 0% -> 0% of each run, Pallas kernels for 7% -> 9%
where the time goes in v5:
time: 135 us
  blocking collectives  81.5 us (60%)
  starting transfers between devices  26.6 us (20%)
  Pallas kernels  20.7 us (15%)
  waiting for transfers between devices  4.49 us (3%)
  between operations  1.45 us (1%)
    all_to_all x4, blocking collectives, swap(): lax.all_to_all(values, 'dev', split_axis=0, concat_axis=0, tiled=True)  81.5 us
    ppermute x4, starting transfers between devices, to_core(): lax.ppermute(values, 'grp', [(i, i ^ 1) for i in range(CHIPS * CORES)])  16.5 us
    ppermute x9, starting transfers between devices, to_chips(): lax.ppermute(values, 'grp', [(i, (i + CORES * shift) % every) for i in ra...  10 us
    pallas_call x1, Pallas kernels, on_device(): kernel_call(functools.partial(main_part, samples_all, classes), (shape((n...  4.39 us
    pallas_call x1, Pallas kernels, on_device(): kernel_call(build_turned, shape((table, nodes), BF16), [pltpu.VMEM(tile_a...  3.12 us
    pallas_call x1, Pallas kernels, on_device(): kernel_call(build_dense, (shape((nodes, table), BF16), shape((nodes, TILE...  3.01 us
  transfers between devices with their start and end apart: 13, of which 5 were waited for; matrix products, arithmetic and copies ran while one was open for 0% of the time, Pallas kernels for 9%

profile of v5, /device:TPU:1, one launch (start us, length us, event | category | flops | bytes accessed | tf_op | source)
XLA Modules:
  0.0 134.7 jit_solution(6920199205249176822)
XLA Ops:
  0.6 1.7 %shard_map.189 = bf16[1280,128]{1,0:T(8,128)(2,1)S(1)} custom-call(bf16[512,128]{1,0:T(8,128)(2,1)} %features_ref.3, s32[1,32,32]{2,1,0:T(8,128)} %send_any.1, s32[1,32]{1,0:T(1,128)} %refs_5_.1, s32[1,4]{1,0:T(1,128)} %refs_6_.1), custom_call_target="tpu_custom_call" | custom-call | tf_op jit(solution)/shard_map/pallas_call | solution.py:533
  2.4 22.0 %all_to_all.20.refs_13_.arrived_ref.feature_arrived_ref = bf16[32,40,128]{2,1,0:T(8,128)(2,1)S(1)} all-to-all(bf16[32,40,128]{2,1,0:T(8,128)(2,1)S(1)} %bitcast.9), channel_id=1, replica_groups=mesh['grp'=8,'dev'=32] {'dev'}, dimensions={0} | all-to-all | bytes 655360 | tf_op jit(solution)/shard_map/all_to_all | solution.py:483
  24.4 2.6 %collective-permute-start.2 = (bf16[128,128]{1,0:T(8,128)(2,1)S(1)}, bf16[128,128]{1,0:T(8,128)(2,1)S(1)}, u32[]{:S(2)}, u32[]{:S(2)}) collective-permute-start(bf16[128,128]{1,0:T(8,128)(2,1)S(1)} %shard_map.191.refs_0_), channel_id=1, source_target_pairs={{0,192},{32,224},{64,0},{96,32},{128,64},{160,96},{192,128},{224,1... | collective-permute-start | bytes 98312 | tf_op jit(solution)/shard_map/ppermute | solution.py:493
  28.7 3.0 %shard_map.190 = (bf16[512,2560]{1,0:T(8,128)(2,1)S(1)}, f32[512,128]{1,0:T(8,128)S(1)}, bf16[768,512]{1,0:T(8,128)(2,1)S(1)}, s32[40,32]{1,0:T(8,128)S(1)}, bf16[1280,512]{1,0:T(8,128)(2,1)S(1)}) custom-call(bf16[32,128,128]{2,1,0:T(8,128)(2,1)} %adj_any.1, s32[1,32]{1,0:T(1,128)} %dst_any.1, s32[1,32]{1,0:T(1,128)} %src_any.1, ...), custom_call_target="tpu_custom_call" | custom-call | flops 335544320 | bytes 8388608 | tf_op jit(solution)/shard_map/pallas_call | solution.py:552
  31.8 5.8 %collective-permute-start.3 = (bf16[512,128]{1,0:T(8,128)(2,1)S(1)}, bf16[512,128]{1,0:T(8,128)(2,1)S(1)}, u32[]{:S(2)}, u32[]{:S(2)}) collective-permute-start(bf16[512,128]{1,0:T(8,128)(2,1)S(1)} %shard_map.192.own_hub_ref.feature_ref), channel_id=1, source_target_pairs={{0,32},{32,0},{64,96},{96,64},{128,160},{160,128},{192,224},{224,1... | collective-permute-start | bytes 393224 | tf_op jit(solution)/shard_map/ppermute | solution.py:487
  37.6 0.9 shard_map.193.part_ref
  38.6 1.0 shard_map.194
  39.6 14.7 %all_to_all.21.arrived_ref.unused = bf16[32,40,128]{2,1,0:T(8,128)(2,1)S(1)} all-to-all(bf16[32,40,128]{2,1,0:T(8,128)(2,1)S(1)} %bitcast.10), channel_id=1, replica_groups=mesh['grp'=8,'dev'=32] {'dev'}, dimensions={0} | all-to-all | bytes 655360 | tf_op jit(solution)/shard_map/all_to_all | solution.py:483
  54.3 1.6 %collective-permute-start.6 = (bf16[128,128]{1,0:T(8,128)(2,1)S(1)}, bf16[128,128]{1,0:T(8,128)(2,1)S(1)}, u32[]{:S(2)}, u32[]{:S(2)}) collective-permute-start(bf16[128,128]{1,0:T(8,128)(2,1)S(1)} %shard_map.196.refs_0_), channel_id=1, source_target_pairs={{0,192},{32,224},{64,0},{96,32},{128,64},{160,96},{192,128},{224,1... | collective-permute-start | bytes 98312 | tf_op jit(solution)/shard_map/ppermute | solution.py:493
  55.8 1.3 collective-permute-start.5
  57.1 1.6 %shard_map.195 = (bf16[512,512]{1,0:T(8,128)(2,1)}, bf16[256,1536]{1,0:T(8,128)(2,1)S(1)}, bf16[1536,512]{1,0:T(8,128)(2,1)S(1)}, f32[512,512]{1,0:T(8,128)S(1)}, f32[512,256]{1,0:T(8,128)S(1)}) custom-call(bf16[512,128]{1,0:T(8,128)(2,1)S(1)} %copy-done, bf16[32,40,128]{2,1,0:T(8,128)(2,1)S(1)} %all_to_all.20.refs_13_.arrived_ref.feature_arrived_ref, ...), custom_call_target="tpu_custom_call" | custom-call | flops 1610612736 | bytes 8388608 | tf_op jit(solution)/shard_map/pallas_call | solution.py:598
  58.7 3.1 %shard_map.197.refs_5_.adjoint_ref = bf16[2560,512]{1,0:T(8,128)(2,1)S(1)} custom-call(bf16[32,128,128]{2,1,0:T(8,128)(2,1)} %adj_any.1, s32[1,32]{1,0:T(1,128)} %dst_any.1, s32[1,32]{1,0:T(1,128)} %src_any.1, s32[1]{0:T(128)S(6)} %copy.21.refs_3_.live_ref, bf16[32,40,128]{2,1,0:T(8,128)(2,1)S(1)} %all_to_all.21.arrived_ref.unused), custom_call_target="tpu_custom_call" | custom-call | bytes 4194304 | tf_op jit(solution)/shard_map/pallas_call | solution.py:612
  61.9 5.0 %collective-permute-start.7 = (bf16[512,128]{1,0:T(8,128)(2,1)S(1)}, bf16[512,128]{1,0:T(8,128)(2,1)S(1)}, u32[]{:S(2)}, u32[]{:S(2)}) collective-permute-start(bf16[512,128]{1,0:T(8,128)(2,1)S(1)} %shard_map.198.mean_ref), channel_id=1, source_target_pairs={{0,32},{32,0},{64,96},{96,64},{128,160},{160,128},{192,224},{224,1... | collective-permute-start | bytes 393224 | tf_op jit(solution)/shard_map/ppermute | solution.py:487
  66.9 0.7 shard_map.199
  67.9 4.4 %shard_map.200 = (f32[512,512]{1,0:T(8,128)S(1)}, bf16[32,48,128]{2,1,0:T(8,128)(2,1)S(1)}, bf16[32,64,128]{2,1,0:T(8,128)(2,1)S(1)}, bf16[32,64,128]{2,1,0:T(8,128)(2,1)S(1)}) custom-call(bf16[256,1536]{1,0:T(8,128)(2,1)S(1)} %get-tuple-element.40.early_turned_ref, bf16[1536,512]{1,0:T(8,128)(2,1)S(1)} %get-tuple-element.41.early_source_ref, ...), custom_call_target="tpu_custom_call" | custom-call | tf_op jit(solution)/shard_map/pallas_call | solution.py:642
  72.7 1.5 %collective-permute-done.8.arrived_ref = bf16[32,64,128]{2,1,0:T(8,128)(2,1)S(1)} collective-permute-done((bf16[32,64,128]{2,1,0:T(8,128)(2,1)S(1)}, bf16[32,64,128]{2,1,0:T(8,128)(2,1)S(1)}, u32[]{:S(2)}, u32[]{:S(2)}) %collective-permute-start.8) | collective-permute-done | bytes 524320 | tf_op jit(solution)/shard_map/ppermute | solution.py:487
  74.4 26.7 %all_to_all.22.arrived_ref = bf16[32,112,128]{2,1,0:T(8,128)(2,1)S(1)} all-to-all(bf16[32,112,128]{2,1,0:T(8,128)(2,1)S(1)} %shard_map.201), channel_id=1, replica_groups=mesh['grp'=8,'dev'=32] {'dev'}, dimensions={0} | all-to-all | bytes 1835008 | tf_op jit(solution)/shard_map/all_to_all | solution.py:483
  101.2 2.8 %collective-permute-start.11 = (f32[64,128]{1,0:T(8,128)S(1)}, f32[64,128]{1,0:T(8,128)S(1)}, u32[]{:S(2)}, u32[]{:S(2)}) collective-permute-start(f32[64,128]{1,0:T(8,128)S(1)} %shard_map.203.refs_0_), channel_id=1, source_target_pairs={{0,192},{32,224},{64,0},{96,32},{128,64},{160,96},{192,128},{224,1... | collective-permute-start | bytes 98312 | tf_op jit(solution)/shard_map/ppermute | solution.py:493
  104.7 1.3 shard_map.202.refs_4_.base_ref
  106.1 2.3 %collective-permute-done.10.refs_2_ = f32[64,128]{1,0:T(8,128)S(1)} collective-permute-done((f32[64,128]{1,0:T(8,128)S(1)}, f32[64,128]{1,0:T(8,128)S(1)}, u32[]{:S(2)}, u32[]{:S(2)}) %collective-permute-start.10) | collective-permute-done | bytes 32800 | tf_op jit(solution)/shard_map/ppermute | solution.py:493
  108.8 18.1 %all_to_all.23.mine_ref = bf16[32,40,128]{2,1,0:T(8,128)(2,1)S(1)} all-to-all(bf16[32,40,128]{2,1,0:T(8,128)(2,1)S(1)} %get-tuple-element.53), channel_id=1, replica_groups=mesh['grp'=8,'dev'=32] {'dev'}, dimensions={0} | all-to-all | bytes 655360 | tf_op jit(solution)/shard_map/all_to_all | solution.py:483
  126.8 5.3 %collective-permute-start.12 = (bf16[32,40,128]{2,1,0:T(8,128)(2,1)S(1)}, bf16[32,40,128]{2,1,0:T(8,128)(2,1)S(1)}, u32[]{:S(2)}, u32[]{:S(2)}) collective-permute-start(bf16[32,40,128]{2,1,0:T(8,128)(2,1)S(1)} %all_to_all.23.mine_ref), channel_id=1, source_target_pairs={{0,32},{32,0},{64,96},{96,64},{128,160},{160,128},{192,224},{224,1... | collective-permute-start | bytes 983048 | tf_op jit(solution)/shard_map/ppermute | solution.py:487
  132.1 1.5 %shard_map.205 = f32[512,512]{1,0:T(8,128)} custom-call(f32[512,512]{1,0:T(8,128)S(1)} %shard_map.202.refs_4_.base_ref, f32[8,256]{1,0:T(8,128)S(1)} %get-tuple-element.52.hub_ref, s32[40,32]{1,0:T(8,128)S(1)} %get-tuple-element.51.wanted_ref, bf16[768,512]{1,0:T(8,128)(2,1)S(1)} %get-tuple-element.38.weights_ref), custom_call_target="tpu_custom_call" | custom-call | flops 268435456 | bytes 4194304 | tf_op jit(solution)/shard_map/pallas_call | solution.py:682
  133.6 1.1 shard_map.206
  (26 shorter events, 3.2 us)
Async XLA Ops:
  0.6 37.0 %copy-start = (bf16[512,128]{1,0:T(8,128)(2,1)S(1)}, bf16[512,128]{1,0:T(8,128)(2,1)}, u32[]{:S(2)}) copy-start(bf16[512,128]{1,0:T(8,128)(2,1)} %features_ref.3) | copy-start | bytes 393220
  24.4 7.3 %collective-permute-start.2 = (bf16[128,128]{1,0:T(8,128)(2,1)S(1)}, bf16[128,128]{1,0:T(8,128)(2,1)S(1)}, u32[]{:S(2)}, u32[]{:S(2)}) collective-permute-start(bf16[128,128]{1,0:T(8,128)(2,1)S(1)} %shard_map.191.refs_0_), channel_id=1, source_target_pairs={{0,192},{32,224},{64,0},{96,32},{128,64},{160,96},{192,128},{224,1... | collective-permute-start | bytes 98312 | tf_op jit(solution)/shard_map/ppermute | solution.py:493
  27.0 4.8 %collective-permute-start.1 = (bf16[128,128]{1,0:T(8,128)(2,1)S(1)}, bf16[128,128]{1,0:T(8,128)(2,1)S(1)}, u32[]{:S(2)}, u32[]{:S(2)}) collective-permute-start(bf16[128,128]{1,0:T(8,128)(2,1)S(1)} %shard_map.191.refs_0_), channel_id=1, source_target_pairs={{0,128},{32,160},{64,192},{96,224},{128,0},{160,32},{192,64},{224,... | collective-permute-start | bytes 98312 | tf_op jit(solution)/shard_map/ppermute | solution.py:493
  27.5 4.3 %collective-permute-start = (bf16[128,128]{1,0:T(8,128)(2,1)S(1)}, bf16[128,128]{1,0:T(8,128)(2,1)S(1)}, u32[]{:S(2)}, u32[]{:S(2)}) collective-permute-start(bf16[128,128]{1,0:T(8,128)(2,1)S(1)} %shard_map.191.refs_0_), channel_id=1, source_target_pairs={{0,64},{32,96},{64,128},{96,160},{128,192},{160,224},{192,0},{224,... | collective-permute-start | bytes 98312 | tf_op jit(solution)/shard_map/ppermute | solution.py:493
  31.8 6.8 %collective-permute-start.3 = (bf16[512,128]{1,0:T(8,128)(2,1)S(1)}, bf16[512,128]{1,0:T(8,128)(2,1)S(1)}, u32[]{:S(2)}, u32[]{:S(2)}) collective-permute-start(bf16[512,128]{1,0:T(8,128)(2,1)S(1)} %shard_map.192.own_hub_ref.feature_ref), channel_id=1, source_target_pairs={{0,32},{32,0},{64,96},{96,64},{128,160},{160,128},{192,224},{224,1... | collective-permute-start | bytes 393224 | tf_op jit(solution)/shard_map/ppermute | solution.py:487
  54.3 7.6 %collective-permute-start.6 = (bf16[128,128]{1,0:T(8,128)(2,1)S(1)}, bf16[128,128]{1,0:T(8,128)(2,1)S(1)}, u32[]{:S(2)}, u32[]{:S(2)}) collective-permute-start(bf16[128,128]{1,0:T(8,128)(2,1)S(1)} %shard_map.196.refs_0_), channel_id=1, source_target_pairs={{0,192},{32,224},{64,0},{96,32},{128,64},{160,96},{192,128},{224,1... | collective-permute-start | bytes 98312 | tf_op jit(solution)/shard_map/ppermute | solution.py:493
  55.8 6.0 %collective-permute-start.5 = (bf16[128,128]{1,0:T(8,128)(2,1)S(1)}, bf16[128,128]{1,0:T(8,128)(2,1)S(1)}, u32[]{:S(2)}, u32[]{:S(2)}) collective-permute-start(bf16[128,128]{1,0:T(8,128)(2,1)S(1)} %shard_map.196.refs_0_), channel_id=1, source_target_pairs={{0,128},{32,160},{64,192},{96,224},{128,0},{160,32},{192,64},{224,... | collective-permute-start | bytes 98312 | tf_op jit(solution)/shard_map/ppermute | solution.py:493
  57.1 4.8 %collective-permute-start.4 = (bf16[128,128]{1,0:T(8,128)(2,1)S(1)}, bf16[128,128]{1,0:T(8,128)(2,1)S(1)}, u32[]{:S(2)}, u32[]{:S(2)}) collective-permute-start(bf16[128,128]{1,0:T(8,128)(2,1)S(1)} %shard_map.196.refs_0_), channel_id=1, source_target_pairs={{0,64},{32,96},{64,128},{96,160},{128,192},{160,224},{192,0},{224,... | collective-permute-start | bytes 98312 | tf_op jit(solution)/shard_map/ppermute | solution.py:493
  61.9 6.0 %collective-permute-start.7 = (bf16[512,128]{1,0:T(8,128)(2,1)S(1)}, bf16[512,128]{1,0:T(8,128)(2,1)S(1)}, u32[]{:S(2)}, u32[]{:S(2)}) collective-permute-start(bf16[512,128]{1,0:T(8,128)(2,1)S(1)} %shard_map.198.mean_ref), channel_id=1, source_target_pairs={{0,32},{32,0},{64,96},{96,64},{128,160},{160,128},{192,224},{224,1... | collective-permute-start | bytes 393224 | tf_op jit(solution)/shard_map/ppermute | solution.py:487
  72.3 2.0 %collective-permute-start.8 = (bf16[32,64,128]{2,1,0:T(8,128)(2,1)S(1)}, bf16[32,64,128]{2,1,0:T(8,128)(2,1)S(1)}, u32[]{:S(2)}, u32[]{:S(2)}) collective-permute-start(bf16[32,64,128]{2,1,0:T(8,128)(2,1)S(1)} %get-tuple-element.49), channel_id=1, source_target_pairs={{0,32},{32,0},{64,96},{96,64},{128,160},{160,128},{192,224},{224,1... | collective-permute-start | bytes 1572872 | tf_op jit(solution)/shard_map/ppermute | solution.py:487
  101.2 4.9 %collective-permute-start.11 = (f32[64,128]{1,0:T(8,128)S(1)}, f32[64,128]{1,0:T(8,128)S(1)}, u32[]{:S(2)}, u32[]{:S(2)}) collective-permute-start(f32[64,128]{1,0:T(8,128)S(1)} %shard_map.203.refs_0_), channel_id=1, source_target_pairs={{0,192},{32,224},{64,0},{96,32},{128,64},{160,96},{192,128},{224,1... | collective-permute-start | bytes 98312 | tf_op jit(solution)/shard_map/ppermute | solution.py:493
  104.1 4.4 %collective-permute-start.10 = (f32[64,128]{1,0:T(8,128)S(1)}, f32[64,128]{1,0:T(8,128)S(1)}, u32[]{:S(2)}, u32[]{:S(2)}) collective-permute-start(f32[64,128]{1,0:T(8,128)S(1)} %shard_map.203.refs_0_), channel_id=1, source_target_pairs={{0,128},{32,160},{64,192},{96,224},{128,0},{160,32},{192,64},{224,... | collective-permute-start | bytes 98312 | tf_op jit(solution)/shard_map/ppermute | solution.py:493
  104.3 4.3 %collective-permute-start.9 = (f32[64,128]{1,0:T(8,128)S(1)}, f32[64,128]{1,0:T(8,128)S(1)}, u32[]{:S(2)}, u32[]{:S(2)}) collective-permute-start(f32[64,128]{1,0:T(8,128)S(1)} %shard_map.203.refs_0_), channel_id=1, source_target_pairs={{0,64},{32,96},{64,128},{96,160},{128,192},{160,224},{192,0},{224,... | collective-permute-start | bytes 98312 | tf_op jit(solution)/shard_map/ppermute | solution.py:493
  126.8 6.8 %collective-permute-start.12 = (bf16[32,40,128]{2,1,0:T(8,128)(2,1)S(1)}, bf16[32,40,128]{2,1,0:T(8,128)(2,1)S(1)}, u32[]{:S(2)}, u32[]{:S(2)}) collective-permute-start(bf16[32,40,128]{2,1,0:T(8,128)(2,1)S(1)} %all_to_all.23.mine_ref), channel_id=1, source_target_pairs={{0,32},{32,0},{64,96},{96,64},{128,160},{160,128},{192,224},{224,1... | collective-permute-start | bytes 983048 | tf_op jit(solution)/shard_map/ppermute | solution.py:487

commit v6 on v4

--- a/solution.py
+++ b/solution.py
@@ -408,9 +408,8 @@
 
 def sum_chips(*refs):
     sum_refs, out_ref, hub_ref = refs[:CHIPS], refs[-2], refs[-1]
-    piece = sum_refs[0][HUB_PACKED:SUM_ROWS, :]
-    for sum_ref in sum_refs[1:]:
-        piece += sum_ref[HUB_PACKED:SUM_ROWS, :]
+    parts = [sum_ref[HUB_PACKED:SUM_ROWS, :] for sum_ref in sum_refs]
+    piece = (parts[0] + parts[2]) + (parts[1] + parts[3])
     hubs = jnp.zeros((8, 2 * TILE), F32)
     for shift, sum_ref in enumerate(sum_refs):
         i = (CHIPS - shift) % CHIPS
@@ -435,23 +434,30 @@
     out_ref[...] = base_ref[...] + tn(owner, high) + tn(owner, low)
 
 
-def weight_outputs(samples_all, mine_ref, theirs_ref, first_self_ref, first_mean_ref, self_ref, mean_ref, loss_ref, stack_ref):
+def weight_outputs(samples_all, mine_ref, theirs_ref, first_self_ref, first_mean_ref, self_ref, mean_ref, loss_ref):
     unused, core = position()
     half = STACK_ROWS // CORES
+    classes = self_ref.shape[0]
+    spans = (
+        (0, TILE, first_self_ref),
+        (TILE, 2 * TILE, first_mean_ref),
+        (SELF_AT, SELF_AT + classes, self_ref),
+        (MEAN_AT, MEAN_AT + classes, mean_ref),
+    )
     for n in range(PEERS):
         mine = mine_ref[n].astype(F32)
         theirs = theirs_ref[n].astype(F32)
         lanes = slice(TILE * (n // 8), TILE * (n // 8 + 1))
-        at = PIECE * (n % 8)
-        stack_ref[at : at + PIECE, lanes] = jnp.where(core == 0, mine, theirs)
-        stack_ref[half + at : half + at + PIECE, lanes] = jnp.where(core == 0, theirs, mine)
-    classes = self_ref.shape[0]
-    first_self_ref[...] = stack_ref[0:TILE, :]
-    first_mean_ref[...] = stack_ref[TILE : 2 * TILE, :]
-    self_ref[...] = stack_ref[SELF_AT : SELF_AT + classes, :]
-    mean_ref[...] = stack_ref[MEAN_AT : MEAN_AT + classes, :]
-    parts = stack_ref[LOSS_AT : LOSS_AT + 8, 0:1]
-    loss_ref[...] = (parts[0:1] + parts[1:2] + parts[2:3]) / samples_all
+        for at, piece in (
+            (PIECE * (n % 8), jnp.where(core == 0, mine, theirs)),
+            (half + PIECE * (n % 8), jnp.where(core == 0, theirs, mine)),
+        ):
+            for start, end, out_ref in spans:
+                low, high = max(start, at), min(end, at + PIECE)
+                if low < high:
+                    out_ref[low - start : high - start, lanes] = piece[low - at : high - at]
+            if at == LOSS_AT and lanes.start == 0:
+                loss_ref[...] = (piece[0:1, 0:1] + piece[1:2, 0:1] + piece[2:3, 0:1]) / samples_all
 
 
 def shape(dims, dtype):
@@ -656,7 +662,6 @@
             shape((classes, width), F32),
             shape((1, 1), F32),
         ),
-        [pltpu.VMEM((STACK_ROWS, width), F32)],
     )(pieces, to_core(pieces))
     return hidden, grad_hidden, loss[0, 0], first_self_sum, first_mean_sum, self_sum.T, mean_sum.T
 

time: 133 us -> 133 us (level)
  no operation moved by 1% of the time
where the time goes in v6:
time: 133 us
  blocking collectives  81.8 us (62%)
  starting transfers between devices  24.6 us (18%)
  Pallas kernels  18.6 us (14%)
  waiting for transfers between devices  6.62 us (5%)
  between operations  1.41 us (1%)
    all_to_all x4, blocking collectives, swap(): lax.all_to_all(values, 'dev', split_axis=0, concat_axis=0, tiled=True)  81.8 us
    ppermute x4, starting transfers between devices, to_core(): lax.ppermute(values, 'grp', [(i, i ^ 1) for i in range(CHIPS * CORES)])  16.4 us
    ppermute x9, starting transfers between devices, to_chips(): lax.ppermute(values, 'grp', [(i, (i + CORES * shift) % every) for i in ra...  8.17 us
    pallas_call x1, Pallas kernels, on_device(): kernel_call(functools.partial(main_part, samples_all, classes), (shape((n...  5.32 us
    ppermute x9, waiting for transfers between devices, to_chips(): lax.ppermute(values, 'grp', [(i, (i + CORES * shift) % every) for i in ra...  4.71 us
    pallas_call x1, Pallas kernels, on_device(): kernel_call(build_dense, (shape((nodes, table), BF16), shape((nodes, TILE...  3.01 us
  transfers between devices with their start and end apart: 13, of which 8 were waited for; matrix products, arithmetic and copies ran while one was open for 0% of the time, Pallas kernels for 7%

profile of v6, /device:TPU:1, one launch (start us, length us, event | category | flops | bytes accessed | tf_op | source)
XLA Modules:
  0.0 133.0 jit_solution(4882546368595790124)
XLA Ops:
  0.6 1.7 %shard_map.189 = bf16[1280,128]{1,0:T(8,128)(2,1)S(1)} custom-call(bf16[512,128]{1,0:T(8,128)(2,1)} %features_ref.3, s32[1,32,32]{2,1,0:T(8,128)} %send_any.1, s32[1,32]{1,0:T(1,128)} %refs_5_.1, s32[1,4]{1,0:T(1,128)} %refs_6_.1), custom_call_target="tpu_custom_call" | custom-call | tf_op jit(solution)/shard_map/pallas_call | solution.py:518
  2.4 22.0 %all_to_all.20.refs_13_.arrived_ref.feature_arrived_ref = bf16[32,40,128]{2,1,0:T(8,128)(2,1)S(1)} all-to-all(bf16[32,40,128]{2,1,0:T(8,128)(2,1)S(1)} %bitcast.9), channel_id=1, replica_groups=mesh['grp'=8,'dev'=32] {'dev'}, dimensions={0} | all-to-all | bytes 655360 | tf_op jit(solution)/shard_map/all_to_all | solution.py:468
  24.4 2.6 %collective-permute-start.2 = (bf16[128,128]{1,0:T(8,128)(2,1)S(1)}, bf16[128,128]{1,0:T(8,128)(2,1)S(1)}, u32[]{:S(2)}, u32[]{:S(2)}) collective-permute-start(bf16[128,128]{1,0:T(8,128)(2,1)S(1)} %shard_map.191.refs_0_), channel_id=1, source_target_pairs={{0,192},{32,224},{64,0},{96,32},{128,64},{160,96},{192,128},{224,1... | collective-permute-start | bytes 98312 | tf_op jit(solution)/shard_map/ppermute | solution.py:478
  28.7 3.0 %shard_map.190 = (bf16[512,2560]{1,0:T(8,128)(2,1)S(1)}, f32[512,128]{1,0:T(8,128)S(1)}, bf16[768,512]{1,0:T(8,128)(2,1)S(1)}, s32[40,32]{1,0:T(8,128)S(1)}, bf16[1280,512]{1,0:T(8,128)(2,1)S(1)}) custom-call(bf16[32,128,128]{2,1,0:T(8,128)(2,1)} %refs_0_.1, s32[1,32]{1,0:T(1,128)} %refs_1_.1, s32[1,32]{1,0:T(1,128)} %refs_2_.1, s32[1]{0:T(128)S(6)} %copy.21.refs_3_, ...), custom_call_target="tpu_custom_call" | custom-call | flops 335544320 | bytes 8388608 | tf_op jit(solution)/shard_map/pallas_call | solution.py:537
  31.8 5.8 %collective-permute-start.3 = (bf16[512,128]{1,0:T(8,128)(2,1)S(1)}, bf16[512,128]{1,0:T(8,128)(2,1)S(1)}, u32[]{:S(2)}, u32[]{:S(2)}) collective-permute-start(bf16[512,128]{1,0:T(8,128)(2,1)S(1)} %shard_map.192.own_hub_ref.feature_ref), channel_id=1, source_target_pairs={{0,32},{32,0},{64,96},{96,64},{128,160},{160,128},{192,224},{224,1... | collective-permute-start | bytes 393224 | tf_op jit(solution)/shard_map/ppermute | solution.py:472
  37.6 0.9 shard_map.193.part_ref
  38.6 1.0 shard_map.194
  39.6 14.7 %all_to_all.21.arrived_ref = bf16[32,40,128]{2,1,0:T(8,128)(2,1)S(1)} all-to-all(bf16[32,40,128]{2,1,0:T(8,128)(2,1)S(1)} %bitcast.10), channel_id=1, replica_groups=mesh['grp'=8,'dev'=32] {'dev'}, dimensions={0} | all-to-all | bytes 655360 | tf_op jit(solution)/shard_map/all_to_all | solution.py:468
  54.3 1.6 %collective-permute-start.6 = (bf16[128,128]{1,0:T(8,128)(2,1)S(1)}, bf16[128,128]{1,0:T(8,128)(2,1)S(1)}, u32[]{:S(2)}, u32[]{:S(2)}) collective-permute-start(bf16[128,128]{1,0:T(8,128)(2,1)S(1)} %shard_map.196.refs_0_), channel_id=1, source_target_pairs={{0,192},{32,224},{64,0},{96,32},{128,64},{160,96},{192,128},{224,1... | collective-permute-start | bytes 98312 | tf_op jit(solution)/shard_map/ppermute | solution.py:478
  55.9 1.3 collective-permute-start.5
  57.2 1.6 %shard_map.195 = (bf16[512,512]{1,0:T(8,128)(2,1)}, bf16[256,1536]{1,0:T(8,128)(2,1)S(1)}, bf16[1536,512]{1,0:T(8,128)(2,1)S(1)}, f32[512,512]{1,0:T(8,128)S(1)}, f32[512,256]{1,0:T(8,128)S(1)}) custom-call(bf16[512,128]{1,0:T(8,128)(2,1)S(1)} %copy-done, bf16[32,40,128]{2,1,0:T(8,128)(2,1)S(1)} %all_to_all.20.refs_13_.arrived_ref.feature_arrived_ref, ...), custom_call_target="tpu_custom_call" | custom-call | flops 1610612736 | bytes 8388608 | tf_op jit(solution)/shard_map/pallas_call | solution.py:583
  58.8 1.3 %collective-permute-done.5.refs_2_ = bf16[128,128]{1,0:T(8,128)(2,1)S(1)} collective-permute-done((bf16[128,128]{1,0:T(8,128)(2,1)S(1)}, bf16[128,128]{1,0:T(8,128)(2,1)S(1)}, u32[]{:S(2)}, u32[]{:S(2)}) %collective-permute-start.5) | collective-permute-done | bytes 32800 | tf_op jit(solution)/shard_map/ppermute | solution.py:478
  60.2 1.0 collective-permute-done.4.refs_1_
  61.2 5.8 %collective-permute-start.7 = (bf16[512,128]{1,0:T(8,128)(2,1)S(1)}, bf16[512,128]{1,0:T(8,128)(2,1)S(1)}, u32[]{:S(2)}, u32[]{:S(2)}) collective-permute-start(bf16[512,128]{1,0:T(8,128)(2,1)S(1)} %shard_map.197.mean_ref), channel_id=1, source_target_pairs={{0,32},{32,0},{64,96},{96,64},{128,160},{160,128},{192,224},{224,1... | collective-permute-start | bytes 393224 | tf_op jit(solution)/shard_map/ppermute | solution.py:472
  68.0 5.3 %shard_map.199 = (f32[512,512]{1,0:T(8,128)S(1)}, bf16[32,48,128]{2,1,0:T(8,128)(2,1)S(1)}, bf16[32,64,128]{2,1,0:T(8,128)(2,1)S(1)}, bf16[32,64,128]{2,1,0:T(8,128)(2,1)S(1)}) custom-call(bf16[256,1536]{1,0:T(8,128)(2,1)S(1)} %get-tuple-element.41.early_turned_ref, bf16[1536,512]{1,0:T(8,128)(2,1)S(1)} %get-tuple-element.42.early_source_ref, ...), custom_call_target="tpu_custom_call" | custom-call | tf_op jit(solution)/shard_map/pallas_call | solution.py:611
  73.8 1.5 %collective-permute-done.8.arrived_ref = bf16[32,64,128]{2,1,0:T(8,128)(2,1)S(1)} collective-permute-done((bf16[32,64,128]{2,1,0:T(8,128)(2,1)S(1)}, bf16[32,64,128]{2,1,0:T(8,128)(2,1)S(1)}, u32[]{:S(2)}, u32[]{:S(2)}) %collective-permute-start.8) | collective-permute-done | bytes 524320 | tf_op jit(solution)/shard_map/ppermute | solution.py:472
  75.5 26.7 %all_to_all.22.arrived_ref = bf16[32,112,128]{2,1,0:T(8,128)(2,1)S(1)} all-to-all(bf16[32,112,128]{2,1,0:T(8,128)(2,1)S(1)} %shard_map.200), channel_id=1, replica_groups=mesh['grp'=8,'dev'=32] {'dev'}, dimensions={0} | all-to-all | bytes 1835008 | tf_op jit(solution)/shard_map/all_to_all | solution.py:468
  103.0 0.8 collective-permute-start.9
  103.8 1.3 %shard_map.201.refs_4_.base_ref = f32[512,512]{1,0:T(8,128)S(1)} custom-call(f32[512,512]{1,0:T(8,128)S(1)} %get-tuple-element.49.base_ref, bf16[32,112,128]{2,1,0:T(8,128)(2,1)S(1)} %all_to_all.22.arrived_ref, s32[40,32]{1,0:T(8,128)S(1)} %get-tuple-element.53.wanted_ref, bf16[768,512]{1,0:T(8,128)(2,1)S(1)} %get-tuple-element.39.weights_ref), custom_call_target="tpu_custom_call" | custom-call | flops 402653184 | bytes 4194304 | tf_op jit(solution)/shard_map/pallas_call | solution.py:636
  105.4 1.3 collective-permute-done.10.refs_2_
  107.6 18.4 %all_to_all.23.mine_ref = bf16[32,40,128]{2,1,0:T(8,128)(2,1)S(1)} all-to-all(bf16[32,40,128]{2,1,0:T(8,128)(2,1)S(1)} %get-tuple-element.55), channel_id=1, replica_groups=mesh['grp'=8,'dev'=32] {'dev'}, dimensions={0} | all-to-all | bytes 655360 | tf_op jit(solution)/shard_map/all_to_all | solution.py:468
  126.0 4.4 %collective-permute-start.12 = (bf16[32,40,128]{2,1,0:T(8,128)(2,1)S(1)}, bf16[32,40,128]{2,1,0:T(8,128)(2,1)S(1)}, u32[]{:S(2)}, u32[]{:S(2)}) collective-permute-start(bf16[32,40,128]{2,1,0:T(8,128)(2,1)S(1)} %all_to_all.23.mine_ref), channel_id=1, source_target_pairs={{0,32},{32,0},{64,96},{96,64},{128,160},{160,128},{192,224},{224,1... | collective-permute-start | bytes 983048 | tf_op jit(solution)/shard_map/ppermute | solution.py:472
  130.3 1.5 %shard_map.204 = f32[512,512]{1,0:T(8,128)} custom-call(f32[512,512]{1,0:T(8,128)S(1)} %shard_map.201.refs_4_.base_ref, f32[8,256]{1,0:T(8,128)S(1)} %get-tuple-element.54.hub_ref, s32[40,32]{1,0:T(8,128)S(1)} %get-tuple-element.53.wanted_ref, bf16[768,512]{1,0:T(8,128)(2,1)S(1)} %get-tuple-element.39.weights_ref), custom_call_target="tpu_custom_call" | custom-call | flops 268435456 | bytes 4194304 | tf_op jit(solution)/shard_map/pallas_call | solution.py:650
  131.9 1.1 shard_map.205
  (25 shorter events, 4.7 us)
Async XLA Ops:
  24.4 13.2 %copy-start = (bf16[512,128]{1,0:T(8,128)(2,1)S(1)}, bf16[512,128]{1,0:T(8,128)(2,1)}, u32[]{:S(2)}) copy-start(bf16[512,128]{1,0:T(8,128)(2,1)} %features_ref.3) | copy-start | bytes 393220
  24.4 7.4 %collective-permute-start.2 = (bf16[128,128]{1,0:T(8,128)(2,1)S(1)}, bf16[128,128]{1,0:T(8,128)(2,1)S(1)}, u32[]{:S(2)}, u32[]{:S(2)}) collective-permute-start(bf16[128,128]{1,0:T(8,128)(2,1)S(1)} %shard_map.191.refs_0_), channel_id=1, source_target_pairs={{0,192},{32,224},{64,0},{96,32},{128,64},{160,96},{192,128},{224,1... | collective-permute-start | bytes 98312 | tf_op jit(solution)/shard_map/ppermute | solution.py:478
  27.0 4.8 %collective-permute-start.1 = (bf16[128,128]{1,0:T(8,128)(2,1)S(1)}, bf16[128,128]{1,0:T(8,128)(2,1)S(1)}, u32[]{:S(2)}, u32[]{:S(2)}) collective-permute-start(bf16[128,128]{1,0:T(8,128)(2,1)S(1)} %shard_map.191.refs_0_), channel_id=1, source_target_pairs={{0,128},{32,160},{64,192},{96,224},{128,0},{160,32},{192,64},{224,... | collective-permute-start | bytes 98312 | tf_op jit(solution)/shard_map/ppermute | solution.py:478
  27.5 4.3 %collective-permute-start = (bf16[128,128]{1,0:T(8,128)(2,1)S(1)}, bf16[128,128]{1,0:T(8,128)(2,1)S(1)}, u32[]{:S(2)}, u32[]{:S(2)}) collective-permute-start(bf16[128,128]{1,0:T(8,128)(2,1)S(1)} %shard_map.191.refs_0_), channel_id=1, source_target_pairs={{0,64},{32,96},{64,128},{96,160},{128,192},{160,224},{192,0},{224,... | collective-permute-start | bytes 98312 | tf_op jit(solution)/shard_map/ppermute | solution.py:478
  31.8 6.8 %collective-permute-start.3 = (bf16[512,128]{1,0:T(8,128)(2,1)S(1)}, bf16[512,128]{1,0:T(8,128)(2,1)S(1)}, u32[]{:S(2)}, u32[]{:S(2)}) collective-permute-start(bf16[512,128]{1,0:T(8,128)(2,1)S(1)} %shard_map.192.own_hub_ref.feature_ref), channel_id=1, source_target_pairs={{0,32},{32,0},{64,96},{96,64},{128,160},{160,128},{192,224},{224,1... | collective-permute-start | bytes 393224 | tf_op jit(solution)/shard_map/ppermute | solution.py:472
  54.3 4.6 %collective-permute-start.6 = (bf16[128,128]{1,0:T(8,128)(2,1)S(1)}, bf16[128,128]{1,0:T(8,128)(2,1)S(1)}, u32[]{:S(2)}, u32[]{:S(2)}) collective-permute-start(bf16[128,128]{1,0:T(8,128)(2,1)S(1)} %shard_map.196.refs_0_), channel_id=1, source_target_pairs={{0,192},{32,224},{64,0},{96,32},{128,64},{160,96},{192,128},{224,1... | collective-permute-start | bytes 98312 | tf_op jit(solution)/shard_map/ppermute | solution.py:478
  55.9 4.3 %collective-permute-start.5 = (bf16[128,128]{1,0:T(8,128)(2,1)S(1)}, bf16[128,128]{1,0:T(8,128)(2,1)S(1)}, u32[]{:S(2)}, u32[]{:S(2)}) collective-permute-start(bf16[128,128]{1,0:T(8,128)(2,1)S(1)} %shard_map.196.refs_0_), channel_id=1, source_target_pairs={{0,128},{32,160},{64,192},{96,224},{128,0},{160,32},{192,64},{224,... | collective-permute-start | bytes 98312 | tf_op jit(solution)/shard_map/ppermute | solution.py:478
  57.2 4.0 %collective-permute-start.4 = (bf16[128,128]{1,0:T(8,128)(2,1)S(1)}, bf16[128,128]{1,0:T(8,128)(2,1)S(1)}, u32[]{:S(2)}, u32[]{:S(2)}) collective-permute-start(bf16[128,128]{1,0:T(8,128)(2,1)S(1)} %shard_map.196.refs_0_), channel_id=1, source_target_pairs={{0,64},{32,96},{64,128},{96,160},{128,192},{160,224},{192,0},{224,... | collective-permute-start | bytes 98312 | tf_op jit(solution)/shard_map/ppermute | solution.py:478
  61.2 6.8 %collective-permute-start.7 = (bf16[512,128]{1,0:T(8,128)(2,1)S(1)}, bf16[512,128]{1,0:T(8,128)(2,1)S(1)}, u32[]{:S(2)}, u32[]{:S(2)}) collective-permute-start(bf16[512,128]{1,0:T(8,128)(2,1)S(1)} %shard_map.197.mean_ref), channel_id=1, source_target_pairs={{0,32},{32,0},{64,96},{96,64},{128,160},{160,128},{192,224},{224,1... | collective-permute-start | bytes 393224 | tf_op jit(solution)/shard_map/ppermute | solution.py:472
  73.3 2.0 %collective-permute-start.8 = (bf16[32,64,128]{2,1,0:T(8,128)(2,1)S(1)}, bf16[32,64,128]{2,1,0:T(8,128)(2,1)S(1)}, u32[]{:S(2)}, u32[]{:S(2)}) collective-permute-start(bf16[32,64,128]{2,1,0:T(8,128)(2,1)S(1)} %get-tuple-element.51), channel_id=1, source_target_pairs={{0,32},{32,0},{64,96},{96,64},{128,160},{160,128},{192,224},{224,1... | collective-permute-start | bytes 1572872 | tf_op jit(solution)/shard_map/ppermute | solution.py:472
  102.3 3.1 %collective-permute-start.11 = (f32[64,128]{1,0:T(8,128)S(1)}, f32[64,128]{1,0:T(8,128)S(1)}, u32[]{:S(2)}, u32[]{:S(2)}) collective-permute-start(f32[64,128]{1,0:T(8,128)S(1)} %shard_map.202.refs_0_), channel_id=1, source_target_pairs={{0,192},{32,224},{64,0},{96,32},{128,64},{160,96},{192,128},{224,1... | collective-permute-start | bytes 98312 | tf_op jit(solution)/shard_map/ppermute | solution.py:478
  102.4 4.4 %collective-permute-start.10 = (f32[64,128]{1,0:T(8,128)S(1)}, f32[64,128]{1,0:T(8,128)S(1)}, u32[]{:S(2)}, u32[]{:S(2)}) collective-permute-start(f32[64,128]{1,0:T(8,128)S(1)} %shard_map.202.refs_0_), channel_id=1, source_target_pairs={{0,128},{32,160},{64,192},{96,224},{128,0},{160,32},{192,64},{224,... | collective-permute-start | bytes 98312 | tf_op jit(solution)/shard_map/ppermute | solution.py:478
  103.0 4.5 %collective-permute-start.9 = (f32[64,128]{1,0:T(8,128)S(1)}, f32[64,128]{1,0:T(8,128)S(1)}, u32[]{:S(2)}, u32[]{:S(2)}) collective-permute-start(f32[64,128]{1,0:T(8,128)S(1)} %shard_map.202.refs_0_), channel_id=1, source_target_pairs={{0,64},{32,96},{64,128},{96,160},{128,192},{160,224},{192,0},{224,... | collective-permute-start | bytes 98312 | tf_op jit(solution)/shard_map/ppermute | solution.py:478
  126.0 5.9 %collective-permute-start.12 = (bf16[32,40,128]{2,1,0:T(8,128)(2,1)S(1)}, bf16[32,40,128]{2,1,0:T(8,128)(2,1)S(1)}, u32[]{:S(2)}, u32[]{:S(2)}) collective-permute-start(bf16[32,40,128]{2,1,0:T(8,128)(2,1)S(1)} %all_to_all.23.mine_ref), channel_id=1, source_target_pairs={{0,32},{32,0},{64,96},{96,64},{128,160},{160,128},{192,224},{224,1... | collective-permute-start | bytes 983048 | tf_op jit(solution)/shard_map/ppermute | solution.py:472

commit v7 on v6

--- a/solution.py
+++ b/solution.py
@@ -22,16 +22,18 @@
 FORWARD_ROWS = CAPACITY + 8
 PEER_HUBS = CORES * CHIPS * HUBS_EACH
 EDGE_ROWS = CAPACITY + CAPACITY // 2
-HUB_ROWS = CHIPS * HUBS_EACH
-HUB_PACKED = HUB_ROWS + HUB_ROWS // 2
+HUB_ROWS = 2 * HUBS_EACH
+CHIP_HUBS = PEERS * HUB_ROWS
 STACK_ROWS = 640
 SELF_AT = 256
 LOSS_AT = 440
 MEAN_AT = 448
 CLASS_ROWS = 176
 PIECE = STACK_ROWS // CORES * 4 // PEERS
-SUM_ROWS = HUB_PACKED + PIECE
-BACK_ROWS = EDGE_ROWS + SUM_ROWS
+BACK_ROWS = EDGE_ROWS + PIECE
+CORE_ROWS = CHIPS * CHIP_HUBS + PEERS * PIECE
+CHIP_ROWS = CHIP_HUBS + 2 * PIECE
+LAST_ROWS = HUB_ROWS + PIECE
 
 VM = pl.BlockSpec(memory_space=pltpu.VMEM)
 SM = pl.BlockSpec(memory_space=pltpu.SMEM)
@@ -280,7 +282,7 @@
     early_turned_ref, early_source_ref, logits_ref, own_turned_ref, own_source_ref, own_columns_ref, part_ref,
     dense_ref, numbers_ref, weights_ref, feature_ref, mean_ref,
     base_ref, edge_ref, mine_ref, theirs_ref,
-    other_turned_ref, other_source_ref, other_columns_ref, scaled_ref, masked_ref, stack_ref, rest_ref,
+    other_turned_ref, other_source_ref, other_columns_ref, scaled_ref, masked_ref, stack_ref,
 ):
     nodes, width = base_ref.shape
     padded = SELF_AT
@@ -319,7 +321,7 @@
     def mask(at, source, grad):
         masked_ref[at : at + nodes, :] = jnp.where(source > 0, grad, 0.0).astype(BF16)
 
-    low = iota((8, padded), 0) < HUBS_EACH
+    low = iota((8, TILE), 0) < HUBS_EACH
     hub_at = nodes + PEERS * CAPACITY
     for i, (columns_ref, source_ref, out_ref) in enumerate(
         ((own_columns_ref, own_source_ref, mine_ref), (other_columns_ref, other_source_ref, theirs_ref))
@@ -327,18 +329,17 @@
         found, spread = back(columns_ref[...])
         mask(hub_at + i * nodes, source_ref[...], spread)
         found = found.astype(F32)
-        for n in range(0, PEERS, 2):
-            first, second = [], []
-            for pair in range(CHIPS // 2):
-                at = 2 * pair * GROUP_HUBS + n * HUBS_EACH
-                even = found[at : at + 8]
-                odd = found[at + GROUP_HUBS : at + GROUP_HUBS + 8]
-                first.append(jnp.where(low, even, pltpu.roll(odd, HUBS_EACH, 0)))
-                second.append(jnp.where(low, pltpu.roll(even, HUBS_EACH, 0), odd))
-            for member, blocks in ((n, first), (n + 1, second)):
-                rows = jnp.concatenate([block[:, 0:TILE] for block in blocks], axis=0)
-                out_ref[member, 0:HUB_ROWS, :] = rows.astype(BF16)
-                rest_ref[i, member] = join_rests(blocks[0][:, TILE:], blocks[1][:, TILE:])
+        for block in range(CHIPS):
+            for n in range(0, PEERS, 2):
+                at = block * GROUP_HUBS + n * HUBS_EACH
+                mains = found[at : at + 8, 0:TILE]
+                rests = found[at : at + 8, TILE:]
+                pair = (
+                    jnp.where(low, mains, pltpu.roll(rests, HUBS_EACH, 0)),
+                    jnp.where(low, pltpu.roll(mains, HUBS_EACH, 0), rests),
+                )
+                at = block * CHIP_HUBS + n * HUB_ROWS
+                out_ref[at : at + 2 * HUB_ROWS, :] = jnp.concatenate(pair, axis=0).astype(BF16)
 
     unused, spread = back(dense_ref[:, 0:nodes])
     base = nn(upstream, weights_ref[self_rows, :]) + spread
@@ -371,26 +372,37 @@
         + nn(other_turned_ref[...], masked_ref[hub_at + nodes :, :])
     )
     unused, core = position()
-    for i, (there, out_ref) in enumerate(((core, mine_ref), (1 - core, theirs_ref))):
-        for n in range(PEERS):
+    for there, out_ref in ((core, mine_ref), (1 - core, theirs_ref)):
+        for n in range(0, PEERS, 2):
             at = there * (STACK_ROWS // CORES) + PIECE * (n % 8)
             lanes = slice(TILE * (n // 8), TILE * (n // 8 + 1))
-            piece = stack_ref[pl.ds(pl.multiple_of(at, 8), PIECE), lanes]
-            rows = jnp.concatenate([rest_ref[i, n], piece], axis=0)
-            out_ref[n, HUB_ROWS:SUM_ROWS, :] = rows.astype(BF16)
-
-
-def sum_cores(mine_ref, arrived_ref, edge_ref, out_ref):
+            rows = stack_ref[pl.ds(pl.multiple_of(at, 16), 2 * PIECE), lanes]
+            at = CHIPS * CHIP_HUBS + n * PIECE
+            out_ref[at : at + 2 * PIECE, :] = rows.astype(BF16)
+
+
+def sum_cores(mine_ref, arrived_ref, edge_ref, out_ref, *hub_refs):
     out_ref[:, 0:EDGE_ROWS, :] = edge_ref[...]
     total = mine_ref[...].astype(F32) + arrived_ref[...].astype(F32)
-    out_ref[:, EDGE_ROWS:BACK_ROWS, :] = total.astype(BF16)
-
-
-def sum_peers(arrived_ref, out_ref):
+    for block, hub_ref in enumerate(hub_refs):
+        hub_ref[...] = total[block * CHIP_HUBS : (block + 1) * CHIP_HUBS].astype(BF16)
+    for n in range(PEERS):
+        at = CHIPS * CHIP_HUBS + n * PIECE
+        out_ref[n, EDGE_ROWS:BACK_ROWS, :] = total[at : at + PIECE].astype(BF16)
+
+
+def sum_peers(arrived_ref, *refs):
+    hub_refs, (sum_ref, *out_refs) = refs[: CHIPS - 1], refs[CHIPS - 1 :]
     total = arrived_ref[0, EDGE_ROWS:BACK_ROWS, :].astype(F32)
     for n in range(1, PEERS):
         total += arrived_ref[n, EDGE_ROWS:BACK_ROWS, :].astype(F32)
-    out_ref[...] = total
+    high = total.astype(BF16).astype(F32)
+    low = (total - high).astype(BF16).astype(F32)
+    sum_ref[...] = high + low
+    parts = jnp.concatenate([high, low], axis=0).astype(BF16)
+    for hub_ref, out_ref in zip(hub_refs, out_refs):
+        out_ref[0:CHIP_HUBS, :] = hub_ref[...]
+        out_ref[CHIP_HUBS:CHIP_ROWS, :] = parts
 
 
 def return_edges(base_ref, arrived_ref, wanted_ref, weights_ref, out_ref, found_ref, pick_ref):
@@ -406,31 +418,36 @@
     out_ref[...] = base_ref[...] + nn(rows.astype(BF16), weights_ref[2 * SELF_AT :, :])
 
 
-def sum_chips(*refs):
-    sum_refs, out_ref, hub_ref = refs[:CHIPS], refs[-2], refs[-1]
-    parts = [sum_ref[HUB_PACKED:SUM_ROWS, :] for sum_ref in sum_refs]
-    piece = (parts[0] + parts[2]) + (parts[1] + parts[3])
-    hubs = jnp.zeros((8, 2 * TILE), F32)
-    for shift, sum_ref in enumerate(sum_refs):
-        i = (CHIPS - shift) % CHIPS
-        main = sum_ref[8 * (i // 2) : 8 * (i // 2) + 8, :]
-        rest = part_rests(sum_ref[HUB_ROWS:HUB_PACKED, :])[i // 2]
-        rows = jnp.concatenate([main, rest], axis=1)
-        hubs += pltpu.roll(rows, HUBS_EACH, 0) if i % 2 else rows
-    hub_ref[...] = hubs
+def sum_chips(sum_ref, own_ref, *refs):
+    sent_refs, out_ref = refs[: CHIPS - 1], refs[-1]
+    hubs = own_ref[...].astype(F32)
+    pieces = [sum_ref[...]]
+    for sent_ref in sent_refs:
+        rows = sent_ref[...].astype(F32)
+        hubs += rows[0:CHIP_HUBS]
+        pieces.append(rows[CHIP_HUBS : CHIP_HUBS + PIECE] + rows[CHIP_HUBS + PIECE : CHIP_ROWS])
+    piece = (pieces[0] + pieces[2]) + (pieces[1] + pieces[3])
     unused, core = position()
     holder = (core == LOSS_AT * CORES // STACK_ROWS) & (lax.axis_index("dev") == LOSS_AT % (STACK_ROWS // CORES) // PIECE)
     rest = piece[0:1] - piece[0:1].astype(BF16).astype(F32)
     row = iota(piece.shape, 0)
-    piece = jnp.where((row == 2) & holder, rest, piece).astype(BF16)
+    piece = jnp.where((row == 2) & holder, rest, piece)
+    tail = piece[8:PIECE].astype(BF16)
     for n in range(PEERS):
-        out_ref[n] = piece
-
-
-def return_hubs(base_ref, hub_ref, wanted_ref, weights_ref, out_ref):
+        head = jnp.concatenate([hubs[n * HUB_ROWS : (n + 1) * HUB_ROWS], piece[0:8]], axis=0)
+        out_ref[n, 0:16, :] = head.astype(BF16)
+        out_ref[n, 16:LAST_ROWS, :] = tail
+
+
+def return_hubs(base_ref, arrived_ref, wanted_ref, weights_ref, out_ref):
     nodes = out_ref.shape[0]
-    high, low = split(nn(hub_ref[...].astype(BF16), weights_ref[2 * SELF_AT :, :]))
-    owner = one_hot(wanted_ref[CAPACITY:FORWARD_ROWS, 0:1] == iota((8, nodes), 1))
+    hubs = arrived_ref[0, 0:16, :].astype(F32)
+    for n in range(1, PEERS):
+        hubs += arrived_ref[n, 0:16, :].astype(F32)
+    hubs = hubs[0:HUB_ROWS]
+    hubs = jnp.concatenate([hubs, pltpu.roll(hubs, HUBS_EACH, 0)], axis=1)
+    high, low = split(nn(hubs.astype(BF16), weights_ref[2 * SELF_AT :, :]))
+    owner = one_hot(wanted_ref[CAPACITY:FORWARD_ROWS, 0:1] == iota((HUB_ROWS, nodes), 1))
     out_ref[...] = base_ref[...] + tn(owner, high) + tn(owner, low)
 
 
@@ -445,8 +462,8 @@
         (MEAN_AT, MEAN_AT + classes, mean_ref),
     )
     for n in range(PEERS):
-        mine = mine_ref[n].astype(F32)
-        theirs = theirs_ref[n].astype(F32)
+        mine = mine_ref[n].astype(F32)[HUB_ROWS:]
+        theirs = theirs_ref[n].astype(F32)[HUB_ROWS:]
         lanes = slice(TILE * (n // 8), TILE * (n // 8 + 1))
         for at, piece in (
             (PIECE * (n % 8), jnp.where(core == 0, mine, theirs)),
@@ -472,12 +489,13 @@
     return lax.ppermute(values, "grp", [(i, i ^ 1) for i in range(CHIPS * CORES)])
 
 
+def along_x(values, shift):
+    every = CHIPS * CORES
+    return lax.ppermute(values, "grp", [(i, (i + CORES * shift) % every) for i in range(every)])
+
+
 def to_chips(values):
-    every = CHIPS * CORES
-    return [
-        lax.ppermute(values, "grp", [(i, (i + CORES * shift) % every) for i in range(every)])
-        for shift in range(1, CHIPS)
-    ]
+    return [along_x(values, shift) for shift in range(1, CHIPS)]
 
 
 def on_device(
@@ -613,8 +631,8 @@
         (
             shape((nodes, width), F32),
             shape((PEERS, EDGE_ROWS, TILE), BF16),
-            shape((PEERS, SUM_ROWS, TILE), BF16),
-            shape((PEERS, SUM_ROWS, TILE), BF16),
+            shape((CORE_ROWS, TILE), BF16),
+            shape((CORE_ROWS, TILE), BF16),
         ),
         [
             pltpu.VMEM((2 * inputs, half), BF16),
@@ -623,16 +641,20 @@
             pltpu.VMEM((padded, nodes), BF16),
             pltpu.VMEM((table, width), BF16),
             pltpu.VMEM((STACK_ROWS, width), F32),
-            pltpu.VMEM((CORES, PEERS, HUB_PACKED - HUB_ROWS, TILE), F32),
         ],
         limit=20,
     )(
         early_turned, early_source, own_logits, own_turned, own_source, own_columns, part,
         dense, numbers, weights, feature_hubs[1], mean_hubs[1],
     )
-    rows = kernel_call(sum_cores, shape((PEERS, BACK_ROWS, TILE), BF16))(mine, to_core(theirs), edge_rows)
+    rows, *blocks = kernel_call(
+        sum_cores, (shape((PEERS, BACK_ROWS, TILE), BF16),) + (shape((CHIP_HUBS, TILE), BF16),) * CHIPS
+    )(mine, to_core(theirs), edge_rows)
     arrived = swap(rows)
-    sums = kernel_call(sum_peers, shape((SUM_ROWS, TILE), F32))(arrived)
+    sums, *sent = kernel_call(
+        sum_peers, (shape((PIECE, TILE), F32),) + (shape((CHIP_ROWS, TILE), BF16),) * (CHIPS - 1)
+    )(arrived, *blocks[1:])
+    sent = [along_x(block, -1 - i) for i, block in enumerate(sent)]
     base = kernel_call(
         return_edges,
         shape((nodes, width), F32),
@@ -641,18 +663,18 @@
         flops=2 * nodes * (edges * padded + width * padded),
         moved=4 * MIB,
     )(base, arrived, wanted, weights)
-    pieces, own_hubs = kernel_call(
+    pieces = kernel_call(
         sum_chips,
-        (shape((PEERS, PIECE, TILE), BF16), shape((8, padded), F32)),
-        in_specs=[VM] * CHIPS + [ANY],
-    )(sums, *to_chips(sums), base)
+        shape((PEERS, LAST_ROWS, TILE), BF16),
+        in_specs=[VM] * (CHIPS + 1) + [ANY],
+    )(sums, blocks[0], *sent, base)
     pieces = swap(pieces)
     grad_hidden = kernel_call(
         return_hubs,
         shape((nodes, width), F32),
         flops=4 * nodes * padded * width,
         moved=4 * MIB,
-    )(base, own_hubs, wanted, weights)
+    )(base, pieces, wanted, weights)
     first_self_sum, first_mean_sum, self_sum, mean_sum, loss = kernel_call(
         functools.partial(weight_outputs, samples_all),
         (

time: 133 us -> 132 us (level)
  no operation moved by 1% of the time
where the time goes in v7:
time: 132 us
  blocking collectives  80.9 us (61%)
  starting transfers between devices  23.8 us (18%)
  Pallas kernels  18.6 us (14%)
  waiting for transfers between devices  7.39 us (6%)
  between operations  1.41 us (1%)
    all_to_all x4, blocking collectives, swap(): lax.all_to_all(values, 'dev', split_axis=0, concat_axis=0, tiled=True)  80.9 us
    ppermute x4, starting transfers between devices, to_core(): lax.ppermute(values, 'grp', [(i, i ^ 1) for i in range(CHIPS * CORES)])  15.8 us
    ppermute x9, starting transfers between devices, along_x(): lax.ppermute(values, 'grp', [(i, (i + CORES * shift) % every) for i in ra...  8.03 us
    ppermute x9, waiting for transfers between devices, along_x(): lax.ppermute(values, 'grp', [(i, (i + CORES * shift) % every) for i in ra...  5.39 us
    pallas_call x1, Pallas kernels, on_device(): kernel_call(functools.partial(main_part, samples_all, classes), (shape((n...  5.3 us
    pallas_call x1, Pallas kernels, on_device(): kernel_call(build_dense, (shape((nodes, table), BF16), shape((nodes, TILE...  3.08 us
  transfers between devices with their start and end apart: 13, of which 8 were waited for; matrix products, arithmetic and copies ran while one was open for 0% of the time, Pallas kernels for 7%

profile of v7, /device:TPU:1, one launch (start us, length us, event | category | flops | bytes accessed | tf_op | source)
XLA Modules:
  0.0 132.1 jit_solution(7502329231655968308)
XLA Ops:
  0.6 1.7 %shard_map.189 = bf16[1280,128]{1,0:T(8,128)(2,1)S(1)} custom-call(bf16[512,128]{1,0:T(8,128)(2,1)} %features_ref.3, s32[1,32,32]{2,1,0:T(8,128)} %send_any.1, s32[1,32]{1,0:T(1,128)} %refs_5_.1, s32[1,4]{1,0:T(1,128)} %refs_6_.1), custom_call_target="tpu_custom_call" | custom-call | tf_op jit(solution)/shard_map/pallas_call | solution.py:536
  2.4 22.0 %all_to_all.20.refs_13_.arrived_ref.feature_arrived_ref = bf16[32,40,128]{2,1,0:T(8,128)(2,1)S(1)} all-to-all(bf16[32,40,128]{2,1,0:T(8,128)(2,1)S(1)} %bitcast.9), channel_id=1, replica_groups=mesh['grp'=8,'dev'=32] {'dev'}, dimensions={0} | all-to-all | bytes 655360 | tf_op jit(solution)/shard_map/all_to_all | solution.py:485
  24.4 2.6 %collective-permute-start.2 = (bf16[128,128]{1,0:T(8,128)(2,1)S(1)}, bf16[128,128]{1,0:T(8,128)(2,1)S(1)}, u32[]{:S(2)}, u32[]{:S(2)}) collective-permute-start(bf16[128,128]{1,0:T(8,128)(2,1)S(1)} %shard_map.191.refs_0_), channel_id=1, source_target_pairs={{0,192},{32,224},{64,0},{96,32},{128,64},{160,96},{192,128},{224,1... | collective-permute-start | bytes 98312 | tf_op jit(solution)/shard_map/ppermute | solution.py:494
  28.7 3.1 %shard_map.190 = (bf16[512,2560]{1,0:T(8,128)(2,1)S(1)}, f32[512,128]{1,0:T(8,128)S(1)}, bf16[768,512]{1,0:T(8,128)(2,1)S(1)}, s32[40,32]{1,0:T(8,128)S(1)}, bf16[1280,512]{1,0:T(8,128)(2,1)S(1)}) custom-call(bf16[32,128,128]{2,1,0:T(8,128)(2,1)} %refs_0_.1, s32[1,32]{1,0:T(1,128)} %refs_1_.1, s32[1,32]{1,0:T(1,128)} %refs_2_.1, s32[1]{0:T(128)S(6)} %copy.21.refs_3_, ...), custom_call_target="tpu_custom_call" | custom-call | flops 335544320 | bytes 8388608 | tf_op jit(solution)/shard_map/pallas_call | solution.py:555
  31.9 5.7 %collective-permute-start.3 = (bf16[512,128]{1,0:T(8,128)(2,1)S(1)}, bf16[512,128]{1,0:T(8,128)(2,1)S(1)}, u32[]{:S(2)}, u32[]{:S(2)}) collective-permute-start(bf16[512,128]{1,0:T(8,128)(2,1)S(1)} %shard_map.192.own_hub_ref.feature_ref), channel_id=1, source_target_pairs={{0,32},{32,0},{64,96},{96,64},{128,160},{160,128},{192,224},{224,1... | collective-permute-start | bytes 393224 | tf_op jit(solution)/shard_map/ppermute | solution.py:489
  37.6 0.9 shard_map.193.part_ref
  38.6 1.0 shard_map.194
  39.6 14.7 %all_to_all.21.arrived_ref = bf16[32,40,128]{2,1,0:T(8,128)(2,1)S(1)} all-to-all(bf16[32,40,128]{2,1,0:T(8,128)(2,1)S(1)} %bitcast.10), channel_id=1, replica_groups=mesh['grp'=8,'dev'=32] {'dev'}, dimensions={0} | all-to-all | bytes 655360 | tf_op jit(solution)/shard_map/all_to_all | solution.py:485
  54.3 1.7 %collective-permute-start.6 = (bf16[128,128]{1,0:T(8,128)(2,1)S(1)}, bf16[128,128]{1,0:T(8,128)(2,1)S(1)}, u32[]{:S(2)}, u32[]{:S(2)}) collective-permute-start(bf16[128,128]{1,0:T(8,128)(2,1)S(1)} %shard_map.196.refs_0_), channel_id=1, source_target_pairs={{0,192},{32,224},{64,0},{96,32},{128,64},{160,96},{192,128},{224,1... | collective-permute-start | bytes 98312 | tf_op jit(solution)/shard_map/ppermute | solution.py:494
  55.9 1.1 collective-permute-start.5
  57.1 1.6 %shard_map.195 = (bf16[512,512]{1,0:T(8,128)(2,1)}, bf16[256,1536]{1,0:T(8,128)(2,1)S(1)}, bf16[1536,512]{1,0:T(8,128)(2,1)S(1)}, f32[512,512]{1,0:T(8,128)S(1)}, f32[512,256]{1,0:T(8,128)S(1)}) custom-call(bf16[512,128]{1,0:T(8,128)(2,1)S(1)} %copy-done, bf16[32,40,128]{2,1,0:T(8,128)(2,1)S(1)} %all_to_all.20.refs_13_.arrived_ref.feature_arrived_ref, ...), custom_call_target="tpu_custom_call" | custom-call | flops 1610612736 | bytes 8388608 | tf_op jit(solution)/shard_map/pallas_call | solution.py:601
  58.7 1.5 %collective-permute-done.5.refs_2_ = bf16[128,128]{1,0:T(8,128)(2,1)S(1)} collective-permute-done((bf16[128,128]{1,0:T(8,128)(2,1)S(1)}, bf16[128,128]{1,0:T(8,128)(2,1)S(1)}, u32[]{:S(2)}, u32[]{:S(2)}) %collective-permute-start.5) | collective-permute-done | bytes 32800 | tf_op jit(solution)/shard_map/ppermute | solution.py:494
  60.2 0.8 collective-permute-done.4.refs_1_
  61.1 5.8 %collective-permute-start.7 = (bf16[512,128]{1,0:T(8,128)(2,1)S(1)}, bf16[512,128]{1,0:T(8,128)(2,1)S(1)}, u32[]{:S(2)}, u32[]{:S(2)}) collective-permute-start(bf16[512,128]{1,0:T(8,128)(2,1)S(1)} %shard_map.197.mean_ref), channel_id=1, source_target_pairs={{0,32},{32,0},{64,96},{96,64},{128,160},{160,128},{192,224},{224,1... | collective-permute-start | bytes 393224 | tf_op jit(solution)/shard_map/ppermute | solution.py:489
  67.8 5.3 %shard_map.199 = (f32[512,512]{1,0:T(8,128)S(1)}, bf16[32,48,128]{2,1,0:T(8,128)(2,1)S(1)}, bf16[2304,128]{1,0:T(8,128)(2,1)S(1)}, bf16[2304,128]{1,0:T(8,128)(2,1)S(1)}) custom-call(bf16[256,1536]{1,0:T(8,128)(2,1)S(1)} %get-tuple-element.48.early_turned_ref, bf16[1536,512]{1,0:T(8,128)(2,1)S(1)} %get-tuple-element.49.early_source_ref, ...), custom_call_target="tpu_custom_call" | custom-call | tf_op jit(solution)/shard_map/pallas_call | solution.py:629
  73.6 1.6 %collective-permute-done.8.arrived_ref = bf16[2304,128]{1,0:T(8,128)(2,1)S(1)} collective-permute-done((bf16[2304,128]{1,0:T(8,128)(2,1)S(1)}, bf16[2304,128]{1,0:T(8,128)(2,1)S(1)}, u32[]{:S(2)}, u32[]{:S(2)}) %collective-permute-start.8) | collective-permute-done | bytes 589856 | tf_op jit(solution)/shard_map/ppermute | solution.py:489
  75.4 22.2 %all_to_all.22.arrived_ref = bf16[32,88,128]{2,1,0:T(8,128)(2,1)S(1)} all-to-all(bf16[32,88,128]{2,1,0:T(8,128)(2,1)S(1)} %get-tuple-element.60), channel_id=1, replica_groups=mesh['grp'=8,'dev'=32] {'dev'}, dimensions={0} | all-to-all | bytes 1441792 | tf_op jit(solution)/shard_map/all_to_all | solution.py:485
  99.2 1.3 %shard_map.201.refs_3_.base_ref = f32[512,512]{1,0:T(8,128)S(1)} custom-call(f32[512,512]{1,0:T(8,128)S(1)} %get-tuple-element.56.base_ref, bf16[32,88,128]{2,1,0:T(8,128)(2,1)S(1)} %all_to_all.22.arrived_ref, s32[40,32]{1,0:T(8,128)S(1)} %get-tuple-element.61.wanted_ref, bf16[768,512]{1,0:T(8,128)(2,1)S(1)} %get-tuple-element.46.weights_ref), custom_call_target="tpu_custom_call" | custom-call | flops 402653184 | bytes 4194304 | tf_op jit(solution)/shard_map/pallas_call | solution.py:658
  101.4 1.3 collective-permute-done.10.refs_1_
  102.7 0.9 collective-permute-done.11.refs_2_
  103.7 21.9 %all_to_all.23.arrived_ref.mine_ref = bf16[32,48,128]{2,1,0:T(8,128)(2,1)S(1)} all-to-all(bf16[32,48,128]{2,1,0:T(8,128)(2,1)S(1)} %shard_map.203), channel_id=1, replica_groups=mesh['grp'=8,'dev'=32] {'dev'}, dimensions={0} | all-to-all | bytes 786432 | tf_op jit(solution)/shard_map/all_to_all | solution.py:485
  125.6 3.8 %collective-permute-start.12 = (bf16[32,48,128]{2,1,0:T(8,128)(2,1)S(1)}, bf16[32,48,128]{2,1,0:T(8,128)(2,1)S(1)}, u32[]{:S(2)}, u32[]{:S(2)}) collective-permute-start(bf16[32,48,128]{2,1,0:T(8,128)(2,1)S(1)} %all_to_all.23.arrived_ref.mine_ref), channel_id=1, source_target_pairs={{0,32},{32,0},{64,96},{96,64},{128,160},{160,128},{192,224},{224,1... | collective-permute-start | bytes 1179656 | tf_op jit(solution)/shard_map/ppermute | solution.py:489
  129.4 1.5 %shard_map.204 = f32[512,512]{1,0:T(8,128)} custom-call(f32[512,512]{1,0:T(8,128)S(1)} %shard_map.201.refs_3_.base_ref, bf16[32,48,128]{2,1,0:T(8,128)(2,1)S(1)} %all_to_all.23.arrived_ref.mine_ref, s32[40,32]{1,0:T(8,128)S(1)} %get-tuple-element.61.wanted_ref, bf16[768,512]{1,0:T(8,128)(2,1)S(1)} %get-tuple-element.46.weights_ref), custom_call_target="tpu_custom_call" | custom-call | flops 268435456 | bytes 4194304 | tf_op jit(solution)/shard_map/pallas_call | solution.py:672
  131.0 1.1 shard_map.205
  (25 shorter events, 5.3 us)
Async XLA Ops:
  24.4 13.2 %copy-start = (bf16[512,128]{1,0:T(8,128)(2,1)S(1)}, bf16[512,128]{1,0:T(8,128)(2,1)}, u32[]{:S(2)}) copy-start(bf16[512,128]{1,0:T(8,128)(2,1)} %features_ref.3) | copy-start | bytes 393220
  24.4 7.4 %collective-permute-start.2 = (bf16[128,128]{1,0:T(8,128)(2,1)S(1)}, bf16[128,128]{1,0:T(8,128)(2,1)S(1)}, u32[]{:S(2)}, u32[]{:S(2)}) collective-permute-start(bf16[128,128]{1,0:T(8,128)(2,1)S(1)} %shard_map.191.refs_0_), channel_id=1, source_target_pairs={{0,192},{32,224},{64,0},{96,32},{128,64},{160,96},{192,128},{224,1... | collective-permute-start | bytes 98312 | tf_op jit(solution)/shard_map/ppermute | solution.py:494
  27.0 4.9 %collective-permute-start.1 = (bf16[128,128]{1,0:T(8,128)(2,1)S(1)}, bf16[128,128]{1,0:T(8,128)(2,1)S(1)}, u32[]{:S(2)}, u32[]{:S(2)}) collective-permute-start(bf16[128,128]{1,0:T(8,128)(2,1)S(1)} %shard_map.191.refs_0_), channel_id=1, source_target_pairs={{0,128},{32,160},{64,192},{96,224},{128,0},{160,32},{192,64},{224,... | collective-permute-start | bytes 98312 | tf_op jit(solution)/shard_map/ppermute | solution.py:494
  27.5 4.4 %collective-permute-start = (bf16[128,128]{1,0:T(8,128)(2,1)S(1)}, bf16[128,128]{1,0:T(8,128)(2,1)S(1)}, u32[]{:S(2)}, u32[]{:S(2)}) collective-permute-start(bf16[128,128]{1,0:T(8,128)(2,1)S(1)} %shard_map.191.refs_0_), channel_id=1, source_target_pairs={{0,64},{32,96},{64,128},{96,160},{128,192},{160,224},{192,0},{224,... | collective-permute-start | bytes 98312 | tf_op jit(solution)/shard_map/ppermute | solution.py:494
  31.9 6.7 %collective-permute-start.3 = (bf16[512,128]{1,0:T(8,128)(2,1)S(1)}, bf16[512,128]{1,0:T(8,128)(2,1)S(1)}, u32[]{:S(2)}, u32[]{:S(2)}) collective-permute-start(bf16[512,128]{1,0:T(8,128)(2,1)S(1)} %shard_map.192.own_hub_ref.feature_ref), channel_id=1, source_target_pairs={{0,32},{32,0},{64,96},{96,64},{128,160},{160,128},{192,224},{224,1... | collective-permute-start | bytes 393224 | tf_op jit(solution)/shard_map/ppermute | solution.py:489
  54.3 4.4 %collective-permute-start.6 = (bf16[128,128]{1,0:T(8,128)(2,1)S(1)}, bf16[128,128]{1,0:T(8,128)(2,1)S(1)}, u32[]{:S(2)}, u32[]{:S(2)}) collective-permute-start(bf16[128,128]{1,0:T(8,128)(2,1)S(1)} %shard_map.196.refs_0_), channel_id=1, source_target_pairs={{0,192},{32,224},{64,0},{96,32},{128,64},{160,96},{192,128},{224,1... | collective-permute-start | bytes 98312 | tf_op jit(solution)/shard_map/ppermute | solution.py:494
  55.9 4.3 %collective-permute-start.5 = (bf16[128,128]{1,0:T(8,128)(2,1)S(1)}, bf16[128,128]{1,0:T(8,128)(2,1)S(1)}, u32[]{:S(2)}, u32[]{:S(2)}) collective-permute-start(bf16[128,128]{1,0:T(8,128)(2,1)S(1)} %shard_map.196.refs_0_), channel_id=1, source_target_pairs={{0,128},{32,160},{64,192},{96,224},{128,0},{160,32},{192,64},{224,... | collective-permute-start | bytes 98312 | tf_op jit(solution)/shard_map/ppermute | solution.py:494
  57.1 4.0 %collective-permute-start.4 = (bf16[128,128]{1,0:T(8,128)(2,1)S(1)}, bf16[128,128]{1,0:T(8,128)(2,1)S(1)}, u32[]{:S(2)}, u32[]{:S(2)}) collective-permute-start(bf16[128,128]{1,0:T(8,128)(2,1)S(1)} %shard_map.196.refs_0_), channel_id=1, source_target_pairs={{0,64},{32,96},{64,128},{96,160},{128,192},{160,224},{192,0},{224,... | collective-permute-start | bytes 98312 | tf_op jit(solution)/shard_map/ppermute | solution.py:494
  61.1 6.8 %collective-permute-start.7 = (bf16[512,128]{1,0:T(8,128)(2,1)S(1)}, bf16[512,128]{1,0:T(8,128)(2,1)S(1)}, u32[]{:S(2)}, u32[]{:S(2)}) collective-permute-start(bf16[512,128]{1,0:T(8,128)(2,1)S(1)} %shard_map.197.mean_ref), channel_id=1, source_target_pairs={{0,32},{32,0},{64,96},{96,64},{128,160},{160,128},{192,224},{224,1... | collective-permute-start | bytes 393224 | tf_op jit(solution)/shard_map/ppermute | solution.py:489
  73.1 2.1 %collective-permute-start.8 = (bf16[2304,128]{1,0:T(8,128)(2,1)S(1)}, bf16[2304,128]{1,0:T(8,128)(2,1)S(1)}, u32[]{:S(2)}, u32[]{:S(2)}) collective-permute-start(bf16[2304,128]{1,0:T(8,128)(2,1)S(1)} %get-tuple-element.58), channel_id=1, source_target_pairs={{0,32},{32,0},{64,96},{96,64},{128,160},{160,128},{192,224},{224,1... | collective-permute-start | bytes 1769480 | tf_op jit(solution)/shard_map/ppermute | solution.py:489
  97.7 3.7 %collective-permute-start.9 = (bf16[336,128]{1,0:T(8,128)(2,1)S(1)}, bf16[336,128]{1,0:T(8,128)(2,1)S(1)}, u32[]{:S(2)}, u32[]{:S(2)}) collective-permute-start(bf16[336,128]{1,0:T(8,128)(2,1)S(1)} %get-tuple-element.67), channel_id=1, source_target_pairs={{0,192},{32,224},{64,0},{96,32},{128,64},{160,96},{192,128},{224,1... | collective-permute-start | bytes 258056 | tf_op jit(solution)/shard_map/ppermute | solution.py:494
  97.8 4.9 %collective-permute-start.10 = (bf16[336,128]{1,0:T(8,128)(2,1)S(1)}, bf16[336,128]{1,0:T(8,128)(2,1)S(1)}, u32[]{:S(2)}, u32[]{:S(2)}) collective-permute-start(bf16[336,128]{1,0:T(8,128)(2,1)S(1)} %get-tuple-element.68), channel_id=1, source_target_pairs={{0,128},{32,160},{64,192},{96,224},{128,0},{160,32},{192,64},{224,... | collective-permute-start | bytes 258056 | tf_op jit(solution)/shard_map/ppermute | solution.py:494
  98.5 5.1 %collective-permute-start.11 = (bf16[336,128]{1,0:T(8,128)(2,1)S(1)}, bf16[336,128]{1,0:T(8,128)(2,1)S(1)}, u32[]{:S(2)}, u32[]{:S(2)}) collective-permute-start(bf16[336,128]{1,0:T(8,128)(2,1)S(1)} %get-tuple-element.69), channel_id=1, source_target_pairs={{0,64},{32,96},{64,128},{96,160},{128,192},{160,224},{192,0},{224,... | collective-permute-start | bytes 258056 | tf_op jit(solution)/shard_map/ppermute | solution.py:494
  125.6 5.3 %collective-permute-start.12 = (bf16[32,48,128]{2,1,0:T(8,128)(2,1)S(1)}, bf16[32,48,128]{2,1,0:T(8,128)(2,1)S(1)}, u32[]{:S(2)}, u32[]{:S(2)}) collective-permute-start(bf16[32,48,128]{2,1,0:T(8,128)(2,1)S(1)} %all_to_all.23.arrived_ref.mine_ref), channel_id=1, source_target_pairs={{0,32},{32,0},{64,96},{96,64},{128,160},{160,128},{192,224},{224,1... | collective-permute-start | bytes 1179656 | tf_op jit(solution)/shard_map/ppermute | solution.py:489

commit v8 on v7

--- a/solution.py
+++ b/solution.py
@@ -109,7 +109,7 @@
 
 
 def send_features(
-    features_any, send_any, count_any, hub_any, out_ref, pick_ref, features_ref, send_ref, count_ref, hub_ref, sems
+    features_any, send_any, count_any, hub_any, out_ref, features_ref, send_ref, count_ref, hub_ref, sems
 ):
     loads = fetch(
         (
@@ -122,9 +122,13 @@
     )
     for load in loads[:-1]:
         load.wait()
-    pick_matrix(wanted_rows(send_ref[...], count_ref[...], hub_ref), pick_ref)
+    wanted = wanted_rows(send_ref[...], count_ref[...], hub_ref)
     loads[-1].wait()
-    out_ref[...] = nn(pick_ref[...], features_ref[...]).astype(BF16)
+    features = features_ref[...]
+    lane = iota((8 * FORWARD_ROWS, features.shape[0]), 1)
+    for n in range(0, PEERS, 8):
+        rows = jnp.concatenate([wanted[:, i : i + 1] for i in range(n, n + 8)], axis=0)
+        out_ref[n * FORWARD_ROWS : (n + 8) * FORWARD_ROWS, :] = nn(one_hot(rows == lane), features).astype(BF16)
 
 
 def build_dense(*refs):
@@ -311,12 +315,11 @@
     loss = jnp.sum(times * (jnp.log(total) - chosen), axis=0, keepdims=True)
     upstream = times * ((powers / total - onehot) / samples_all)
     upstream = upstream.astype(BF16)
-    scaled_ref[...] = jnp.transpose((upstream.astype(F32) / degree).astype(BF16))
+    scaled_ref[...] = (upstream.astype(F32) / degree).astype(BF16)
 
     def back(columns):
-        found = nn(scaled_ref[...], columns)
-        found = jnp.transpose(found.astype(BF16))
-        return found, nn(found, weights_ref[mean_rows, :])
+        found = tn(columns, scaled_ref[...])
+        return found, nn(found.astype(BF16), weights_ref[mean_rows, :])
 
     def mask(at, source, grad):
         masked_ref[at : at + nodes, :] = jnp.where(source > 0, grad, 0.0).astype(BF16)
@@ -328,7 +331,6 @@
     ):
         found, spread = back(columns_ref[...])
         mask(hub_at + i * nodes, source_ref[...], spread)
-        found = found.astype(F32)
         for block in range(CHIPS):
             for n in range(0, PEERS, 2):
                 at = block * GROUP_HUBS + n * HUBS_EACH
@@ -352,8 +354,8 @@
         mask(at, early_source_ref[at : at + nodes, :], spread)
         for p in range(each):
             at = p * CAPACITY
-            rest = found[at : at + CAPACITY, TILE:].astype(F32)
-            edge_ref[i * each + p, 0:CAPACITY, :] = found[at : at + CAPACITY, 0:TILE]
+            rest = found[at : at + CAPACITY, TILE:]
+            edge_ref[i * each + p, 0:CAPACITY, :] = found[at : at + CAPACITY, 0:TILE].astype(BF16)
             edge_ref[i * each + p, CAPACITY:EDGE_ROWS, :] = join_rests(
                 rest[0 : CAPACITY // 2], rest[CAPACITY // 2 :]
             ).astype(BF16)
@@ -537,7 +539,6 @@
         send_features,
         shape((slots, inputs), BF16),
         [
-            pltpu.VMEM((slots, nodes), BF16),
             pltpu.VMEM((nodes, inputs), BF16),
             pltpu.VMEM(send_list.shape[1:], I32),
             pltpu.VMEM(send_count.shape, I32),
@@ -638,7 +639,7 @@
             pltpu.VMEM((2 * inputs, half), BF16),
             pltpu.VMEM((half, width), BF16),
             pltpu.VMEM((nodes, half), BF16),
-            pltpu.VMEM((padded, nodes), BF16),
+            pltpu.VMEM((nodes, padded), BF16),
             pltpu.VMEM((table, width), BF16),
             pltpu.VMEM((STACK_ROWS, width), F32),
         ],

time: 132 us -> 131 us (level)
  no operation moved by 1% of the time
where the time goes in v8:
time: 131 us
  blocking collectives  80.8 us (62%)
  starting transfers between devices  24 us (18%)
  Pallas kernels  17.4 us (13%)
  waiting for transfers between devices  7.39 us (6%)
  between operations  1.41 us (1%)
    all_to_all x4, blocking collectives, swap(): lax.all_to_all(values, 'dev', split_axis=0, concat_axis=0, tiled=True)  80.8 us
    ppermute x4, starting transfers between devices, to_core(): lax.ppermute(values, 'grp', [(i, i ^ 1) for i in range(CHIPS * CORES)])  16 us
    ppermute x9, starting transfers between devices, along_x(): lax.ppermute(values, 'grp', [(i, (i + CORES * shift) % every) for i in ra...  7.96 us
    ppermute x9, waiting for transfers between devices, along_x(): lax.ppermute(values, 'grp', [(i, (i + CORES * shift) % every) for i in ra...  5.39 us
    pallas_call x1, Pallas kernels, on_device(): kernel_call(functools.partial(main_part, samples_all, classes), (shape((n...  4.34 us
    pallas_call x1, Pallas kernels, on_device(): kernel_call(build_dense, (shape((nodes, table), BF16), shape((nodes, TILE...  2.88 us
  transfers between devices with their start and end apart: 13, of which 8 were waited for; matrix products, arithmetic and copies ran while one was open for 0% of the time, Pallas kernels for 7%

profile of v8, /device:TPU:1, one launch (start us, length us, event | category | flops | bytes accessed | tf_op | source)
XLA Modules:
  0.0 131.0 jit_solution(13519841777176291158)
XLA Ops:
  0.6 1.7 %shard_map.189 = bf16[1280,128]{1,0:T(8,128)(2,1)S(1)} custom-call(bf16[512,128]{1,0:T(8,128)(2,1)} %features_ref.3, s32[1,32,32]{2,1,0:T(8,128)} %send_any.1, s32[1,32]{1,0:T(1,128)} %refs_5_.1, s32[1,4]{1,0:T(1,128)} %refs_6_.1), custom_call_target="tpu_custom_call" | custom-call | tf_op jit(solution)/shard_map/pallas_call | solution.py:538
  2.3 22.0 %all_to_all.20.refs_13_.arrived_ref.feature_arrived_ref = bf16[32,40,128]{2,1,0:T(8,128)(2,1)S(1)} all-to-all(bf16[32,40,128]{2,1,0:T(8,128)(2,1)S(1)} %bitcast.9), channel_id=1, replica_groups=mesh['grp'=8,'dev'=32] {'dev'}, dimensions={0} | all-to-all | bytes 655360 | tf_op jit(solution)/shard_map/all_to_all | solution.py:487
  24.3 2.5 %collective-permute-start.2 = (bf16[128,128]{1,0:T(8,128)(2,1)S(1)}, bf16[128,128]{1,0:T(8,128)(2,1)S(1)}, u32[]{:S(2)}, u32[]{:S(2)}) collective-permute-start(bf16[128,128]{1,0:T(8,128)(2,1)S(1)} %shard_map.191.refs_0_), channel_id=1, source_target_pairs={{0,192},{32,224},{64,0},{96,32},{128,64},{160,96},{192,128},{224,1... | collective-permute-start | bytes 98312 | tf_op jit(solution)/shard_map/ppermute | solution.py:496
  28.7 2.9 %shard_map.190 = (bf16[512,2560]{1,0:T(8,128)(2,1)S(1)}, f32[512,128]{1,0:T(8,128)S(1)}, bf16[768,512]{1,0:T(8,128)(2,1)S(1)}, s32[40,32]{1,0:T(8,128)S(1)}, bf16[1280,512]{1,0:T(8,128)(2,1)S(1)}) custom-call(bf16[32,128,128]{2,1,0:T(8,128)(2,1)} %refs_0_.1, s32[1,32]{1,0:T(1,128)} %refs_1_.1, s32[1,32]{1,0:T(1,128)} %refs_2_.1, s32[1]{0:T(128)S(6)} %copy.21.refs_3_, ...), custom_call_target="tpu_custom_call" | custom-call | flops 335544320 | bytes 8388608 | tf_op jit(solution)/shard_map/pallas_call | solution.py:556
  31.6 5.9 %collective-permute-start.3 = (bf16[512,128]{1,0:T(8,128)(2,1)S(1)}, bf16[512,128]{1,0:T(8,128)(2,1)S(1)}, u32[]{:S(2)}, u32[]{:S(2)}) collective-permute-start(bf16[512,128]{1,0:T(8,128)(2,1)S(1)} %shard_map.192.own_hub_ref.feature_ref), channel_id=1, source_target_pairs={{0,32},{32,0},{64,96},{96,64},{128,160},{160,128},{192,224},{224,1... | collective-permute-start | bytes 393224 | tf_op jit(solution)/shard_map/ppermute | solution.py:491
  37.5 0.9 shard_map.193.part_ref
  38.5 1.0 shard_map.194
  39.5 14.7 %all_to_all.21.arrived_ref = bf16[32,40,128]{2,1,0:T(8,128)(2,1)S(1)} all-to-all(bf16[32,40,128]{2,1,0:T(8,128)(2,1)S(1)} %bitcast.10), channel_id=1, replica_groups=mesh['grp'=8,'dev'=32] {'dev'}, dimensions={0} | all-to-all | bytes 655360 | tf_op jit(solution)/shard_map/all_to_all | solution.py:487
  54.2 1.6 %collective-permute-start.6 = (bf16[128,128]{1,0:T(8,128)(2,1)S(1)}, bf16[128,128]{1,0:T(8,128)(2,1)S(1)}, u32[]{:S(2)}, u32[]{:S(2)}) collective-permute-start(bf16[128,128]{1,0:T(8,128)(2,1)S(1)} %shard_map.196.refs_0_), channel_id=1, source_target_pairs={{0,192},{32,224},{64,0},{96,32},{128,64},{160,96},{192,128},{224,1... | collective-permute-start | bytes 98312 | tf_op jit(solution)/shard_map/ppermute | solution.py:496
  55.8 1.1 collective-permute-start.5
  56.9 1.6 %shard_map.195 = (bf16[512,512]{1,0:T(8,128)(2,1)}, bf16[256,1536]{1,0:T(8,128)(2,1)S(1)}, bf16[1536,512]{1,0:T(8,128)(2,1)S(1)}, f32[512,512]{1,0:T(8,128)S(1)}, f32[512,256]{1,0:T(8,128)S(1)}) custom-call(bf16[512,128]{1,0:T(8,128)(2,1)S(1)} %copy-done, bf16[32,40,128]{2,1,0:T(8,128)(2,1)S(1)} %all_to_all.20.refs_13_.arrived_ref.feature_arrived_ref, ...), custom_call_target="tpu_custom_call" | custom-call | flops 1610612736 | bytes 8388608 | tf_op jit(solution)/shard_map/pallas_call | solution.py:602
  58.6 1.5 %collective-permute-done.5.refs_2_ = bf16[128,128]{1,0:T(8,128)(2,1)S(1)} collective-permute-done((bf16[128,128]{1,0:T(8,128)(2,1)S(1)}, bf16[128,128]{1,0:T(8,128)(2,1)S(1)}, u32[]{:S(2)}, u32[]{:S(2)}) %collective-permute-start.5) | collective-permute-done | bytes 32800 | tf_op jit(solution)/shard_map/ppermute | solution.py:496
  60.1 0.8 collective-permute-done.4.refs_1_
  60.9 5.8 %collective-permute-start.7 = (bf16[512,128]{1,0:T(8,128)(2,1)S(1)}, bf16[512,128]{1,0:T(8,128)(2,1)S(1)}, u32[]{:S(2)}, u32[]{:S(2)}) collective-permute-start(bf16[512,128]{1,0:T(8,128)(2,1)S(1)} %shard_map.197.mean_ref), channel_id=1, source_target_pairs={{0,32},{32,0},{64,96},{96,64},{128,160},{160,128},{192,224},{224,1... | collective-permute-start | bytes 393224 | tf_op jit(solution)/shard_map/ppermute | solution.py:491
  67.7 4.3 %shard_map.199 = (f32[512,512]{1,0:T(8,128)S(1)}, bf16[32,48,128]{2,1,0:T(8,128)(2,1)S(1)}, bf16[2304,128]{1,0:T(8,128)(2,1)S(1)}, bf16[2304,128]{1,0:T(8,128)(2,1)S(1)}) custom-call(bf16[256,1536]{1,0:T(8,128)(2,1)S(1)} %get-tuple-element.48.early_turned_ref, bf16[1536,512]{1,0:T(8,128)(2,1)S(1)} %get-tuple-element.49.early_source_ref, ...), custom_call_target="tpu_custom_call" | custom-call | tf_op jit(solution)/shard_map/pallas_call | solution.py:630
  72.5 1.6 %collective-permute-done.8.arrived_ref = bf16[2304,128]{1,0:T(8,128)(2,1)S(1)} collective-permute-done((bf16[2304,128]{1,0:T(8,128)(2,1)S(1)}, bf16[2304,128]{1,0:T(8,128)(2,1)S(1)}, u32[]{:S(2)}, u32[]{:S(2)}) %collective-permute-start.8) | collective-permute-done | bytes 589856 | tf_op jit(solution)/shard_map/ppermute | solution.py:491
  74.3 22.2 %all_to_all.22.arrived_ref = bf16[32,88,128]{2,1,0:T(8,128)(2,1)S(1)} all-to-all(bf16[32,88,128]{2,1,0:T(8,128)(2,1)S(1)} %get-tuple-element.60), channel_id=1, replica_groups=mesh['grp'=8,'dev'=32] {'dev'}, dimensions={0} | all-to-all | bytes 1441792 | tf_op jit(solution)/shard_map/all_to_all | solution.py:487
  98.2 1.3 %shard_map.201.refs_3_.base_ref = f32[512,512]{1,0:T(8,128)S(1)} custom-call(f32[512,512]{1,0:T(8,128)S(1)} %get-tuple-element.56.base_ref, bf16[32,88,128]{2,1,0:T(8,128)(2,1)S(1)} %all_to_all.22.arrived_ref, s32[40,32]{1,0:T(8,128)S(1)} %get-tuple-element.61.wanted_ref, bf16[768,512]{1,0:T(8,128)(2,1)S(1)} %get-tuple-element.46.weights_ref), custom_call_target="tpu_custom_call" | custom-call | flops 402653184 | bytes 4194304 | tf_op jit(solution)/shard_map/pallas_call | solution.py:659
  100.3 1.3 %collective-permute-done.10.refs_1_ = bf16[336,128]{1,0:T(8,128)(2,1)S(1)} collective-permute-done((bf16[336,128]{1,0:T(8,128)(2,1)S(1)}, bf16[336,128]{1,0:T(8,128)(2,1)S(1)}, u32[]{:S(2)}, u32[]{:S(2)}) %collective-permute-start.10) | collective-permute-done | bytes 86048 | tf_op jit(solution)/shard_map/ppermute | solution.py:496
  101.6 0.9 collective-permute-done.11.refs_2_
  102.6 21.9 %all_to_all.23.arrived_ref.mine_ref = bf16[32,48,128]{2,1,0:T(8,128)(2,1)S(1)} all-to-all(bf16[32,48,128]{2,1,0:T(8,128)(2,1)S(1)} %shard_map.203), channel_id=1, replica_groups=mesh['grp'=8,'dev'=32] {'dev'}, dimensions={0} | all-to-all | bytes 786432 | tf_op jit(solution)/shard_map/all_to_all | solution.py:487
  124.5 3.8 %collective-permute-start.12 = (bf16[32,48,128]{2,1,0:T(8,128)(2,1)S(1)}, bf16[32,48,128]{2,1,0:T(8,128)(2,1)S(1)}, u32[]{:S(2)}, u32[]{:S(2)}) collective-permute-start(bf16[32,48,128]{2,1,0:T(8,128)(2,1)S(1)} %all_to_all.23.arrived_ref.mine_ref), channel_id=1, source_target_pairs={{0,32},{32,0},{64,96},{96,64},{128,160},{160,128},{192,224},{224,1... | collective-permute-start | bytes 1179656 | tf_op jit(solution)/shard_map/ppermute | solution.py:491
  128.3 1.5 %shard_map.204 = f32[512,512]{1,0:T(8,128)} custom-call(f32[512,512]{1,0:T(8,128)S(1)} %shard_map.201.refs_3_.base_ref, bf16[32,48,128]{2,1,0:T(8,128)(2,1)S(1)} %all_to_all.23.arrived_ref.mine_ref, s32[40,32]{1,0:T(8,128)S(1)} %get-tuple-element.61.wanted_ref, bf16[768,512]{1,0:T(8,128)(2,1)S(1)} %get-tuple-element.46.weights_ref), custom_call_target="tpu_custom_call" | custom-call | flops 268435456 | bytes 4194304 | tf_op jit(solution)/shard_map/pallas_call | solution.py:673
  129.8 1.1 shard_map.205
  (25 shorter events, 5.3 us)
Async XLA Ops:
  24.3 13.2 %copy-start = (bf16[512,128]{1,0:T(8,128)(2,1)S(1)}, bf16[512,128]{1,0:T(8,128)(2,1)}, u32[]{:S(2)}) copy-start(bf16[512,128]{1,0:T(8,128)(2,1)} %features_ref.3) | copy-start | bytes 393220
  24.3 7.2 %collective-permute-start.2 = (bf16[128,128]{1,0:T(8,128)(2,1)S(1)}, bf16[128,128]{1,0:T(8,128)(2,1)S(1)}, u32[]{:S(2)}, u32[]{:S(2)}) collective-permute-start(bf16[128,128]{1,0:T(8,128)(2,1)S(1)} %shard_map.191.refs_0_), channel_id=1, source_target_pairs={{0,192},{32,224},{64,0},{96,32},{128,64},{160,96},{192,128},{224,1... | collective-permute-start | bytes 98312 | tf_op jit(solution)/shard_map/ppermute | solution.py:496
  26.9 4.7 %collective-permute-start.1 = (bf16[128,128]{1,0:T(8,128)(2,1)S(1)}, bf16[128,128]{1,0:T(8,128)(2,1)S(1)}, u32[]{:S(2)}, u32[]{:S(2)}) collective-permute-start(bf16[128,128]{1,0:T(8,128)(2,1)S(1)} %shard_map.191.refs_0_), channel_id=1, source_target_pairs={{0,128},{32,160},{64,192},{96,224},{128,0},{160,32},{192,64},{224,... | collective-permute-start | bytes 98312 | tf_op jit(solution)/shard_map/ppermute | solution.py:496
  27.4 4.2 %collective-permute-start = (bf16[128,128]{1,0:T(8,128)(2,1)S(1)}, bf16[128,128]{1,0:T(8,128)(2,1)S(1)}, u32[]{:S(2)}, u32[]{:S(2)}) collective-permute-start(bf16[128,128]{1,0:T(8,128)(2,1)S(1)} %shard_map.191.refs_0_), channel_id=1, source_target_pairs={{0,64},{32,96},{64,128},{96,160},{128,192},{160,224},{192,0},{224,... | collective-permute-start | bytes 98312 | tf_op jit(solution)/shard_map/ppermute | solution.py:496
  31.6 6.9 %collective-permute-start.3 = (bf16[512,128]{1,0:T(8,128)(2,1)S(1)}, bf16[512,128]{1,0:T(8,128)(2,1)S(1)}, u32[]{:S(2)}, u32[]{:S(2)}) collective-permute-start(bf16[512,128]{1,0:T(8,128)(2,1)S(1)} %shard_map.192.own_hub_ref.feature_ref), channel_id=1, source_target_pairs={{0,32},{32,0},{64,96},{96,64},{128,160},{160,128},{192,224},{224,1... | collective-permute-start | bytes 393224 | tf_op jit(solution)/shard_map/ppermute | solution.py:491
  54.2 4.3 %collective-permute-start.6 = (bf16[128,128]{1,0:T(8,128)(2,1)S(1)}, bf16[128,128]{1,0:T(8,128)(2,1)S(1)}, u32[]{:S(2)}, u32[]{:S(2)}) collective-permute-start(bf16[128,128]{1,0:T(8,128)(2,1)S(1)} %shard_map.196.refs_0_), channel_id=1, source_target_pairs={{0,192},{32,224},{64,0},{96,32},{128,64},{160,96},{192,128},{224,1... | collective-permute-start | bytes 98312 | tf_op jit(solution)/shard_map/ppermute | solution.py:496
  55.8 4.3 %collective-permute-start.5 = (bf16[128,128]{1,0:T(8,128)(2,1)S(1)}, bf16[128,128]{1,0:T(8,128)(2,1)S(1)}, u32[]{:S(2)}, u32[]{:S(2)}) collective-permute-start(bf16[128,128]{1,0:T(8,128)(2,1)S(1)} %shard_map.196.refs_0_), channel_id=1, source_target_pairs={{0,128},{32,160},{64,192},{96,224},{128,0},{160,32},{192,64},{224,... | collective-permute-start | bytes 98312 | tf_op jit(solution)/shard_map/ppermute | solution.py:496
  56.9 4.0 %collective-permute-start.4 = (bf16[128,128]{1,0:T(8,128)(2,1)S(1)}, bf16[128,128]{1,0:T(8,128)(2,1)S(1)}, u32[]{:S(2)}, u32[]{:S(2)}) collective-permute-start(bf16[128,128]{1,0:T(8,128)(2,1)S(1)} %shard_map.196.refs_0_), channel_id=1, source_target_pairs={{0,64},{32,96},{64,128},{96,160},{128,192},{160,224},{192,0},{224,... | collective-permute-start | bytes 98312 | tf_op jit(solution)/shard_map/ppermute | solution.py:496
  60.9 6.8 %collective-permute-start.7 = (bf16[512,128]{1,0:T(8,128)(2,1)S(1)}, bf16[512,128]{1,0:T(8,128)(2,1)S(1)}, u32[]{:S(2)}, u32[]{:S(2)}) collective-permute-start(bf16[512,128]{1,0:T(8,128)(2,1)S(1)} %shard_map.197.mean_ref), channel_id=1, source_target_pairs={{0,32},{32,0},{64,96},{96,64},{128,160},{160,128},{192,224},{224,1... | collective-permute-start | bytes 393224 | tf_op jit(solution)/shard_map/ppermute | solution.py:491
  72.0 2.1 %collective-permute-start.8 = (bf16[2304,128]{1,0:T(8,128)(2,1)S(1)}, bf16[2304,128]{1,0:T(8,128)(2,1)S(1)}, u32[]{:S(2)}, u32[]{:S(2)}) collective-permute-start(bf16[2304,128]{1,0:T(8,128)(2,1)S(1)} %get-tuple-element.58), channel_id=1, source_target_pairs={{0,32},{32,0},{64,96},{96,64},{128,160},{160,128},{192,224},{224,1... | collective-permute-start | bytes 1769480 | tf_op jit(solution)/shard_map/ppermute | solution.py:491
  96.6 3.7 %collective-permute-start.9 = (bf16[336,128]{1,0:T(8,128)(2,1)S(1)}, bf16[336,128]{1,0:T(8,128)(2,1)S(1)}, u32[]{:S(2)}, u32[]{:S(2)}) collective-permute-start(bf16[336,128]{1,0:T(8,128)(2,1)S(1)} %get-tuple-element.67), channel_id=1, source_target_pairs={{0,192},{32,224},{64,0},{96,32},{128,64},{160,96},{192,128},{224,1... | collective-permute-start | bytes 258056 | tf_op jit(solution)/shard_map/ppermute | solution.py:496
  96.7 4.9 %collective-permute-start.10 = (bf16[336,128]{1,0:T(8,128)(2,1)S(1)}, bf16[336,128]{1,0:T(8,128)(2,1)S(1)}, u32[]{:S(2)}, u32[]{:S(2)}) collective-permute-start(bf16[336,128]{1,0:T(8,128)(2,1)S(1)} %get-tuple-element.68), channel_id=1, source_target_pairs={{0,128},{32,160},{64,192},{96,224},{128,0},{160,32},{192,64},{224,... | collective-permute-start | bytes 258056 | tf_op jit(solution)/shard_map/ppermute | solution.py:496
  97.4 5.1 %collective-permute-start.11 = (bf16[336,128]{1,0:T(8,128)(2,1)S(1)}, bf16[336,128]{1,0:T(8,128)(2,1)S(1)}, u32[]{:S(2)}, u32[]{:S(2)}) collective-permute-start(bf16[336,128]{1,0:T(8,128)(2,1)S(1)} %get-tuple-element.69), channel_id=1, source_target_pairs={{0,64},{32,96},{64,128},{96,160},{128,192},{160,224},{192,0},{224,... | collective-permute-start | bytes 258056 | tf_op jit(solution)/shard_map/ppermute | solution.py:496
  124.5 5.4 %collective-permute-start.12 = (bf16[32,48,128]{2,1,0:T(8,128)(2,1)S(1)}, bf16[32,48,128]{2,1,0:T(8,128)(2,1)S(1)}, u32[]{:S(2)}, u32[]{:S(2)}) collective-permute-start(bf16[32,48,128]{2,1,0:T(8,128)(2,1)S(1)} %all_to_all.23.arrived_ref.mine_ref), channel_id=1, source_target_pairs={{0,32},{32,0},{64,96},{96,64},{128,160},{160,128},{192,224},{224,1... | collective-permute-start | bytes 1179656 | tf_op jit(solution)/shard_map/ppermute | solution.py:491

commit v9 on v8

--- a/solution.py
+++ b/solution.py
@@ -132,15 +132,14 @@
 
 
 def build_dense(*refs):
-    count = 13
+    count = 11
     sources, refs = refs[:count], refs[count + 1 :]
     dense_ref, numbers_ref, weights_ref, wanted_ref, pick_ref, *places, sems = refs
     (
-        adj_ref, dst_ref, src_ref, live_ref, send_ref, count_ref, hub_ref,
-        sample_ref, label_ref, raw_self_ref, raw_mean_ref,
+        adj_ref, dst_ref, src_ref, live_ref, send_ref, count_ref, hub_ref, raw_self_ref, raw_mean_ref,
     ) = places
     targets = (
-        adj_ref, dst_ref, src_ref, live_ref, send_ref, count_ref, hub_ref, sample_ref, label_ref,
+        adj_ref, dst_ref, src_ref, live_ref, send_ref, count_ref, hub_ref,
         weights_ref.at[pl.ds(0, TILE)], weights_ref.at[pl.ds(TILE, TILE)], raw_self_ref, raw_mean_ref,
     )
     loads = fetch(zip(sources, targets), sems)
@@ -162,13 +161,8 @@
     wanted = wanted_rows(send_ref[...], count_ref[...], hub_ref)
     wanted_ref[...] = wanted
     pick_matrix(wanted, pick_ref)
-    nodes = dense_ref.shape[0]
-    node = iota((nodes, sample_ref.shape[1]), 0)
-    times = jnp.sum(jnp.where(node == sample_ref[...], 1.0, 0.0), axis=1, keepdims=True)
-    label = jnp.transpose(jnp.broadcast_to(label_ref[...], (8, nodes)))[:, 0:1]
     degree = jnp.maximum(nn(dense_ref[...], jnp.ones((dense_ref.shape[1], TILE), BF16)), 1.0)
-    lane = iota(degree.shape, 1)
-    numbers_ref[...] = jnp.where(lane == 0, degree, jnp.where(lane == 1, times, label.astype(F32)))
+    numbers_ref[...] = degree
 
 
 def group_hubs(arrived_ref, out_ref):
@@ -273,18 +267,27 @@
 
 
 def own_hub_part(
-    dense_ref, weights_ref, part_ref, feature_ref, mean_ref, turned_ref, source_ref, columns_ref, out_ref
+    dense_ref, weights_ref, part_ref, feature_ref, mean_ref, sample_any, label_any,
+    turned_ref, source_ref, columns_ref, out_ref, times_ref, sample_ref, label_ref, sems,
 ):
+    loads = fetch(((sample_any, sample_ref), (label_any, label_ref)), sems)
     total = hub_part(
         dense_ref, weights_ref, feature_ref[...], mean_ref[...], False, turned_ref, source_ref, columns_ref
     )
     out_ref[...] = part_ref[...] + total
+    for load in loads:
+        load.wait()
+    nodes = dense_ref.shape[0]
+    node = iota((nodes, sample_ref.shape[1]), 0)
+    times = jnp.sum(jnp.where(node == sample_ref[...], 1.0, 0.0), axis=1, keepdims=True)
+    label = jnp.transpose(jnp.broadcast_to(label_ref[...], (8, nodes)))[:, 0:1]
+    times_ref[...] = jnp.where(iota(times_ref.shape, 1) == 0, times, label.astype(F32))
 
 
 def main_part(
     samples_all, classes,
     early_turned_ref, early_source_ref, logits_ref, own_turned_ref, own_source_ref, own_columns_ref, part_ref,
-    dense_ref, numbers_ref, weights_ref, feature_ref, mean_ref,
+    dense_ref, numbers_ref, times_ref, weights_ref, feature_ref, mean_ref,
     base_ref, edge_ref, mine_ref, theirs_ref,
     other_turned_ref, other_source_ref, other_columns_ref, scaled_ref, masked_ref, stack_ref,
 ):
@@ -299,8 +302,8 @@
     )
     hidden = early_source_ref[0:nodes, :]
     degree = numbers_ref[:, 0:1]
-    times = numbers_ref[:, 1:2]
-    label = numbers_ref[:, 2:3].astype(I32)
+    times = times_ref[:, 0:1]
+    label = times_ref[:, 1:2].astype(I32)
     mean = ((part_ref[...] + total) / degree).astype(BF16)
     logits = logits_ref[...] + nt(mean, weights_ref[mean_rows, :])
 
@@ -551,7 +554,7 @@
     raw = (second_self.T, second_mean.T)
     operands = (
         tile_adj, tile_dst, tile_src, tile_count, send_list[0], send_count, hub_list,
-        sample_ids, labels.reshape(1, nodes), first_self, first_mean, *raw,
+        first_self, first_mean, *raw,
     )
     dense, numbers, weights, wanted, picks = kernel_call(
         build_dense,
@@ -570,8 +573,6 @@
             pltpu.VMEM(send_list.shape[1:], I32),
             pltpu.VMEM(send_count.shape, I32),
             pltpu.SMEM(hub_list.shape, I32),
-            pltpu.VMEM(sample_ids.shape, I32),
-            pltpu.VMEM((1, nodes), I32),
             pltpu.VMEM(raw[0].shape, BF16),
             pltpu.VMEM(raw[1].shape, BF16),
             pltpu.SemaphoreType.DMA((len(operands),)),
@@ -615,18 +616,28 @@
     )(features, feature_arrived, mean_rows, mean_arrived, dense, weights)
     mean_hubs = gather_hubs(mean_arrived, [own_logits])
     half = CHIPS * GROUP_HUBS
-    own_turned, own_source, own_columns, part = kernel_call(
+    own_turned, own_source, own_columns, part, times = kernel_call(
         own_hub_part,
         (
             shape((2 * inputs, half), BF16),
             shape((half, width), BF16),
             shape((nodes, half), BF16),
             shape((nodes, width), F32),
+            shape((nodes, TILE), F32),
         ),
+        [
+            pltpu.VMEM(sample_ids.shape, I32),
+            pltpu.VMEM((1, nodes), I32),
+            pltpu.SemaphoreType.DMA((2,)),
+        ],
+        [VM] * 5 + [HBM] * 2,
         limit=6,
         flops=4 * nodes * half * width,
         moved=4 * MIB,
-    )(dense, weights, part, feature_hubs[0], mean_hubs[0])
+    )(
+        dense, weights, part, feature_hubs[0], mean_hubs[0],
+        *(pltpu.with_memory_space_constraint(operand, pltpu.HBM) for operand in (sample_ids, labels.reshape(1, nodes))),
+    )
     base, edge_rows, mine, theirs = kernel_call(
         functools.partial(main_part, samples_all, classes),
         (
@@ -646,7 +657,7 @@
         limit=20,
     )(
         early_turned, early_source, own_logits, own_turned, own_source, own_columns, part,
-        dense, numbers, weights, feature_hubs[1], mean_hubs[1],
+        dense, numbers, times, weights, feature_hubs[1], mean_hubs[1],
     )
     rows, *blocks = kernel_call(
         sum_cores, (shape((PEERS, BACK_ROWS, TILE), BF16),) + (shape((CHIP_HUBS, TILE), BF16),) * CHIPS

time: 131 us -> 131 us (level)
  transfers between devices with their start and end apart: 13 -> 13, of which waited for: 8 -> 7; matrix products, arithmetic and copies ran while one was open for 0% -> 0% of each run, Pallas kernels for 7% -> 7%
where the time goes in v9:
time: 131 us
  blocking collectives  79.9 us (61%)
  starting transfers between devices  24.2 us (18%)
  Pallas kernels  18.1 us (14%)
  waiting for transfers between devices  7.54 us (6%)
  between operations  1.41 us (1%)
    all_to_all x4, blocking collectives, swap(): lax.all_to_all(values, 'dev', split_axis=0, concat_axis=0, tiled=True)  79.9 us
    ppermute x4, starting transfers between devices, to_core(): lax.ppermute(values, 'grp', [(i, i ^ 1) for i in range(CHIPS * CORES)])  16.5 us
    ppermute x9, starting transfers between devices, along_x(): lax.ppermute(values, 'grp', [(i, (i + CORES * shift) % every) for i in ra...  7.74 us
    ppermute x9, waiting for transfers between devices, along_x(): lax.ppermute(values, 'grp', [(i, (i + CORES * shift) % every) for i in ra...  5.5 us
    pallas_call x1, Pallas kernels, on_device(): kernel_call(functools.partial(main_part, samples_all, classes), (shape((n...  4.38 us
    pallas_call x1, Pallas kernels, on_device(): kernel_call(build_dense, (shape((nodes, table), BF16), shape((nodes, TILE...  2.85 us
  transfers between devices with their start and end apart: 13, of which 7 were waited for; matrix products, arithmetic and copies ran while one was open for 0% of the time, Pallas kernels for 7%

profile of v9, /device:TPU:1, one launch (start us, length us, event | category | flops | bytes accessed | tf_op | source)
XLA Modules:
  0.0 131.1 jit_solution(6608920316523296291)
XLA Ops:
  0.6 1.7 %shard_map.189 = bf16[1280,128]{1,0:T(8,128)(2,1)S(1)} custom-call(bf16[512,128]{1,0:T(8,128)(2,1)} %features_ref.3, s32[1,32,32]{2,1,0:T(8,128)} %send_any.1, s32[1,32]{1,0:T(1,128)} %refs_5_.1, s32[1,4]{1,0:T(1,128)} %refs_6_.1), custom_call_target="tpu_custom_call" | custom-call | tf_op jit(solution)/shard_map/pallas_call | solution.py:541
  2.3 22.0 %all_to_all.20.refs_11_.arrived_ref.feature_arrived_ref = bf16[32,40,128]{2,1,0:T(8,128)(2,1)S(1)} all-to-all(bf16[32,40,128]{2,1,0:T(8,128)(2,1)S(1)} %bitcast.9), channel_id=1, replica_groups=mesh['grp'=8,'dev'=32] {'dev'}, dimensions={0} | all-to-all | bytes 655360 | tf_op jit(solution)/shard_map/all_to_all | solution.py:490
  24.3 2.5 %collective-permute-start.2 = (bf16[128,128]{1,0:T(8,128)(2,1)S(1)}, bf16[128,128]{1,0:T(8,128)(2,1)S(1)}, u32[]{:S(2)}, u32[]{:S(2)}) collective-permute-start(bf16[128,128]{1,0:T(8,128)(2,1)S(1)} %shard_map.191.refs_0_), channel_id=1, source_target_pairs={{0,192},{32,224},{64,0},{96,32},{128,64},{160,96},{192,128},{224,1... | collective-permute-start | bytes 98312 | tf_op jit(solution)/shard_map/ppermute | solution.py:499
  28.7 2.9 %shard_map.190 = (bf16[512,2560]{1,0:T(8,128)(2,1)S(1)}, f32[512,128]{1,0:T(8,128)S(1)}, bf16[768,512]{1,0:T(8,128)(2,1)S(1)}, s32[40,32]{1,0:T(8,128)S(1)}, bf16[1280,512]{1,0:T(8,128)(2,1)S(1)}) custom-call(bf16[32,128,128]{2,1,0:T(8,128)(2,1)} %refs_0_.1, s32[1,32]{1,0:T(1,128)} %refs_1_.1, s32[1,32]{1,0:T(1,128)} %refs_2_.1, s32[1]{0:T(128)S(6)} %copy.21.refs_3_, ...), custom_call_target="tpu_custom_call" | custom-call | flops 335544320 | bytes 8388608 | tf_op jit(solution)/shard_map/pallas_call | solution.py:559
  31.6 6.0 %collective-permute-start.3 = (bf16[512,128]{1,0:T(8,128)(2,1)S(1)}, bf16[512,128]{1,0:T(8,128)(2,1)S(1)}, u32[]{:S(2)}, u32[]{:S(2)}) collective-permute-start(bf16[512,128]{1,0:T(8,128)(2,1)S(1)} %shard_map.192.own_hub_ref.feature_ref), channel_id=1, source_target_pairs={{0,32},{32,0},{64,96},{96,64},{128,160},{160,128},{192,224},{224,1... | collective-permute-start | bytes 393224 | tf_op jit(solution)/shard_map/ppermute | solution.py:494
  37.5 0.9 shard_map.193.part_ref
  38.5 1.0 shard_map.194
  39.5 14.7 %all_to_all.21.arrived_ref = bf16[32,40,128]{2,1,0:T(8,128)(2,1)S(1)} all-to-all(bf16[32,40,128]{2,1,0:T(8,128)(2,1)S(1)} %bitcast.10), channel_id=1, replica_groups=mesh['grp'=8,'dev'=32] {'dev'}, dimensions={0} | all-to-all | bytes 655360 | tf_op jit(solution)/shard_map/all_to_all | solution.py:490
  54.2 1.2 collective-permute-start.6
  55.4 1.3 collective-permute-start.5
  56.7 1.6 %shard_map.195 = (bf16[512,512]{1,0:T(8,128)(2,1)}, bf16[256,1536]{1,0:T(8,128)(2,1)S(1)}, bf16[1536,512]{1,0:T(8,128)(2,1)S(1)}, f32[512,512]{1,0:T(8,128)S(1)}, f32[512,256]{1,0:T(8,128)S(1)}) custom-call(bf16[512,128]{1,0:T(8,128)(2,1)S(1)} %copy-done, bf16[32,40,128]{2,1,0:T(8,128)(2,1)S(1)} %all_to_all.20.refs_11_.arrived_ref.feature_arrived_ref, ...), custom_call_target="tpu_custom_call" | custom-call | flops 1610612736 | bytes 8388608 | tf_op jit(solution)/shard_map/pallas_call | solution.py:603
  58.3 1.4 %collective-permute-done.5.refs_2_ = bf16[128,128]{1,0:T(8,128)(2,1)S(1)} collective-permute-done((bf16[128,128]{1,0:T(8,128)(2,1)S(1)}, bf16[128,128]{1,0:T(8,128)(2,1)S(1)}, u32[]{:S(2)}, u32[]{:S(2)}) %collective-permute-start.5) | collective-permute-done | bytes 32800 | tf_op jit(solution)/shard_map/ppermute | solution.py:499
  59.7 1.0 collective-permute-done.4.refs_1_
  60.7 5.8 %collective-permute-start.7 = (bf16[512,128]{1,0:T(8,128)(2,1)S(1)}, bf16[512,128]{1,0:T(8,128)(2,1)S(1)}, u32[]{:S(2)}, u32[]{:S(2)}) collective-permute-start(bf16[512,128]{1,0:T(8,128)(2,1)S(1)} %shard_map.197.mean_ref), channel_id=1, source_target_pairs={{0,32},{32,0},{64,96},{96,64},{128,160},{160,128},{192,224},{224,1... | collective-permute-start | bytes 393224 | tf_op jit(solution)/shard_map/ppermute | solution.py:494
  66.5 1.3 %shard_map.198 = (bf16[256,512]{1,0:T(8,128)(2,1)S(1)}, bf16[512,512]{1,0:T(8,128)(2,1)S(1)}, bf16[512,512]{1,0:T(8,128)(2,1)S(1)}, f32[512,512]{1,0:T(8,128)S(1)}, f32[512,128]{1,0:T(8,128)S(1)}) custom-call(bf16[512,2560]{1,0:T(8,128)(2,1)S(1)} %get-tuple-element.42.dense_ref, bf16[768,512]{1,0:T(8,128)(2,1)S(1)} %get-tuple-element.47.weights_ref, ...), custom_call_target="tpu_custom_call" | custom-call | flops 536870912 | bytes 4194304 | tf_op jit(solution)/shard_map/pallas_call | solution.py:619
  67.9 4.4 %shard_map.199 = (f32[512,512]{1,0:T(8,128)S(1)}, bf16[32,48,128]{2,1,0:T(8,128)(2,1)S(1)}, bf16[2304,128]{1,0:T(8,128)(2,1)S(1)}, bf16[2304,128]{1,0:T(8,128)(2,1)S(1)}) custom-call(bf16[256,1536]{1,0:T(8,128)(2,1)S(1)} %get-tuple-element.49.early_turned_ref, bf16[1536,512]{1,0:T(8,128)(2,1)S(1)} %get-tuple-element.50.early_source_ref, ...), custom_call_target="tpu_custom_call" | custom-call | tf_op jit(solution)/shard_map/pallas_call | solution.py:641
  72.4 2.0 %collective-permute-done.8.arrived_ref = bf16[2304,128]{1,0:T(8,128)(2,1)S(1)} collective-permute-done((bf16[2304,128]{1,0:T(8,128)(2,1)S(1)}, bf16[2304,128]{1,0:T(8,128)(2,1)S(1)}, u32[]{:S(2)}, u32[]{:S(2)}) %collective-permute-start.8) | collective-permute-done | bytes 589856 | tf_op jit(solution)/shard_map/ppermute | solution.py:494
  74.5 22.5 %all_to_all.22.arrived_ref = bf16[32,88,128]{2,1,0:T(8,128)(2,1)S(1)} all-to-all(bf16[32,88,128]{2,1,0:T(8,128)(2,1)S(1)} %get-tuple-element.62), channel_id=1, replica_groups=mesh['grp'=8,'dev'=32] {'dev'}, dimensions={0} | all-to-all | bytes 1441792 | tf_op jit(solution)/shard_map/all_to_all | solution.py:490
  98.6 1.3 %shard_map.201.refs_3_.base_ref = f32[512,512]{1,0:T(8,128)S(1)} custom-call(f32[512,512]{1,0:T(8,128)S(1)} %get-tuple-element.58.base_ref, bf16[32,88,128]{2,1,0:T(8,128)(2,1)S(1)} %all_to_all.22.arrived_ref, s32[40,32]{1,0:T(8,128)S(1)} %get-tuple-element.63.wanted_ref, bf16[768,512]{1,0:T(8,128)(2,1)S(1)} %get-tuple-element.47.weights_ref), custom_call_target="tpu_custom_call" | custom-call | flops 402653184 | bytes 4194304 | tf_op jit(solution)/shard_map/pallas_call | solution.py:670
  100.7 1.6 %collective-permute-done.10.refs_1_ = bf16[336,128]{1,0:T(8,128)(2,1)S(1)} collective-permute-done((bf16[336,128]{1,0:T(8,128)(2,1)S(1)}, bf16[336,128]{1,0:T(8,128)(2,1)S(1)}, u32[]{:S(2)}, u32[]{:S(2)}) %collective-permute-start.10) | collective-permute-done | bytes 86048 | tf_op jit(solution)/shard_map/ppermute | solution.py:499
  103.2 20.6 %all_to_all.23.arrived_ref.mine_ref = bf16[32,48,128]{2,1,0:T(8,128)(2,1)S(1)} all-to-all(bf16[32,48,128]{2,1,0:T(8,128)(2,1)S(1)} %shard_map.203), channel_id=1, replica_groups=mesh['grp'=8,'dev'=32] {'dev'}, dimensions={0} | all-to-all | bytes 786432 | tf_op jit(solution)/shard_map/all_to_all | solution.py:490
  123.8 4.6 %collective-permute-start.12 = (bf16[32,48,128]{2,1,0:T(8,128)(2,1)S(1)}, bf16[32,48,128]{2,1,0:T(8,128)(2,1)S(1)}, u32[]{:S(2)}, u32[]{:S(2)}) collective-permute-start(bf16[32,48,128]{2,1,0:T(8,128)(2,1)S(1)} %all_to_all.23.arrived_ref.mine_ref), channel_id=1, source_target_pairs={{0,32},{32,0},{64,96},{96,64},{128,160},{160,128},{192,224},{224,1... | collective-permute-start | bytes 1179656 | tf_op jit(solution)/shard_map/ppermute | solution.py:494
  128.4 1.5 %shard_map.204 = f32[512,512]{1,0:T(8,128)} custom-call(f32[512,512]{1,0:T(8,128)S(1)} %shard_map.201.refs_3_.base_ref, bf16[32,48,128]{2,1,0:T(8,128)(2,1)S(1)} %all_to_all.23.arrived_ref.mine_ref, s32[40,32]{1,0:T(8,128)S(1)} %get-tuple-element.63.wanted_ref, bf16[768,512]{1,0:T(8,128)(2,1)S(1)} %get-tuple-element.47.weights_ref), custom_call_target="tpu_custom_call" | custom-call | flops 268435456 | bytes 4194304 | tf_op jit(solution)/shard_map/pallas_call | solution.py:684
  130.0 1.1 shard_map.205
  (25 shorter events, 4.8 us)
Async XLA Ops:
  24.3 13.2 %copy-start = (bf16[512,128]{1,0:T(8,128)(2,1)S(1)}, bf16[512,128]{1,0:T(8,128)(2,1)}, u32[]{:S(2)}) copy-start(bf16[512,128]{1,0:T(8,128)(2,1)} %features_ref.3) | copy-start | bytes 393220
  24.3 7.2 %collective-permute-start.2 = (bf16[128,128]{1,0:T(8,128)(2,1)S(1)}, bf16[128,128]{1,0:T(8,128)(2,1)S(1)}, u32[]{:S(2)}, u32[]{:S(2)}) collective-permute-start(bf16[128,128]{1,0:T(8,128)(2,1)S(1)} %shard_map.191.refs_0_), channel_id=1, source_target_pairs={{0,192},{32,224},{64,0},{96,32},{128,64},{160,96},{192,128},{224,1... | collective-permute-start | bytes 98312 | tf_op jit(solution)/shard_map/ppermute | solution.py:499
  26.9 4.7 %collective-permute-start.1 = (bf16[128,128]{1,0:T(8,128)(2,1)S(1)}, bf16[128,128]{1,0:T(8,128)(2,1)S(1)}, u32[]{:S(2)}, u32[]{:S(2)}) collective-permute-start(bf16[128,128]{1,0:T(8,128)(2,1)S(1)} %shard_map.191.refs_0_), channel_id=1, source_target_pairs={{0,128},{32,160},{64,192},{96,224},{128,0},{160,32},{192,64},{224,... | collective-permute-start | bytes 98312 | tf_op jit(solution)/shard_map/ppermute | solution.py:499
  27.4 4.1 %collective-permute-start = (bf16[128,128]{1,0:T(8,128)(2,1)S(1)}, bf16[128,128]{1,0:T(8,128)(2,1)S(1)}, u32[]{:S(2)}, u32[]{:S(2)}) collective-permute-start(bf16[128,128]{1,0:T(8,128)(2,1)S(1)} %shard_map.191.refs_0_), channel_id=1, source_target_pairs={{0,64},{32,96},{64,128},{96,160},{128,192},{160,224},{192,0},{224,... | collective-permute-start | bytes 98312 | tf_op jit(solution)/shard_map/ppermute | solution.py:499
  31.6 6.9 %collective-permute-start.3 = (bf16[512,128]{1,0:T(8,128)(2,1)S(1)}, bf16[512,128]{1,0:T(8,128)(2,1)S(1)}, u32[]{:S(2)}, u32[]{:S(2)}) collective-permute-start(bf16[512,128]{1,0:T(8,128)(2,1)S(1)} %shard_map.192.own_hub_ref.feature_ref), channel_id=1, source_target_pairs={{0,32},{32,0},{64,96},{96,64},{128,160},{160,128},{192,224},{224,1... | collective-permute-start | bytes 393224 | tf_op jit(solution)/shard_map/ppermute | solution.py:494
  54.2 4.1 %collective-permute-start.6 = (bf16[128,128]{1,0:T(8,128)(2,1)S(1)}, bf16[128,128]{1,0:T(8,128)(2,1)S(1)}, u32[]{:S(2)}, u32[]{:S(2)}) collective-permute-start(bf16[128,128]{1,0:T(8,128)(2,1)S(1)} %shard_map.196.refs_0_), channel_id=1, source_target_pairs={{0,192},{32,224},{64,0},{96,32},{128,64},{160,96},{192,128},{224,1... | collective-permute-start | bytes 98312 | tf_op jit(solution)/shard_map/ppermute | solution.py:499
  55.4 4.3 %collective-permute-start.5 = (bf16[128,128]{1,0:T(8,128)(2,1)S(1)}, bf16[128,128]{1,0:T(8,128)(2,1)S(1)}, u32[]{:S(2)}, u32[]{:S(2)}) collective-permute-start(bf16[128,128]{1,0:T(8,128)(2,1)S(1)} %shard_map.196.refs_0_), channel_id=1, source_target_pairs={{0,128},{32,160},{64,192},{96,224},{128,0},{160,32},{192,64},{224,... | collective-permute-start | bytes 98312 | tf_op jit(solution)/shard_map/ppermute | solution.py:499
  56.7 4.0 %collective-permute-start.4 = (bf16[128,128]{1,0:T(8,128)(2,1)S(1)}, bf16[128,128]{1,0:T(8,128)(2,1)S(1)}, u32[]{:S(2)}, u32[]{:S(2)}) collective-permute-start(bf16[128,128]{1,0:T(8,128)(2,1)S(1)} %shard_map.196.refs_0_), channel_id=1, source_target_pairs={{0,64},{32,96},{64,128},{96,160},{128,192},{160,224},{192,0},{224,... | collective-permute-start | bytes 98312 | tf_op jit(solution)/shard_map/ppermute | solution.py:499
  60.7 7.1 %collective-permute-start.7 = (bf16[512,128]{1,0:T(8,128)(2,1)S(1)}, bf16[512,128]{1,0:T(8,128)(2,1)S(1)}, u32[]{:S(2)}, u32[]{:S(2)}) collective-permute-start(bf16[512,128]{1,0:T(8,128)(2,1)S(1)} %shard_map.197.mean_ref), channel_id=1, source_target_pairs={{0,32},{32,0},{64,96},{96,64},{128,160},{160,128},{192,224},{224,1... | collective-permute-start | bytes 393224 | tf_op jit(solution)/shard_map/ppermute | solution.py:494
  72.2 2.1 %collective-permute-start.8 = (bf16[2304,128]{1,0:T(8,128)(2,1)S(1)}, bf16[2304,128]{1,0:T(8,128)(2,1)S(1)}, u32[]{:S(2)}, u32[]{:S(2)}) collective-permute-start(bf16[2304,128]{1,0:T(8,128)(2,1)S(1)} %get-tuple-element.60), channel_id=1, source_target_pairs={{0,32},{32,0},{64,96},{96,64},{128,160},{160,128},{192,224},{224,1... | collective-permute-start | bytes 1769480 | tf_op jit(solution)/shard_map/ppermute | solution.py:494
  97.1 3.6 %collective-permute-start.9 = (bf16[336,128]{1,0:T(8,128)(2,1)S(1)}, bf16[336,128]{1,0:T(8,128)(2,1)S(1)}, u32[]{:S(2)}, u32[]{:S(2)}) collective-permute-start(bf16[336,128]{1,0:T(8,128)(2,1)S(1)} %get-tuple-element.69), channel_id=1, source_target_pairs={{0,192},{32,224},{64,0},{96,32},{128,64},{160,96},{192,128},{224,1... | collective-permute-start | bytes 258056 | tf_op jit(solution)/shard_map/ppermute | solution.py:499
  97.4 4.9 %collective-permute-start.10 = (bf16[336,128]{1,0:T(8,128)(2,1)S(1)}, bf16[336,128]{1,0:T(8,128)(2,1)S(1)}, u32[]{:S(2)}, u32[]{:S(2)}) collective-permute-start(bf16[336,128]{1,0:T(8,128)(2,1)S(1)} %get-tuple-element.70), channel_id=1, source_target_pairs={{0,128},{32,160},{64,192},{96,224},{128,0},{160,32},{192,64},{224,... | collective-permute-start | bytes 258056 | tf_op jit(solution)/shard_map/ppermute | solution.py:499
  98.0 5.1 %collective-permute-start.11 = (bf16[336,128]{1,0:T(8,128)(2,1)S(1)}, bf16[336,128]{1,0:T(8,128)(2,1)S(1)}, u32[]{:S(2)}, u32[]{:S(2)}) collective-permute-start(bf16[336,128]{1,0:T(8,128)(2,1)S(1)} %get-tuple-element.71), channel_id=1, source_target_pairs={{0,64},{32,96},{64,128},{96,160},{128,192},{160,224},{192,0},{224,... | collective-permute-start | bytes 258056 | tf_op jit(solution)/shard_map/ppermute | solution.py:499
  123.8 6.2 %collective-permute-start.12 = (bf16[32,48,128]{2,1,0:T(8,128)(2,1)S(1)}, bf16[32,48,128]{2,1,0:T(8,128)(2,1)S(1)}, u32[]{:S(2)}, u32[]{:S(2)}) collective-permute-start(bf16[32,48,128]{2,1,0:T(8,128)(2,1)S(1)} %all_to_all.23.arrived_ref.mine_ref), channel_id=1, source_target_pairs={{0,32},{32,0},{64,96},{96,64},{128,160},{160,128},{192,224},{224,1... | collective-permute-start | bytes 1179656 | tf_op jit(solution)/shard_map/ppermute | solution.py:494

commit v10 on v9

--- a/solution.py
+++ b/solution.py
@@ -227,9 +227,10 @@
 
 
 def early_part(
-    features_ref, feature_arrived_ref, mean_ref, arrived_ref, dense_ref, weights_ref,
-    hidden_ref, turned_ref, source_ref, part_ref, logits_ref, table_ref,
+    features_ref, feature_arrived_ref, mean_ref, arrived_ref, dense_ref, weights_ref, sample_any, label_any,
+    hidden_ref, turned_ref, source_ref, part_ref, logits_ref, times_ref, table_ref, sample_ref, label_ref, sems,
 ):
+    loads = fetch(((sample_any, sample_ref), (label_any, label_ref)), sems)
     nodes, width = hidden_ref.shape
     edges = PEERS * CAPACITY
     edge_at = dense_ref.shape[1] - edges
@@ -248,6 +249,12 @@
     hidden_ref[...] = hidden
     part_ref[...] = nn(dense_ref[:, 0:nodes], hidden) + nn(dense_ref[:, edge_at:], source_ref[nodes:, :])
     logits_ref[...] = nt(hidden, weights_ref[SELF_AT : 2 * SELF_AT, :])
+    for load in loads:
+        load.wait()
+    node = iota((nodes, sample_ref.shape[1]), 0)
+    times = jnp.sum(jnp.where(node == sample_ref[...], 1.0, 0.0), axis=1, keepdims=True)
+    label = jnp.transpose(jnp.broadcast_to(label_ref[...], (8, nodes)))[:, 0:1]
+    times_ref[...] = jnp.where(iota(times_ref.shape, 1) == 0, times, label.astype(F32))
 
 
 def hub_part(
@@ -267,21 +274,12 @@
 
 
 def own_hub_part(
-    dense_ref, weights_ref, part_ref, feature_ref, mean_ref, sample_any, label_any,
-    turned_ref, source_ref, columns_ref, out_ref, times_ref, sample_ref, label_ref, sems,
+    dense_ref, weights_ref, part_ref, feature_ref, mean_ref, turned_ref, source_ref, columns_ref, out_ref
 ):
-    loads = fetch(((sample_any, sample_ref), (label_any, label_ref)), sems)
     total = hub_part(
         dense_ref, weights_ref, feature_ref[...], mean_ref[...], False, turned_ref, source_ref, columns_ref
     )
     out_ref[...] = part_ref[...] + total
-    for load in loads:
-        load.wait()
-    nodes = dense_ref.shape[0]
-    node = iota((nodes, sample_ref.shape[1]), 0)
-    times = jnp.sum(jnp.where(node == sample_ref[...], 1.0, 0.0), axis=1, keepdims=True)
-    label = jnp.transpose(jnp.broadcast_to(label_ref[...], (8, nodes)))[:, 0:1]
-    times_ref[...] = jnp.where(iota(times_ref.shape, 1) == 0, times, label.astype(F32))
 
 
 def main_part(
@@ -600,7 +598,7 @@
     )(part, dense, numbers, picks, feature_hubs[1])
     mean_arrived = swap(rows.reshape(PEERS, FORWARD_ROWS, inputs))
 
-    hidden, early_turned, early_source, part, own_logits = kernel_call(
+    hidden, early_turned, early_source, part, own_logits, times = kernel_call(
         early_part,
         (
             shape((nodes, width), BF16),
@@ -608,36 +606,36 @@
             shape((nodes + edges, width), BF16),
             shape((nodes, width), F32),
             shape((nodes, padded), F32),
+            shape((nodes, TILE), F32),
         ),
-        [pltpu.VMEM((nodes + edges, 2 * inputs), BF16)],
+        [
+            pltpu.VMEM((nodes + edges, 2 * inputs), BF16),
+            pltpu.VMEM(sample_ids.shape, I32),
+            pltpu.VMEM((1, nodes), I32),
+            pltpu.SemaphoreType.DMA((2,)),
+        ],
+        [VM] * 6 + [HBM] * 2,
         limit=8,
         flops=6 * nodes * edges * width,
         moved=8 * MIB,
-    )(features, feature_arrived, mean_rows, mean_arrived, dense, weights)
+    )(
+        features, feature_arrived, mean_rows, mean_arrived, dense, weights,
+        *(pltpu.with_memory_space_constraint(operand, pltpu.HBM) for operand in (sample_ids, labels.reshape(1, nodes))),
+    )
     mean_hubs = gather_hubs(mean_arrived, [own_logits])
     half = CHIPS * GROUP_HUBS
-    own_turned, own_source, own_columns, part, times = kernel_call(
+    own_turned, own_source, own_columns, part = kernel_call(
         own_hub_part,
         (
             shape((2 * inputs, half), BF16),
             shape((half, width), BF16),
             shape((nodes, half), BF16),
             shape((nodes, width), F32),
-            shape((nodes, TILE), F32),
         ),
-        [
-            pltpu.VMEM(sample_ids.shape, I32),
-            pltpu.VMEM((1, nodes), I32),
-            pltpu.SemaphoreType.DMA((2,)),
-        ],
-        [VM] * 5 + [HBM] * 2,
         limit=6,
         flops=4 * nodes * half * width,
         moved=4 * MIB,
-    )(
-        dense, weights, part, feature_hubs[0], mean_hubs[0],
-        *(pltpu.with_memory_space_constraint(operand, pltpu.HBM) for operand in (sample_ids, labels.reshape(1, nodes))),
-    )
+    )(dense, weights, part, feature_hubs[0], mean_hubs[0])
     base, edge_rows, mine, theirs = kernel_call(
         functools.partial(main_part, samples_all, classes),
         (

time: 131 us -> 131 us (level)
  transfers between devices with their start and end apart: 13 -> 13, of which waited for: 7 -> 9; matrix products, arithmetic and copies ran while one was open for 0% -> 0% of each run, Pallas kernels for 7% -> 7%
where the time goes in v10:
time: 131 us
  blocking collectives  80.1 us (61%)
  starting transfers between devices  24.5 us (19%)
  Pallas kernels  18.1 us (14%)
  waiting for transfers between devices  6.88 us (5%)
  between operations  1.39 us (1%)
    all_to_all x4, blocking collectives, swap(): lax.all_to_all(values, 'dev', split_axis=0, concat_axis=0, tiled=True)  80.1 us
    ppermute x4, starting transfers between devices, to_core(): lax.ppermute(values, 'grp', [(i, i ^ 1) for i in range(CHIPS * CORES)])  16.7 us
    ppermute x9, starting transfers between devices, along_x(): lax.ppermute(values, 'grp', [(i, (i + CORES * shift) % every) for i in ra...  7.81 us
    ppermute x9, waiting for transfers between devices, along_x(): lax.ppermute(values, 'grp', [(i, (i + CORES * shift) % every) for i in ra...  4.88 us
    pallas_call x1, Pallas kernels, on_device(): kernel_call(functools.partial(main_part, samples_all, classes), (shape((n...  4.38 us
    pallas_call x1, Pallas kernels, on_device(): kernel_call(build_dense, (shape((nodes, table), BF16), shape((nodes, TILE...  2.71 us
  transfers between devices with their start and end apart: 13, of which 9 were waited for; matrix products, arithmetic and copies ran while one was open for 0% of the time, Pallas kernels for 7%

profile of v10, /device:TPU:1, one launch (start us, length us, event | category | flops | bytes accessed | tf_op | source)
XLA Modules:
  0.0 131.0 jit_solution(4405074997450468566)
XLA Ops:
  0.6 1.7 %shard_map.189 = bf16[1280,128]{1,0:T(8,128)(2,1)S(1)} custom-call(bf16[512,128]{1,0:T(8,128)(2,1)} %features_ref.3, s32[1,32,32]{2,1,0:T(8,128)} %send_any.1, s32[1,32]{1,0:T(1,128)} %refs_5_.1, s32[1,4]{1,0:T(1,128)} %refs_6_.1), custom_call_target="tpu_custom_call" | custom-call | tf_op jit(solution)/shard_map/pallas_call | solution.py:539
  2.3 22.0 %all_to_all.20.refs_11_.arrived_ref.feature_arrived_ref = bf16[32,40,128]{2,1,0:T(8,128)(2,1)S(1)} all-to-all(bf16[32,40,128]{2,1,0:T(8,128)(2,1)S(1)} %bitcast.9), channel_id=1, replica_groups=mesh['grp'=8,'dev'=32] {'dev'}, dimensions={0} | all-to-all | bytes 655360 | tf_op jit(solution)/shard_map/all_to_all | solution.py:488
  24.3 2.5 %collective-permute-start.2 = (bf16[128,128]{1,0:T(8,128)(2,1)S(1)}, bf16[128,128]{1,0:T(8,128)(2,1)S(1)}, u32[]{:S(2)}, u32[]{:S(2)}) collective-permute-start(bf16[128,128]{1,0:T(8,128)(2,1)S(1)} %shard_map.191.refs_0_), channel_id=1, source_target_pairs={{0,192},{32,224},{64,0},{96,32},{128,64},{160,96},{192,128},{224,1... | collective-permute-start | bytes 98312 | tf_op jit(solution)/shard_map/ppermute | solution.py:497
  28.7 2.7 %shard_map.190 = (bf16[512,2560]{1,0:T(8,128)(2,1)S(1)}, f32[512,128]{1,0:T(8,128)S(1)}, bf16[768,512]{1,0:T(8,128)(2,1)S(1)}, s32[40,32]{1,0:T(8,128)S(1)}, bf16[1280,512]{1,0:T(8,128)(2,1)S(1)}) custom-call(bf16[32,128,128]{2,1,0:T(8,128)(2,1)} %refs_0_.1, s32[1,32]{1,0:T(1,128)} %refs_1_.1, s32[1,32]{1,0:T(1,128)} %refs_2_.1, s32[1]{0:T(128)S(6)} %copy.21.refs_3_, ...), custom_call_target="tpu_custom_call" | custom-call | flops 335544320 | bytes 8388608 | tf_op jit(solution)/shard_map/pallas_call | solution.py:557
  31.5 6.0 %collective-permute-start.3 = (bf16[512,128]{1,0:T(8,128)(2,1)S(1)}, bf16[512,128]{1,0:T(8,128)(2,1)S(1)}, u32[]{:S(2)}, u32[]{:S(2)}) collective-permute-start(bf16[512,128]{1,0:T(8,128)(2,1)S(1)} %shard_map.192.own_hub_ref.feature_ref), channel_id=1, source_target_pairs={{0,32},{32,0},{64,96},{96,64},{128,160},{160,128},{192,224},{224,1... | collective-permute-start | bytes 393224 | tf_op jit(solution)/shard_map/ppermute | solution.py:492
  37.5 0.9 shard_map.193.part_ref
  38.5 1.0 shard_map.194
  39.5 14.7 %all_to_all.21.arrived_ref = bf16[32,40,128]{2,1,0:T(8,128)(2,1)S(1)} all-to-all(bf16[32,40,128]{2,1,0:T(8,128)(2,1)S(1)} %bitcast.10), channel_id=1, replica_groups=mesh['grp'=8,'dev'=32] {'dev'}, dimensions={0} | all-to-all | bytes 655360 | tf_op jit(solution)/shard_map/all_to_all | solution.py:488
  54.2 1.4 %collective-permute-start.6 = (bf16[128,128]{1,0:T(8,128)(2,1)S(1)}, bf16[128,128]{1,0:T(8,128)(2,1)S(1)}, u32[]{:S(2)}, u32[]{:S(2)}) collective-permute-start(bf16[128,128]{1,0:T(8,128)(2,1)S(1)} %shard_map.196.refs_0_), channel_id=1, source_target_pairs={{0,192},{32,224},{64,0},{96,32},{128,64},{160,96},{192,128},{224,1... | collective-permute-start | bytes 98312 | tf_op jit(solution)/shard_map/ppermute | solution.py:497
  55.6 1.2 collective-permute-start.5
  56.8 2.4 %shard_map.195 = (bf16[512,512]{1,0:T(8,128)(2,1)}, bf16[256,1536]{1,0:T(8,128)(2,1)S(1)}, bf16[1536,512]{1,0:T(8,128)(2,1)S(1)}, f32[512,512]{1,0:T(8,128)S(1)}...) custom-call(bf16[512,128]{1,0:T(8,128)(2,1)S(1)} %copy-done, ...), custom_call_target="tpu_custom_call" | custom-call | flops 1610612736 | bytes 8388608 | tf_op jit(solution)/shard_map/pallas_call | solution.py:601
  59.9 0.9 collective-permute-done.4.refs_1_
  60.8 5.8 %collective-permute-start.7 = (bf16[512,128]{1,0:T(8,128)(2,1)S(1)}, bf16[512,128]{1,0:T(8,128)(2,1)S(1)}, u32[]{:S(2)}, u32[]{:S(2)}) collective-permute-start(bf16[512,128]{1,0:T(8,128)(2,1)S(1)} %shard_map.197.mean_ref), channel_id=1, source_target_pairs={{0,32},{32,0},{64,96},{96,64},{128,160},{160,128},{192,224},{224,1... | collective-permute-start | bytes 393224 | tf_op jit(solution)/shard_map/ppermute | solution.py:492
  67.5 4.4 %shard_map.199 = (f32[512,512]{1,0:T(8,128)S(1)}, bf16[32,48,128]{2,1,0:T(8,128)(2,1)S(1)}, bf16[2304,128]{1,0:T(8,128)(2,1)S(1)}, bf16[2304,128]{1,0:T(8,128)(2,1)S(1)}) custom-call(bf16[256,1536]{1,0:T(8,128)(2,1)S(1)} %get-tuple-element.49.early_turned_ref, bf16[1536,512]{1,0:T(8,128)(2,1)S(1)} %get-tuple-element.50.early_source_ref, ...), custom_call_target="tpu_custom_call" | custom-call | tf_op jit(solution)/shard_map/pallas_call | solution.py:639
  72.4 1.6 %collective-permute-done.8.arrived_ref = bf16[2304,128]{1,0:T(8,128)(2,1)S(1)} collective-permute-done((bf16[2304,128]{1,0:T(8,128)(2,1)S(1)}, bf16[2304,128]{1,0:T(8,128)(2,1)S(1)}, u32[]{:S(2)}, u32[]{:S(2)}) %collective-permute-start.8) | collective-permute-done | bytes 589856 | tf_op jit(solution)/shard_map/ppermute | solution.py:492
  74.2 22.2 %all_to_all.22.arrived_ref = bf16[32,88,128]{2,1,0:T(8,128)(2,1)S(1)} all-to-all(bf16[32,88,128]{2,1,0:T(8,128)(2,1)S(1)} %get-tuple-element.62), channel_id=1, replica_groups=mesh['grp'=8,'dev'=32] {'dev'}, dimensions={0} | all-to-all | bytes 1441792 | tf_op jit(solution)/shard_map/all_to_all | solution.py:488
  98.0 1.3 %shard_map.201.refs_3_.base_ref = f32[512,512]{1,0:T(8,128)S(1)} custom-call(f32[512,512]{1,0:T(8,128)S(1)} %get-tuple-element.58.base_ref, bf16[32,88,128]{2,1,0:T(8,128)(2,1)S(1)} %all_to_all.22.arrived_ref, s32[40,32]{1,0:T(8,128)S(1)} %get-tuple-element.63.wanted_ref, bf16[768,512]{1,0:T(8,128)(2,1)S(1)} %get-tuple-element.47.weights_ref), custom_call_target="tpu_custom_call" | custom-call | flops 402653184 | bytes 4194304 | tf_op jit(solution)/shard_map/pallas_call | solution.py:668
  99.4 0.8 collective-permute-done.9.refs_0_
  100.2 1.5 %collective-permute-done.10.refs_1_ = bf16[336,128]{1,0:T(8,128)(2,1)S(1)} collective-permute-done((bf16[336,128]{1,0:T(8,128)(2,1)S(1)}, bf16[336,128]{1,0:T(8,128)(2,1)S(1)}, u32[]{:S(2)}, u32[]{:S(2)}) %collective-permute-start.10) | collective-permute-done | bytes 86048 | tf_op jit(solution)/shard_map/ppermute | solution.py:497
  101.7 0.9 collective-permute-done.11.refs_2_
  102.7 21.2 %all_to_all.23.arrived_ref.mine_ref = bf16[32,48,128]{2,1,0:T(8,128)(2,1)S(1)} all-to-all(bf16[32,48,128]{2,1,0:T(8,128)(2,1)S(1)} %shard_map.203), channel_id=1, replica_groups=mesh['grp'=8,'dev'=32] {'dev'}, dimensions={0} | all-to-all | bytes 786432 | tf_op jit(solution)/shard_map/all_to_all | solution.py:488
  123.9 4.4 %collective-permute-start.12 = (bf16[32,48,128]{2,1,0:T(8,128)(2,1)S(1)}, bf16[32,48,128]{2,1,0:T(8,128)(2,1)S(1)}, u32[]{:S(2)}, u32[]{:S(2)}) collective-permute-start(bf16[32,48,128]{2,1,0:T(8,128)(2,1)S(1)} %all_to_all.23.arrived_ref.mine_ref), channel_id=1, source_target_pairs={{0,32},{32,0},{64,96},{96,64},{128,160},{160,128},{192,224},{224,1... | collective-permute-start | bytes 1179656 | tf_op jit(solution)/shard_map/ppermute | solution.py:492
  128.3 1.5 %shard_map.204 = f32[512,512]{1,0:T(8,128)} custom-call(f32[512,512]{1,0:T(8,128)S(1)} %shard_map.201.refs_3_.base_ref, bf16[32,48,128]{2,1,0:T(8,128)(2,1)S(1)} %all_to_all.23.arrived_ref.mine_ref, s32[40,32]{1,0:T(8,128)S(1)} %get-tuple-element.63.wanted_ref, bf16[768,512]{1,0:T(8,128)(2,1)S(1)} %get-tuple-element.47.weights_ref), custom_call_target="tpu_custom_call" | custom-call | flops 268435456 | bytes 4194304 | tf_op jit(solution)/shard_map/pallas_call | solution.py:682
  129.9 1.1 shard_map.205
  (25 shorter events, 5.3 us)
Async XLA Ops:
  24.3 13.2 %copy-start = (bf16[512,128]{1,0:T(8,128)(2,1)S(1)}, bf16[512,128]{1,0:T(8,128)(2,1)}, u32[]{:S(2)}) copy-start(bf16[512,128]{1,0:T(8,128)(2,1)} %features_ref.3) | copy-start | bytes 393220
  24.3 7.1 %collective-permute-start.2 = (bf16[128,128]{1,0:T(8,128)(2,1)S(1)}, bf16[128,128]{1,0:T(8,128)(2,1)S(1)}, u32[]{:S(2)}, u32[]{:S(2)}) collective-permute-start(bf16[128,128]{1,0:T(8,128)(2,1)S(1)} %shard_map.191.refs_0_), channel_id=1, source_target_pairs={{0,192},{32,224},{64,0},{96,32},{128,64},{160,96},{192,128},{224,1... | collective-permute-start | bytes 98312 | tf_op jit(solution)/shard_map/ppermute | solution.py:497
  26.9 4.5 %collective-permute-start.1 = (bf16[128,128]{1,0:T(8,128)(2,1)S(1)}, bf16[128,128]{1,0:T(8,128)(2,1)S(1)}, u32[]{:S(2)}, u32[]{:S(2)}) collective-permute-start(bf16[128,128]{1,0:T(8,128)(2,1)S(1)} %shard_map.191.refs_0_), channel_id=1, source_target_pairs={{0,128},{32,160},{64,192},{96,224},{128,0},{160,32},{192,64},{224,... | collective-permute-start | bytes 98312 | tf_op jit(solution)/shard_map/ppermute | solution.py:497
  27.4 4.1 %collective-permute-start = (bf16[128,128]{1,0:T(8,128)(2,1)S(1)}, bf16[128,128]{1,0:T(8,128)(2,1)S(1)}, u32[]{:S(2)}, u32[]{:S(2)}) collective-permute-start(bf16[128,128]{1,0:T(8,128)(2,1)S(1)} %shard_map.191.refs_0_), channel_id=1, source_target_pairs={{0,64},{32,96},{64,128},{96,160},{128,192},{160,224},{192,0},{224,... | collective-permute-start | bytes 98312 | tf_op jit(solution)/shard_map/ppermute | solution.py:497
  31.5 7.0 %collective-permute-start.3 = (bf16[512,128]{1,0:T(8,128)(2,1)S(1)}, bf16[512,128]{1,0:T(8,128)(2,1)S(1)}, u32[]{:S(2)}, u32[]{:S(2)}) collective-permute-start(bf16[512,128]{1,0:T(8,128)(2,1)S(1)} %shard_map.192.own_hub_ref.feature_ref), channel_id=1, source_target_pairs={{0,32},{32,0},{64,96},{96,64},{128,160},{160,128},{192,224},{224,1... | collective-permute-start | bytes 393224 | tf_op jit(solution)/shard_map/ppermute | solution.py:492
  54.2 5.0 %collective-permute-start.6 = (bf16[128,128]{1,0:T(8,128)(2,1)S(1)}, bf16[128,128]{1,0:T(8,128)(2,1)S(1)}, u32[]{:S(2)}, u32[]{:S(2)}) collective-permute-start(bf16[128,128]{1,0:T(8,128)(2,1)S(1)} %shard_map.196.refs_0_), channel_id=1, source_target_pairs={{0,192},{32,224},{64,0},{96,32},{128,64},{160,96},{192,128},{224,1... | collective-permute-start | bytes 98312 | tf_op jit(solution)/shard_map/ppermute | solution.py:497
  55.6 4.3 %collective-permute-start.5 = (bf16[128,128]{1,0:T(8,128)(2,1)S(1)}, bf16[128,128]{1,0:T(8,128)(2,1)S(1)}, u32[]{:S(2)}, u32[]{:S(2)}) collective-permute-start(bf16[128,128]{1,0:T(8,128)(2,1)S(1)} %shard_map.196.refs_0_), channel_id=1, source_target_pairs={{0,128},{32,160},{64,192},{96,224},{128,0},{160,32},{192,64},{224,... | collective-permute-start | bytes 98312 | tf_op jit(solution)/shard_map/ppermute | solution.py:497
  56.8 4.0 %collective-permute-start.4 = (bf16[128,128]{1,0:T(8,128)(2,1)S(1)}, bf16[128,128]{1,0:T(8,128)(2,1)S(1)}, u32[]{:S(2)}, u32[]{:S(2)}) collective-permute-start(bf16[128,128]{1,0:T(8,128)(2,1)S(1)} %shard_map.196.refs_0_), channel_id=1, source_target_pairs={{0,64},{32,96},{64,128},{96,160},{128,192},{160,224},{192,0},{224,... | collective-permute-start | bytes 98312 | tf_op jit(solution)/shard_map/ppermute | solution.py:497
  60.8 6.8 %collective-permute-start.7 = (bf16[512,128]{1,0:T(8,128)(2,1)S(1)}, bf16[512,128]{1,0:T(8,128)(2,1)S(1)}, u32[]{:S(2)}, u32[]{:S(2)}) collective-permute-start(bf16[512,128]{1,0:T(8,128)(2,1)S(1)} %shard_map.197.mean_ref), channel_id=1, source_target_pairs={{0,32},{32,0},{64,96},{96,64},{128,160},{160,128},{192,224},{224,1... | collective-permute-start | bytes 393224 | tf_op jit(solution)/shard_map/ppermute | solution.py:492
  71.9 2.1 %collective-permute-start.8 = (bf16[2304,128]{1,0:T(8,128)(2,1)S(1)}, bf16[2304,128]{1,0:T(8,128)(2,1)S(1)}, u32[]{:S(2)}, u32[]{:S(2)}) collective-permute-start(bf16[2304,128]{1,0:T(8,128)(2,1)S(1)} %get-tuple-element.60), channel_id=1, source_target_pairs={{0,32},{32,0},{64,96},{96,64},{128,160},{160,128},{192,224},{224,1... | collective-permute-start | bytes 1769480 | tf_op jit(solution)/shard_map/ppermute | solution.py:492
  96.5 3.7 %collective-permute-start.9 = (bf16[336,128]{1,0:T(8,128)(2,1)S(1)}, bf16[336,128]{1,0:T(8,128)(2,1)S(1)}, u32[]{:S(2)}, u32[]{:S(2)}) collective-permute-start(bf16[336,128]{1,0:T(8,128)(2,1)S(1)} %get-tuple-element.69), channel_id=1, source_target_pairs={{0,192},{32,224},{64,0},{96,32},{128,64},{160,96},{192,128},{224,1... | collective-permute-start | bytes 258056 | tf_op jit(solution)/shard_map/ppermute | solution.py:497
  96.9 4.9 %collective-permute-start.10 = (bf16[336,128]{1,0:T(8,128)(2,1)S(1)}, bf16[336,128]{1,0:T(8,128)(2,1)S(1)}, u32[]{:S(2)}, u32[]{:S(2)}) collective-permute-start(bf16[336,128]{1,0:T(8,128)(2,1)S(1)} %get-tuple-element.70), channel_id=1, source_target_pairs={{0,128},{32,160},{64,192},{96,224},{128,0},{160,32},{192,64},{224,... | collective-permute-start | bytes 258056 | tf_op jit(solution)/shard_map/ppermute | solution.py:497
  97.4 5.2 %collective-permute-start.11 = (bf16[336,128]{1,0:T(8,128)(2,1)S(1)}, bf16[336,128]{1,0:T(8,128)(2,1)S(1)}, u32[]{:S(2)}, u32[]{:S(2)}) collective-permute-start(bf16[336,128]{1,0:T(8,128)(2,1)S(1)} %get-tuple-element.71), channel_id=1, source_target_pairs={{0,64},{32,96},{64,128},{96,160},{128,192},{160,224},{192,0},{224,... | collective-permute-start | bytes 258056 | tf_op jit(solution)/shard_map/ppermute | solution.py:497
  123.9 6.0 %collective-permute-start.12 = (bf16[32,48,128]{2,1,0:T(8,128)(2,1)S(1)}, bf16[32,48,128]{2,1,0:T(8,128)(2,1)S(1)}, u32[]{:S(2)}, u32[]{:S(2)}) collective-permute-start(bf16[32,48,128]{2,1,0:T(8,128)(2,1)S(1)} %all_to_all.23.arrived_ref.mine_ref), channel_id=1, source_target_pairs={{0,32},{32,0},{64,96},{96,64},{128,160},{160,128},{192,224},{224,1... | collective-permute-start | bytes 1179656 | tf_op jit(solution)/shard_map/ppermute | solution.py:492
